TPU v7x, 128 devices: a whole 4x4x4 slice. The times are simulated.
128 devices in a mesh: leaf: 16 (over x, z), front: 8 (over y, core).
Axes of the slice: x: 4, y: 4, z: 4, core: 2. Of those that a mesh axis runs over, the one named last changes fastest.
Arguments:
- block_now: float32 [64, 266240], P(None, ('leaf', 'front')), may hold values from -18 to 18
- block_before: float32 [64, 266240], P(None, ('leaf', 'front')), may hold values from -6 to 6
- coupling: float32 [64, 64], replicated, may hold values from -1.8 to 1.8, as said below
- vertex_to_tree: int32 [266240], P(('leaf', 'front')), may hold values from 0 to 266239, as said below
- tree_to_vertex: int32 [266240], P(('leaf', 'front')), may hold values from 0 to 266239, as said below
- leaf_inverse: float32 [1024, 256, 256], P(('leaf', 'front')), may hold values from -1 to 2, as said below
- leaf_below: float32 [1024, 256, 256], P(('leaf', 'front')), may hold values from -0.02734375 to 0.02734375
- leaf_rows: int32 [1024, 256], P(('leaf', 'front')), may hold values from 0 to 1279, as said below
- sep_inverse: float32 [16, 256, 256], replicated, may hold values from -1 to 2, as said below
- sep_parent: float32 [15, 256, 256], replicated, may hold values from -0.1875 to 0.1875
Outputs:
- projection: float32 [64, 64], replicated
- factor: float32 [64, 64], replicated
- next_block: float32 [64, 266240], P(None, ('leaf', 'front'))
Inputs may be any that keep to these rules, and one draw needn't show every extreme that they name: `vertex_to_tree`: a permutation; the vertices of one device go to every device in near-equal numbers, 16 or 17 to each, and some device sends 17 to some device. `tree_to_vertex`: the inverse permutation of vertex_to_tree. `leaf_rows`: each row holds 256 different path positions in increasing order, and every row includes position 1279. `leaf_inverse`: each block is lower triangular with a positive diagonal. `sep_inverse`: each block is lower triangular with a positive diagonal. `coupling`: upper triangular.
All inputs are finite; a program needn't handle non-finite values.
Results may differ from a plain program's by a relative error of at most 0.0012.
Values sent between devices are 32-bit elements; how exact they have to be, the bound alone decides.
No kernel may reach another device: no remote copies, remote signals or barrier semaphores. Data moves between devices by JAX's collectives and lax.ppermute only.
A program may use at most 64 MiB of HBM per device.

v0:
```python
import jax
import jax.numpy as jnp
from jax import lax
from jax.sharding import PartitionSpec as P

HIGHEST = lax.Precision.HIGHEST


def partner_2(value, axis, apart):
    mask = 2**apart
    pairs = [(source, source ^ mask) for source in range(lax.axis_size(axis))]
    return lax.ppermute(value, axis, pairs)


def place_tables(sort_keys, rows_here, devices, capacity):
    bucket = sort_keys // rows_here
    ordering = jnp.argsort(sort_keys)
    ranked = bucket[ordering]
    device_ids = jnp.arange(devices, dtype=jnp.int32)
    first_slot = jnp.searchsorted(ranked, device_ids, side="left")
    after_slot = jnp.searchsorted(ranked, device_ids, side="right")
    slot_index = first_slot[:, None] + jnp.arange(capacity, dtype=jnp.int32)[None, :]
    filled = slot_index < after_slot[:, None]
    picked = ordering[jnp.minimum(slot_index, rows_here - 1)]
    position = jnp.argsort(ordering)
    landing = bucket * capacity + position - first_slot[bucket]
    return (picked, filled, landing)


def per_device(
    block_now,
    block_before,
    coupling,
    vertex_to_tree,
    tree_to_vertex,
    leaf_inverse,
    leaf_below,
    leaf_rows,
    sep_inverse,
    sep_parent,
):
    group_count = lax.axis_size("leaf")
    front_count = lax.axis_size("front")
    devices = group_count * front_count
    vector_count, rows_here = block_now.shape
    capacity = (rows_here + devices - 1) // devices
    total_rows = rows_here * devices
    leaf_count = leaf_inverse.shape[0]
    leaf_width = leaf_inverse.shape[1]
    leaf_span = leaf_count * leaf_width
    sep_width = sep_inverse.shape[1]
    sep_share = sep_width // front_count
    levels = group_count.bit_length()
    my_group = lax.axis_index("leaf")
    my_front = lax.axis_index("front")
    own_start = my_front * sep_share
    local_ids = jnp.arange(rows_here, dtype=jnp.int32)
    send_pick, send_fill, send_land = place_tables(
        vertex_to_tree // rows_here * rows_here + local_ids, rows_here, devices, capacity
    )
    tree_pick, tree_fill, tree_land = place_tables(tree_to_vertex, rows_here, devices, capacity)
    outgoing = jnp.where(send_fill[None], block_now[:, send_pick], 0.0)
    arrived = lax.all_to_all(
        outgoing.reshape(vector_count, devices * capacity),
        ("leaf", "front"),
        split_axis=1,
        concat_axis=1,
        tiled=True,
    )
    tree_block = arrived[:, tree_land]
    leaf_source = tree_block[:, :leaf_span].reshape(vector_count, leaf_count, leaf_width)
    own_sep = tree_block[:, leaf_span:]
    leaf_solved = jnp.einsum("bij,kbj->kbi", leaf_inverse, leaf_source, precision=HIGHEST)
    update = jnp.einsum("brj,kbj->kbr", leaf_below, leaf_solved, precision=HIGHEST)
    pushed = (
        jnp.zeros((vector_count, levels * sep_width), jnp.float32)
        .at[:, leaf_rows.reshape(-1)]
        .add(update.reshape(vector_count, -1))
    )
    pending = lax.psum_scatter(
        pushed.reshape(vector_count, levels, sep_width), "front", scatter_dimension=2, tiled=True
    )
    home_slot = jnp.zeros((), jnp.int32)
    for bit_index in range(levels - 1):
        home_slot = home_slot + (my_group % (2 << bit_index) == 0).astype(jnp.int32)
    slot_marks = (jnp.arange(levels, dtype=jnp.int32) == home_slot).astype(jnp.float32)
    pending = pending - slot_marks[None, :, None] * own_sep[:, None, :]
    inverses = []
    parent_links = []
    solved_seps = []
    for height in range(1, levels + 1):
        path_slot = height - 1
        if height < levels:
            partner = partner_2(pending[:, path_slot:], "leaf", height - 1)
            pending = jnp.concatenate(
                [pending[:, :path_slot], pending[:, path_slot:] + partner], axis=1
            )
            sep_id = group_count + my_group >> height
        else:
            sep_id = jnp.zeros((), jnp.int32)
        inverse = lax.dynamic_index_in_dim(sep_inverse, sep_id, 0, keepdims=False)
        inverses.append(inverse)
        if height < levels:
            parent_links.append(lax.dynamic_index_in_dim(sep_parent, sep_id - 1, 0, keepdims=False))
        whole_source = lax.all_gather(-pending[:, path_slot], "front", axis=1, tiled=True)
        inverse_rows = lax.dynamic_slice_in_dim(inverse, own_start, sep_share, 0)
        values = jnp.einsum("ij,kj->ki", inverse_rows, whole_source, precision=HIGHEST)
        if height < levels:
            link_columns = lax.dynamic_slice_in_dim(
                parent_links[path_slot], own_start, sep_share, 1
            )
            partial_update = jnp.einsum("ij,kj->ki", link_columns, values, precision=HIGHEST)
            pending = pending.at[:, path_slot + 1].add(
                lax.psum_scatter(partial_update, "front", scatter_dimension=1, tiled=True)
            )
        solved_seps.append(values)
    sep_values = lax.all_gather(jnp.stack(solved_seps, axis=1), "front", axis=2, tiled=True)
    sep_back = [None] * levels
    for path_slot in range(levels - 1, -1, -1):
        corrected = sep_values[:, path_slot]
        if path_slot < levels - 1:
            corrected = corrected - jnp.einsum(
                "ji,kj->ki", parent_links[path_slot], sep_back[path_slot + 1], precision=HIGHEST
            )
        sep_back[path_slot] = jnp.einsum(
            "ji,kj->ki", inverses[path_slot], corrected, precision=HIGHEST
        )
    path_back = jnp.stack(sep_back, axis=1)
    known_rows = path_back.reshape(vector_count, levels * sep_width)[:, leaf_rows]
    leaf_corrected = leaf_solved - jnp.einsum(
        "brj,kbr->kbj", leaf_below, known_rows, precision=HIGHEST
    )
    leaf_back = jnp.einsum("bji,kbj->kbi", leaf_inverse, leaf_corrected, precision=HIGHEST)
    home_values = lax.dynamic_index_in_dim(path_back, home_slot, 1, keepdims=False)
    home_rows = lax.dynamic_slice_in_dim(home_values, own_start, sep_share, 1)
    tree_out = jnp.concatenate([leaf_back.reshape(vector_count, leaf_span), home_rows], axis=1)
    returning = jnp.where(tree_fill[None], tree_out[:, tree_pick], 0.0)
    returned = lax.all_to_all(
        returning.reshape(vector_count, devices * capacity),
        ("leaf", "front"),
        split_axis=1,
        concat_axis=1,
        tiled=True,
    )
    solved_block = returned[:, send_land]
    projection = (
        lax.psum(
            jnp.einsum("kn,jn->kj", block_now, solved_block, precision=HIGHEST), ("leaf", "front")
        )
        / total_rows
    )
    residual = (
        solved_block
        - jnp.einsum("jk,jn->kn", projection, block_now, precision=HIGHEST)
        - jnp.einsum("kj,jn->kn", coupling, block_before, precision=HIGHEST)
    )
    gram_matrix = (
        lax.psum(jnp.einsum("kn,jn->kj", residual, residual, precision=HIGHEST), ("leaf", "front"))
        / total_rows
    )
    lower_factor = jnp.linalg.cholesky(gram_matrix)
    next_block = jax.scipy.linalg.solve_triangular(lower_factor, residual, lower=True)
    return (projection, lower_factor.T, next_block)


def solution(mesh):
    placed = (
        P(None, ("leaf", "front")),
        P(None, ("leaf", "front")),
        P(),
        P(("leaf", "front")),
        P(("leaf", "front")),
        P(("leaf", "front"), None, None),
        P(("leaf", "front"), None, None),
        P(("leaf", "front"), None),
        P(),
        P(),
    )
    return jax.shard_map(
        per_device,
        mesh=mesh,
        in_specs=placed,
        out_specs=(P(), P(), P(None, ("leaf", "front"))),
        check_vma=False,
    )
```

profile of v0, /device:TPU:1, one launch (start us, length us, event | category | flops | bytes accessed | tf_op | source)
XLA Modules:
  0.0 694.6 jit_solution(2028547475116550155)
XLA Ops:
  8.1 6.5 sort.59
  14.6 5.8 sort.61
  21.2 5.8 sort.60
  27.0 11.4 %gather_fusion.5 = s32[2080]{0:T(1024)S(1)} fusion(s32[2080]{0:T(1024)S(1)} %add_select_fusion, s32[3072]{0:T(1024)S(1)} %pad_clamp_fusion.12), kind=kCustom, calls=%fused_computation.5 | custom fusion | bytes 24960 | tf_op jit(solution)/shard_map/gather | solution.py:18
  38.4 14.6 %while.81 = (s32[]{:T(128)}, u32[128]{0:T(128)S(1)}, u32[128]{0:T(128)S(1)}, s32[2080]{0:T(1024)S(1)}, s32[]{:T(128)}, /*index=5*/s32[]{:T(128)}, s32[]{}) while((s32[]{:T(128)}, u32[128]{0:T(128)S(1)}, u32[128]{0:T(128)S(1)}, s32[2080]{0:T(1024)S(1)}, s32[]{:T(128)}, /*index=5*/s32[]{:T(128)}, s32[]{}) %tuple.150), condition=%wide.region_9.10_spmd.clone, body=%wide.region_8.9_spmd.clone.sunk | while | flops 2692 | bytes 10340 | solution.py:21
  53.0 14.6 %while.80 = (s32[]{:T(128)}, u32[128]{0:T(128)S(1)}, u32[128]{0:T(128)S(1)}, s32[2080]{0:T(1024)S(1)}, s32[]{:T(128)}, /*index=5*/s32[]{:T(128)}, s32[]{}) while((s32[]{:T(128)}, u32[128]{0:T(128)S(1)}, u32[128]{0:T(128)S(1)}, s32[2080]{0:T(1024)S(1)}, s32[]{:T(128)}, /*index=5*/s32[]{:T(128)}, s32[]{}) %tuple.167), condition=%wide.region_7.8_spmd.clone, body=%wide.region_6.7_spmd.clone.sunk | while | flops 2692 | bytes 10340 | solution.py:20
  67.8 11.4 %gather_fusion.4 = s32[2080]{0:T(1024)S(1)} fusion(s32[2080]{0:T(1024)S(1)} %get-tuple-element.422, s32[3072]{0:T(1024)S(1)} %pad_clamp_fusion.13), kind=kCustom, calls=%fused_computation.4 | custom fusion | bytes 24960 | tf_op jit(solution)/shard_map/gather | solution.py:18
  79.2 14.6 %while.78 = (s32[]{:T(128)}, u32[128]{0:T(128)S(1)}, u32[128]{0:T(128)S(1)}, s32[2080]{0:T(1024)S(1)}, s32[]{:T(128)}, /*index=5*/s32[]{:T(128)}, s32[]{}) while((s32[]{:T(128)}, u32[128]{0:T(128)S(1)}, u32[128]{0:T(128)S(1)}, s32[2080]{0:T(1024)S(1)}, s32[]{:T(128)}, /*index=5*/s32[]{:T(128)}, s32[]{}) %tuple.144), condition=%wide.region_2.3_spmd.clone, body=%wide.region_1.2_spmd.clone.sunk | while | flops 2692 | bytes 10340 | solution.py:20
  94.1 11.7 %gather_fusion.6 = s32[2176]{0:T(1024)S(1)} fusion(s32[2080]{0:T(1024)S(1)} %get-tuple-element.298, s32[3072]{0:T(1024)S(1)} %pad_clamp_fusion.11), kind=kCustom, calls=%fused_computation.6 | custom fusion | bytes 26112 | tf_op jit(solution)/shard_map/gather | solution.py:24
  107.6 12.3 %gather_fusion.8 = s32[2080]{0:T(1024)S(1)} fusion(s32[128]{0:T(128)S(1)} %convert_element_type.48, s32[3072]{0:T(1024)S(1)} %pad_clamp_fusion.9), kind=kCustom, calls=%fused_computation.8 | custom fusion | bytes 24960 | tf_op jit(solution)/shard_map/gather | solution.py:26
  133.0 11.5 %all-to-all-start = ((f32[128,1,1088]{2,1,0:T(1,128)}), f32[128,1,1088]{2,1,0:T(1,128)S(1)}, u32[]{:S(2)}, u32[]{:S(2)}) async-start(f32[128,1,1088]{2,1,0:T(1,128)} %reshape.567), calls=%async_computation | async-start | bytes 1179648 | tf_op jit(solution)/shard_map/all_to_all | solution.py:63
  144.9 13.8 %all-to-all-done = f32[128,1,1088]{2,1,0:T(1,128)S(1)} async-done(((f32[128,1,1088]{2,1,0:T(1,128)}), f32[128,1,1088]{2,1,0:T(1,128)S(1)}, u32[]{:S(2)}, u32[]{:S(2)}) %all-to-all-start) | async-done | bytes 557088 | tf_op jit(solution)/shard_map/all_to_all | solution.py:63
  176.9 12.7 %scatter_custom_fusion = f32[64,1280]{0,1:T(8,128)} fusion(s32[2048]{0:T(1024)S(1)} %bitcast.250, f32[2048,64]{1,0:T(8,128)} %copy.23, f32[]{:T(128)} %constant.497.clone.1), kind=kCustom, calls=%fused_computation.67 | custom fusion | flops 131072 | bytes 328192 | tf_op jit(solution)/shard_map/scatter-add | solution.py:78
  190.5 24.2 %reduce-scatter.6.cloned.1.call-done = f32[64,5,32]{0,2,1:T(8,128)} async-done(((f32[64,5,256]{0,2,1:T(8,128)}), f32[64,5,32]{0,2,1:T(8,128)}) %reduce-scatter.6.cloned.1.call-update) | async-done | bytes 40976 | tf_op jit(solution)/shard_map/reduce_scatter | solution.py:80
  217.2 14.6 %while.79 = (s32[]{:T(128)}, u32[128]{0:T(128)S(1)}, u32[128]{0:T(128)S(1)}, s32[2080]{0:T(1024)S(1)}, s32[]{:T(128)}, /*index=5*/s32[]{:T(128)}, s32[]{}) while((s32[]{:T(128)}, u32[128]{0:T(128)S(1)}, u32[128]{0:T(128)S(1)}, s32[2080]{0:T(1024)S(1)}, s32[]{:T(128)}, /*index=5*/s32[]{:T(128)}, s32[]{}) %tuple.166), condition=%wide.region_4.5_spmd.clone, body=%wide.region_3.4_spmd.clone.sunk | while | flops 2692 | bytes 10340 | solution.py:21
  232.0 16.2 %all-gather = f32[64,1,256]{0,2,1:T(8,128)S(1)} all-gather(f32[64,1,32]{0,2,1:T(8,128)S(1)} %slice_negate_fusion.3), channel_id=2, replica_groups=mesh['leaf'=16,'front'=8] {'front'}, dimensions={2}, use_global_device_ids=true | all-gather | bytes 73728 | tf_op jit(solution)/shard_map/all_gather | solution.py:105
  251.4 11.7 %gather_fusion.11 = s32[2176]{0:T(1024)S(1)} fusion(s32[2080]{0:T(1024)S(1)} %get-tuple-element.295, s32[3072]{0:T(1024)S(1)} %pad_clamp_fusion.7), kind=kCustom, calls=%fused_computation.11 | custom fusion | bytes 26112 | tf_op jit(solution)/shard_map/gather | solution.py:24
  263.3 14.4 %reduce-scatter.8.cloned.1.call-done = f32[64,32]{0,1:T(8,128)} async-done(((f32[64,256]{0,1:T(8,128)}), f32[64,32]{0,1:T(8,128)}) %reduce-scatter.8.cloned.1.call-update) | async-done | bytes 8208 | tf_op jit(solution)/shard_map/reduce_scatter | solution.py:114
  283.1 17.1 %all-gather.1 = f32[64,1,256]{0,2,1:T(8,128)S(1)} all-gather(f32[64,1,32]{0,2,1:T(8,128)S(1)} %slice_negate_fusion.2), channel_id=3, replica_groups=mesh['leaf'=16,'front'=8] {'front'}, dimensions={2}, use_global_device_ids=true | all-gather | bytes 73728 | tf_op jit(solution)/shard_map/all_gather | solution.py:105
  303.2 10.9 %reduce-scatter.12.cloned.1.call-start = ((), (), s32[]{:S(2)}) async-start(), calls=%async_computation.10 | async-start | bytes 147456 | tf_op jit(solution)/shard_map/reduce_scatter | solution.py:114
  314.0 12.3 %gather_fusion.13 = s32[2080]{0:T(1024)S(1)} fusion(s32[128]{0:T(128)S(1)} %convert_element_type.50, s32[3072]{0:T(1024)S(1)} %pad_clamp_fusion.5), kind=kCustom, calls=%fused_computation.13 | custom fusion | bytes 24960 | tf_op jit(solution)/shard_map/gather | solution.py:26
  335.9 15.1 %all-gather.2 = f32[64,1,256]{0,2,1:T(8,128)S(1)} all-gather(f32[64,1,32]{0,2,1:T(8,128)S(1)} %slice_negate_fusion.1), channel_id=4, replica_groups=mesh['leaf'=16,'front'=8] {'front'}, dimensions={2}, use_global_device_ids=true | all-gather | bytes 73728 | tf_op jit(solution)/shard_map/all_gather | solution.py:105
  354.1 26.8 %reduce-scatter.12.cloned.1.call-done = f32[64,32]{0,1:T(8,128)} async-done(((f32[64,256]{0,1:T(8,128)}), f32[64,32]{0,1:T(8,128)}) %reduce-scatter.12.cloned.1.call-update) | async-done | bytes 8208 | tf_op jit(solution)/shard_map/reduce_scatter | solution.py:114
  385.9 17.1 %all-gather.3 = f32[64,1,256]{0,2,1:T(8,128)S(1)} all-gather(f32[64,1,32]{0,2,1:T(8,128)S(1)} %slice_negate_fusion), channel_id=5, replica_groups=mesh['leaf'=16,'front'=8] {'front'}, dimensions={2}, use_global_device_ids=true | all-gather | bytes 73728 | tf_op jit(solution)/shard_map/all_gather | solution.py:105
  406.2 26.8 %reduce-scatter.14.cloned.1.call-done = f32[64,32]{0,1:T(8,128)} async-done(((f32[64,256]{0,1:T(8,128)}), f32[64,32]{0,1:T(8,128)}) %reduce-scatter.14.cloned.1.call-update) | async-done | bytes 8208 | tf_op jit(solution)/shard_map/reduce_scatter | solution.py:114
  433.7 16.1 %all-gather.4 = f32[64,1,256]{0,2,1:T(8,128)S(1)} all-gather(f32[64,1,32]{0,2,1:T(8,128)S(1)} %fusion.77), channel_id=6, replica_groups=mesh['leaf'=16,'front'=8] {'front'}, dimensions={2}, use_global_device_ids=true | all-gather | bytes 73728 | tf_op jit(solution)/shard_map/all_gather | solution.py:105
  449.9 13.3 %all_gather.23 = f32[64,5,256]{0,2,1:T(8,128)S(1)} all-gather(f32[64,5,32]{0,2,1:T(8,128)S(1)} %fusion.18), channel_id=1, replica_groups=mesh['leaf'=16,'front'=8] {'front'}, dimensions={2}, use_global_device_ids=true | all-gather | bytes 368640 | tf_op jit(solution)/shard_map/all_gather | solution.py:117
  479.5 7.6 %gather_fusion.10 = f32[2048,64]{1,0:T(8,128)} fusion(f32[64,1280]{0,1:T(8,128)S(1)} %bitcast.236, s32[2048]{0:T(1024)S(1)} %broadcast_clamp_fusion), kind=kCustom, calls=%fused_computation.10 | custom fusion | bytes 1056768 | tf_op jit(solution)/shard_map/gather | solution.py:129
  506.7 21.6 %all_to_all.18 = f32[128,1,1088]{2,1,0:T(1,128)S(1)} all-to-all(f32[128,1,1088]{2,1,0:T(1,128)S(1)} %reshape.569), channel_id=1, replica_groups=mesh['leaf'=16,'front'=8] {'leaf','front'}, dimensions={0} | all-to-all | bytes 1114112 | tf_op jit(solution)/shard_map/all_to_all | solution.py:138
  542.9 63.1 %psum.14 = f32[64,64]{0,1:T(8,128)S(1)} all-reduce(f32[64,64]{0,1:T(8,128)S(1)} %convolution_bitcast_fusion.5), channel_id=1, replica_groups=mesh['leaf'=16,'front'=8] {'leaf','front'}, use_global_device_ids=true, to_apply=%region_18.19 | all-reduce | flops 4096 | bytes 32768 | tf_op jit(solution)/shard_map/psum | solution.py:147
  610.8 62.6 %psum.15 = f32[64,64]{0,1:T(8,128)S(1)} all-reduce(f32[64,64]{0,1:T(8,128)S(1)} %fusion.108), channel_id=1, replica_groups=mesh['leaf'=16,'front'=8] {'leaf','front'}, use_global_device_ids=true, to_apply=%region_19.20 | all-reduce | flops 4096 | bytes 32768 | tf_op jit(solution)/shard_map/psum | solution.py:158
  673.5 5.8 cholesky.18
  (369 shorter events, 192.5 us)
Async XLA Ops:
  7.2 166.2 %copy-start = (f32[8,256,256]{2,1,0:T(8,128)S(1)}, f32[8,256,256]{2,1,0:T(8,128)}, u32[]{:S(2)}) copy-start(f32[8,256,256]{2,1,0:T(8,128)} %param.32) | copy-start | bytes 6291460
  107.6 12.3 %copy-start.6 = (s32[2080]{0:T(1024)S(1)}, s32[2080]{0:T(1024)}, u32[]{:S(2)}) copy-start(s32[2080]{0:T(1024)} %param.30) | copy-start | bytes 24964
  130.0 14.8 %copy-start.7 = (s32[8,256]{1,0:T(8,128)S(1)}, s32[8,256]{1,0:T(8,128)}, u32[]{:S(2)}) copy-start(s32[8,256]{1,0:T(8,128)} %param.33) | copy-start | bytes 24580
  133.0 25.7 %all-to-all-start = ((f32[128,1,1088]{2,1,0:T(1,128)}), f32[128,1,1088]{2,1,0:T(1,128)S(1)}, u32[]{:S(2)}, u32[]{:S(2)}) async-start(f32[128,1,1088]{2,1,0:T(1,128)} %reshape.567), calls=%async_computation | async-start | bytes 1179648 | tf_op jit(solution)/shard_map/all_to_all | solution.py:63
  144.5 70.2 %reduce-scatter.6.cloned.1.call-start = ((), (), s32[]{:S(2)}) async-start(), calls=%async_computation.7 | async-start | bytes 737280 | tf_op jit(solution)/shard_map/reduce_scatter | solution.py:80
  169.2 1.9 copy-start.1
  189.6 88.1 %reduce-scatter.8.cloned.1.call-start = ((), (), s32[]{:S(2)}) async-start(), calls=%async_computation.8 | async-start | bytes 147456 | tf_op jit(solution)/shard_map/reduce_scatter | solution.py:114
  214.7 17.2 %copy-start.5 = (f32[64,5,32]{0,2,1:T(8,128)S(1)}, f32[64,5,32]{0,2,1:T(8,128)}, u32[]{:S(2)}) copy-start(f32[64,5,32]{0,2,1:T(8,128)} %reduce-scatter.6.cloned.1.call-done) | copy-start | bytes 122884
  215.7 16.1 %collective-permute-start = (f32[64,5,32]{0,2,1:T(8,128)S(1)}, f32[64,5,32]{0,2,1:T(8,128)S(1)}, u32[]{:S(2)}, u32[]{:S(2)}) collective-permute-start(f32[64,5,32]{0,2,1:T(8,128)S(1)} %multiply_subtract_fusion), channel_id=1, source_target_pairs={{0,8},{8,0},{16,24},{24,16},{32,40},{40,32},{48,56},{56,48},{64,72... | collective-permute-start | bytes 122888 | tf_op jit(solution)/shard_map/ppermute | solution.py:12
  251.1 81.1 %reduce-scatter.10.cloned.1.call-start = ((), (), s32[]{:S(2)}) async-start(), calls=%async_computation.9 | async-start | bytes 147456 | tf_op jit(solution)/shard_map/reduce_scatter | solution.py:114
  278.4 4.7 collective-permute-start.1
  303.2 77.8 %reduce-scatter.12.cloned.1.call-start = ((), (), s32[]{:S(2)}) async-start(), calls=%async_computation.10 | async-start | bytes 147456 | tf_op jit(solution)/shard_map/reduce_scatter | solution.py:114
  326.3 123.4 %slice-start = ((f32[16,256,256]{2,1,0:T(8,128)}), f32[1,256,256]{2,1,0:T(8,128)S(1)}, s32[]{:S(2)}) async-start(f32[16,256,256]{2,1,0:T(8,128)} %param.34), calls=%async_computation.12 | async-start | bytes 524288 | tf_op jit(solution)/shard_map/jit(dynamic_index_in_dim)/dynamic_slice | solution.py:101
  332.9 2.9 collective-permute-start.2
  353.9 79.0 %reduce-scatter.14.cloned.1.call-start = ((), (), s32[]{:S(2)}) async-start(), calls=%async_computation.11 | async-start | bytes 147456 | tf_op jit(solution)/shard_map/reduce_scatter | solution.py:114
  381.6 4.3 collective-permute-start.3
  433.6 38.2 %copy-start.4 = (f32[16,256,256]{2,1,0:T(8,128)S(1)}, f32[16,256,256]{2,1,0:T(8,128)}, u32[]{:S(2)}) copy-start(f32[16,256,256]{2,1,0:T(8,128)} %param.34) | copy-start | bytes 12582916
  487.1 3.2 copy-start.2
  538.3 3.4 copy-start.3
  541.7 66.8 %copy-start.8 = (f32[64,64]{1,0:T(8,128)S(1)}, f32[64,64]{1,0:T(8,128)}, u32[]{:S(2)}) copy-start(f32[64,64]{1,0:T(8,128)} %param.28) | copy-start | bytes 49156
Sparse Core Ops, SparseCore 0:
  189.7 24.8 reduce-scatter.5
  251.2 26.4 reduce-scatter.7
  303.3 26.9 reduce-scatter.9
  354.0 26.8 reduce-scatter.11
  406.0 26.8 reduce-scatter.13
where the time goes:
time: 704 us; the launch traced here: 695 us
  blocking collectives  242 us (34%)
  local copies, waits for them, and re-layouts  185 us (26%)
  waiting for transfers between devices  111 us (16%)
  other arithmetic  66.9 us (10%)
  matrix products  41.3 us (6%)
  starting transfers between devices  31.2 us (4%)
  between operations  15 us (2%)
    all_gather x5, blocking collectives, per_device(): lax.all_gather(-pending[:, path_slot], 'front', axis=1, tiled=True)  81.5 us
    reduce_scatter x4, waiting for transfers between devices, per_device(): lax.psum_scatter(partial_update, 'front', scatter_dimension=1, tiled=True)  67.9 us
    psum x1, blocking collectives, per_device(): lax.psum(jnp.einsum('kn,jn->kj', block_now, solved_block, precision=HIGHE...  63.1 us
    psum x1, blocking collectives, per_device(): lax.psum(jnp.einsum('kn,jn->kj', residual, residual, precision=HIGHEST),...  62.6 us
    gather x24, local copies, waits for them, and re-layouts, place_tables(): first_slot = jnp.searchsorted(ranked, device_ids, side='left')  27.6 us
    gather x24, local copies, waits for them, and re-layouts, place_tables(): after_slot = jnp.searchsorted(ranked, device_ids, side='right')  27.6 us
    gather x2, local copies, waits for them, and re-layouts, place_tables(): landing = bucket * capacity + position - first_slot[bucket]  24.6 us
    reduce_scatter x1, waiting for transfers between devices, per_device(): lax.psum_scatter(pushed.reshape(vector_count, levels, sep_width), 'front'...  24.2 us
  transfers between devices with their start and end apart: 10, of which 8 were waited for; matrix products, arithmetic and copies ran while one was open for 7% of the time, Pallas kernels for 0%

commit v1 on v0

v1 whole, which is shorter than its diff:
```python
import jax
import jax.numpy as jnp
from jax import lax
from jax.experimental import pallas as pl
from jax.experimental.pallas import tpu as pltpu
from jax.sharding import PartitionSpec as P

F32 = jnp.float32
BF16 = jnp.bfloat16
HIGHEST = lax.Precision.HIGHEST
AXES = ("leaf", "front")
DEV = 128
CAP = 17
ROWS = 2080
PAD = 2176
VEC = 64
LEAF = 256
NLEAF = 8
SPAN = 2048
GROUPS = 16
FRONT = 8
SHARE = 32
LEVELS = 5
PATH = 1280
S1 = 18
S2 = 10
S3 = 5
S4 = 10
MIB = 1024 * 1024


def nn(a, b):
    return lax.dot_general(a, b, (((1,), (0,)), ((), ())), preferred_element_type=F32)


def nt(a, b):
    return lax.dot_general(a, b, (((1,), (1,)), ((), ())), preferred_element_type=F32)


def nn32(a, b):
    return lax.dot_general(
        a, b, (((1,), (0,)), ((), ())), preferred_element_type=F32, precision=HIGHEST
    )


def nt32(a, b):
    return lax.dot_general(
        a, b, (((1,), (1,)), ((), ())), preferred_element_type=F32, precision=HIGHEST
    )


def split(x):
    hi = x.astype(BF16)
    lo = (x - hi.astype(F32)).astype(BF16)
    return hi, lo


def iota(shape, dim):
    return lax.broadcasted_iota(jnp.int32, shape, dim)


def onehot(mask):
    return jnp.where(mask, 1.0, 0.0).astype(BF16)


def both(x):
    return x + pltpu.roll(x, 64, 1)


def lanes_split(x):
    hi, lo = split(x)
    return jnp.where(iota(x.shape, 1) < 64, hi.astype(F32), lo.astype(F32)).astype(BF16)


def pack_kernel(vt_ref, now_ref, before_ref, out_ref, key_ref, dest, member, value, mark):
    dest[...] = jnp.full((8, PAD), -1, jnp.int32)
    dest[0:1, 0:ROWS] = vt_ref[...]
    target = dest[0:1, :]
    bucket = ((target.astype(F32) + 0.5) * (1.0 / ROWS)).astype(jnp.int32)
    bucket = jnp.where(target < 0, -1, bucket)
    place = target - bucket * ROWS
    member[...] = onehot(jnp.broadcast_to(bucket, (DEV, PAD)) == iota((DEV, PAD), 0))
    value[...] = jnp.zeros((4 * VEC, PAD), BF16)
    now_hi, now_lo = split(now_ref[...])
    bef_hi, bef_lo = split(before_ref[...])
    value[0:64, 0:ROWS] = now_hi
    value[64:128, 0:ROWS] = bef_hi
    value[128:192, 0:ROWS] = now_lo
    value[192:256, 0:ROWS] = bef_lo
    before = onehot(
        (iota((128, 256), 0) < iota((128, 256), 1)) | (iota((128, 256), 1) >= 128)
    )
    carry = jnp.zeros((DEV, 128), F32)
    ranks = []
    for b in range(CAP):
        part = member[:, b * 128 : (b + 1) * 128]
        counts = nn(part, before)
        ranks.append(
            jnp.sum(part.astype(F32) * (counts[:, 0:128] + carry), axis=0, keepdims=True)
        )
        carry = carry + counts[:, 128:256]
    rank = jnp.concatenate(ranks, axis=1).astype(jnp.int32)
    key = jnp.where(target < 0, -1, rank * DEV + bucket)
    key_ref[...] = key[:, 0:ROWS]
    for k in range(CAP):
        mark[k * DEV : (k + 1) * DEV, :] = onehot(
            jnp.broadcast_to(key, (DEV, PAD)) == iota((DEV, PAD), 0) + k * DEV
        )
    for c in range(CAP):
        block = nt(mark[c * DEV : (c + 1) * DEV, :], value[...])
        out_ref[pl.ds(c, DEV, stride=S1), :] = block[:, 0:128] + block[:, 128:256]
    ranked = jnp.broadcast_to(rank, (32, PAD)) == iota((32, PAD), 0)
    high = place // 64
    marks = jnp.concatenate(
        [
            jnp.where(ranked, jnp.broadcast_to(high, (32, PAD)).astype(F32), 0.0),
            jnp.where(ranked, jnp.broadcast_to(place - high * 64, (32, PAD)).astype(F32), 0.0),
            jnp.zeros((64, PAD), F32),
        ],
        axis=0,
    ).astype(BF16)
    found = nt(member[...], marks)
    where = found * 64.0 + pltpu.roll(found, 96, 1)
    lane = iota((DEV, 128), 1)
    filled = (lane.astype(F32) < carry) & (lane < CAP)
    out_ref[pl.ds(CAP, DEV, stride=S1), :] = jnp.where(filled, where, -1.0)


def own_gram_kernel(now_ref, before_ref, out_ref, value):
    now_hi, now_lo = split(now_ref[...])
    bef_hi, bef_lo = split(before_ref[...])
    value[0:64, :] = now_hi
    value[64:128, :] = bef_hi
    value[128:192, :] = now_lo
    value[192:256, :] = bef_lo
    gram = nt(value[...], value[...])
    rows = gram[0:128] + gram[128:256]
    out_ref[...] = rows[:, 0:128] + rows[:, 128:256]


def forward_kernel(
    home_ref,
    recv_ref,
    inv_ref,
    below_ref,
    rows_ref,
    out_ref,
    solved_ref,
    tree_ref,
    idx_ref,
    mark,
    value,
    moved,
    update,
):
    idx = recv_ref[pl.ds(CAP, DEV, stride=S1), :]
    idx_ref[...] = idx
    slots = idx.T.astype(jnp.int32)
    for k in range(CAP):
        hi, lo = split(recv_ref[pl.ds(k, DEV, stride=S1), :])
        value[k * DEV : (k + 1) * DEV, 0:128] = hi
        value[k * DEV : (k + 1) * DEV, 128:256] = lo
        mark[:, k * DEV : (k + 1) * DEV] = onehot(
            jnp.broadcast_to(slots[k : k + 1, :], (ROWS, DEV)) == iota((ROWS, DEV), 0)
        )
    got = nn(mark[...], value[...])
    tree_ref[...] = got[:, 0:128] + got[:, 128:256]
    for q in range(NLEAF):
        moved[:, q * LEAF : (q + 1) * LEAF] = onehot(
            jnp.broadcast_to(rows_ref[q : q + 1, :], (PATH, LEAF)) == iota((PATH, LEAF), 0)
        )
    low = iota((LEAF, 128), 1) < 64
    for q in range(NLEAF):
        source = tree_ref[q * LEAF : (q + 1) * LEAF, :]
        source = lanes_split(jnp.where(low, source, pltpu.roll(source, 64, 1)))
        hi, lo = split(inv_ref[q])
        solved = both(nn(hi, source) + nn(lo, source))
        solved_ref[:, q * LEAF : (q + 1) * LEAF] = solved.T[0:64, :]
        hi, lo = split(below_ref[q])
        solved = lanes_split(solved)
        update[q * LEAF : (q + 1) * LEAF, :] = lanes_split(both(nn(hi, solved) + nn(lo, solved)))
    pushed = both(nn(moved[...], update[...]))
    own = tree_ref[SPAN:ROWS, :]
    own = jnp.where(iota((SHARE, 128), 1) < 64, own, pltpu.roll(own, 64, 1))
    start = home_ref[0]
    for j in range(S2):
        chunk = -pushed[j * 128 : (j + 1) * 128, :]
        spread = jnp.concatenate([own] * 4, axis=0)
        at = iota((128, 128), 0) + (j * 128 - start)
        chunk = chunk + jnp.where((at >= 0) & (at < SHARE), spread, 0.0)
        out_ref[pl.ds(j, DEV, stride=S2), :] = chunk.T


def to_row(column, eye):
    top = jnp.sum(jnp.where(eye, column[0:128], 0.0), axis=0, keepdims=True)
    bottom = jnp.sum(jnp.where(eye, column[128:256], 0.0), axis=0, keepdims=True)
    return jnp.concatenate([top, bottom], axis=1)


def to_column(row, eye):
    top = jnp.sum(jnp.where(eye, row[:, 0:128], 0.0), axis=1, keepdims=True)
    bottom = jnp.sum(jnp.where(eye, row[:, 128:256], 0.0), axis=1, keepdims=True)
    return jnp.concatenate([top, bottom], axis=0)


def apply(matrix, row, eye):
    product = matrix * row
    return to_row(jnp.sum(product[:, 0:128] + product[:, 128:256], axis=1, keepdims=True), eye)


def apply_t(matrix, row, eye):
    return jnp.sum(matrix * to_column(row, eye), axis=0, keepdims=True)


def separator_kernel(half_ref, recv_ref, inv_ref, parent_ref, out_ref):
    eye = iota((128, 128), 0) == iota((128, 128), 1)
    source = {}
    for height in range(1, LEVELS + 1):
        count = max(GROUPS >> height, 1)
        first = count if height < LEVELS else 0
        span = DEV // count
        left = recv_ref[pl.ds(2 * height - 2, DEV, stride=S2), :]
        right = recv_ref[pl.ds(2 * height - 1, DEV, stride=S2), :]
        for c in range(count):
            at = slice(c * span, (c + 1) * span)
            source[first + c] = jnp.concatenate(
                [
                    jnp.sum(left[at], axis=0, keepdims=True),
                    jnp.sum(right[at], axis=0, keepdims=True),
                ],
                axis=1,
            )
    solved = {}
    for height in range(1, LEVELS + 1):
        count = max(GROUPS >> height, 1)
        first = count if height < LEVELS else 0
        for s in range(first, first + count):
            right = source[s]
            if height > 1:
                children = (1,) if s == 0 else (2 * s, 2 * s + 1)
                for c in children:
                    right = right - apply(parent_ref[c - 1], solved[c], eye)
            solved[s] = apply(inv_ref[s], right, eye)
    back = {}
    for height in range(LEVELS, 0, -1):
        count = max(GROUPS >> height, 1)
        first = count if height < LEVELS else 0
        for s in range(first, first + count):
            right = solved[s]
            if s > 0:
                right = right - apply_t(parent_ref[s - 1], back[s // 2], eye)
            back[s] = apply_t(inv_ref[s], right, eye)
    upper = half_ref[0] == 1
    for jj in range(S3):
        lines = []
        for g in range(GROUPS):
            ends = []
            for j in (jj, S3 + jj):
                s = (GROUPS + g) >> (j // 2 + 1)
                ends.append(back[s][:, (j % 2) * 128 : (j % 2) * 128 + 128])
            line = jnp.where(upper, ends[1], ends[0])
            lines.append(jnp.broadcast_to(line, (FRONT, 128)))
        out_ref[pl.ds(jj, DEV, stride=S3), :] = jnp.concatenate(lines, axis=0)


def backward_kernel(
    home_ref,
    recv_ref,
    inv_ref,
    below_ref,
    rows_ref,
    solved_ref,
    tree_ref,
    idx_ref,
    gram_ref,
    out_ref,
    known,
    parts,
    moved,
    mark,
    result,
    other,
):
    for q in range(NLEAF):
        moved[:, q * LEAF : (q + 1) * LEAF] = onehot(
            jnp.broadcast_to(rows_ref[q : q + 1, :], (PATH, LEAF)) == iota((PATH, LEAF), 0)
        )
    for h in range(2):
        for jj in range(S3):
            j = h * S3 + jj
            chunk = recv_ref[pl.ds(h * 64 * S3 + jj, 64, stride=S3), :]
            known[:, j * 128 : (j + 1) * 128] = chunk
            hi, lo = split(chunk)
            parts[0:64, j * 128 : (j + 1) * 128] = hi
            parts[64:128, j * 128 : (j + 1) * 128] = lo
    picked = nn(parts[...], moved[...])
    result[:, SPAN:PAD] = jnp.zeros((128, PAD - SPAN), BF16)
    start = home_ref[0]
    tile = pl.multiple_of((start // 128) * 128, 128)
    home = pltpu.roll(known[:, pl.ds(tile, 128)], (128 - start % 128) % 128, 1)
    home = jnp.where(iota((64, 128), 1) < SHARE, home, 0.0)
    hi, lo = split(home)
    result[0:64, SPAN:PAD] = hi
    result[64:128, SPAN:PAD] = lo
    for q in range(NLEAF):
        cols = slice(q * LEAF, (q + 1) * LEAF)
        rows = picked[0:64, cols] + picked[64:128, cols]
        hi, lo = split(rows)
        rows = jnp.concatenate([hi, lo], axis=0)
        hi, lo = split(below_ref[q])
        lifted = nn(rows, hi) + nn(rows, lo)
        source = solved_ref[:, cols] - (lifted[0:64] + lifted[64:128])
        hi, lo = split(source)
        source = jnp.concatenate([hi, lo], axis=0)
        hi, lo = split(inv_ref[q])
        solved = nn(source, hi) + nn(source, lo)
        hi, lo = split(solved[0:64] + solved[64:128])
        result[0:64, cols] = hi
        result[64:128, cols] = lo
    hi, lo = split(tree_ref[...])
    other[ROWS:PAD, :] = jnp.zeros((PAD - ROWS, 256), BF16)
    other[0:ROWS, 0:128] = hi
    other[0:ROWS, 128:256] = lo
    cross = nn(result[...], other[...])
    cross = cross[0:64] + cross[64:128]
    cross = cross[:, 0:128] + cross[:, 128:256]
    square = nt(result[...], result[...])
    square = both(square[0:64] + square[64:128])
    idx = idx_ref[...].astype(jnp.int32)
    for k in range(CAP):
        mark[k * DEV : (k + 1) * DEV, :] = onehot(
            jnp.broadcast_to(idx[:, k : k + 1], (DEV, PAD)) == iota((DEV, PAD), 1)
        )
    lane = iota((DEV, 128), 1) < 64
    packed = both(nt(mark[...], result[...]))
    for j in range(8):
        out_ref[pl.ds(j, DEV, stride=S4), :] = jnp.where(
            lane,
            packed[2 * j * DEV : (2 * j + 1) * DEV],
            packed[(2 * j + 1) * DEV : (2 * j + 2) * DEV],
        )
    late = jnp.concatenate([square, gram_ref[64:128, :]], axis=0)
    out_ref[pl.ds(8, DEV, stride=S4), :] = jnp.where(lane, packed[16 * DEV : 17 * DEV], late)
    out_ref[pl.ds(9, DEV, stride=S4), :] = jnp.concatenate([cross, gram_ref[0:64, :]], axis=0)


def total_kernel(recv_ref, out_ref):
    first = jnp.sum(recv_ref[pl.ds(9, DEV, stride=S4), :], axis=0, keepdims=True)
    second = jnp.sum(recv_ref[pl.ds(8, DEV, stride=S4), :], axis=0, keepdims=True)
    out_ref[pl.ds(0, DEV, stride=2), :] = jnp.broadcast_to(first, (DEV, 128))
    out_ref[pl.ds(1, DEV, stride=2), :] = jnp.broadcast_to(second, (DEV, 128))


def unpack_kernel(key_ref, recv_ref, out_ref, mark, value):
    lane = iota((DEV, 128), 1) < 64
    for j in range(9):
        got = recv_ref[pl.ds(j, DEV, stride=S4), :]
        hi, lo = split(got)
        hi, lo = hi.astype(F32), lo.astype(F32)
        value[2 * j * DEV : (2 * j + 1) * DEV, :] = jnp.where(
            lane, hi, pltpu.roll(lo, 64, 1)
        ).astype(BF16)
        if j < 8:
            value[(2 * j + 1) * DEV : (2 * j + 2) * DEV, :] = jnp.where(
                lane, pltpu.roll(hi, 64, 1), lo
            ).astype(BF16)
    key = key_ref[...]
    for k in range(CAP):
        mark[:, k * DEV : (k + 1) * DEV] = onehot(
            jnp.broadcast_to(key, (ROWS, DEV)) == iota((ROWS, DEV), 1) + k * DEV
        )
    solved = both(nn(mark[...], value[...]))
    for c in range(16):
        out_ref[:, c * 128 : (c + 1) * 128] = solved[c * 128 : (c + 1) * 128].T[0:64]
    out_ref[:, SPAN:ROWS] = solved[SPAN:ROWS].T[0:64]


def finish_kernel(
    recv_ref, solved_ref, now_ref, before_ref, coupling_ref, proj_ref, factor_ref, next_ref, value
):
    first = recv_ref[pl.ds(0, DEV, stride=2), :]
    second = recv_ref[pl.ds(1, DEV, stride=2), :]
    count = 1.0 / (ROWS * DEV)
    s_b = first[0:64, 0:64] * count
    s_a = first[0:64, 64:128] * count
    b_b = first[64:128, 0:64] * count
    b_a = first[64:128, 64:128] * count
    s_s = second[0:64, 64:128] * count
    a_a = second[64:128, 64:128] * count
    coupling = coupling_ref[...]
    proj_ref[...] = s_b.T
    line_s = s_s - nt32(s_b, s_b) - nt32(coupling, s_a)
    line_b = s_b - nn32(s_b, b_b) - nt32(coupling, b_a)
    line_a = s_a - nn32(s_b, b_a) - nn32(coupling, a_a)
    gram = line_s - nt32(line_b, s_b) - nt32(line_a, coupling)
    eye = iota((64, 64), 0) == iota((64, 64), 1)
    work = jnp.concatenate([gram, jnp.where(eye, 1.0, 0.0)], axis=1)
    below = iota((64, 128), 0)
    for j in range(63):
        row = work[j : j + 1, :]
        ratio = work[:, j : j + 1] / row[:, j : j + 1]
        work = work - jnp.where(below > j, ratio * row, 0.0)
    scale = lax.rsqrt(jnp.sum(jnp.where(eye, work[:, 0:64], 0.0), axis=1, keepdims=True))
    work = work * scale
    factor_ref[...] = jnp.where(iota((64, 64), 0) <= iota((64, 64), 1), work[:, 0:64], 0.0)
    inverse = work[:, 64:128]
    weight = jnp.concatenate(
        [inverse, -nn32(inverse, s_b), -nn32(inverse, coupling)], axis=1
    )
    hi, lo = split(weight)
    weight = jnp.concatenate([hi, lo], axis=0)
    for b, ref in enumerate((solved_ref, now_ref, before_ref)):
        hi, lo = split(ref[...])
        value[b * 64 : (b + 1) * 64, 0:ROWS] = hi
        value[b * 64 : (b + 1) * 64, PAD : PAD + ROWS] = lo
    high = nn(weight, value[:, 0:ROWS])
    low = nn(weight, value[:, PAD : PAD + ROWS])
    total = high + low
    next_ref[...] = total[0:64] + total[64:128]


def vmem(count):
    return [pl.BlockSpec(memory_space=pltpu.VMEM)] * count


def call(kernel, outs, operands, scratch=(), scalars=0, limit=56):
    return pl.pallas_call(
        kernel,
        out_shape=[jax.ShapeDtypeStruct(shape, dtype) for shape, dtype in outs],
        in_specs=[pl.BlockSpec(memory_space=pltpu.SMEM)] * scalars
        + vmem(len(operands) - scalars),
        out_specs=vmem(len(outs)),
        scratch_shapes=list(scratch),
        compiler_params=pltpu.CompilerParams(vmem_limit_bytes=limit * MIB),
    )(*operands)


def exchange(x, lines):
    return lax.all_to_all(
        x.reshape(DEV, 1, lines * 128), AXES, split_axis=0, concat_axis=0, tiled=True
    ).reshape(DEV * lines, 128)


def per_device(
    block_now,
    block_before,
    coupling,
    vertex_to_tree,
    tree_to_vertex,
    leaf_inverse,
    leaf_below,
    leaf_rows,
    sep_inverse,
    sep_parent,
):
    my_group = lax.axis_index("leaf")
    my_front = lax.axis_index("front")
    home_slot = jnp.zeros((), jnp.int32)
    for bit in range(LEVELS - 1):
        home_slot = home_slot + (my_group % (2 << bit) == 0).astype(jnp.int32)
    home_at = (home_slot * LEAF + my_front * SHARE).astype(jnp.int32).reshape(1)
    half = (my_group // 8).astype(jnp.int32).reshape(1)
    V = pltpu.VMEM
    packed, key = call(
        pack_kernel,
        [((DEV * S1, 128), F32), ((1, ROWS), jnp.int32)],
        (vertex_to_tree.reshape(1, ROWS), block_now, block_before),
        [V((8, PAD), jnp.int32), V((DEV, PAD), BF16), V((256, PAD), BF16), V((PAD, PAD), BF16)],
    )
    (own_gram,) = call(
        own_gram_kernel, [((128, 128), F32)], (block_now, block_before), [V((256, ROWS), BF16)]
    )
    arrived = exchange(packed, S1)
    pushed, leaf_solved, tree, idx = call(
        forward_kernel,
        [((DEV * S2, 128), F32), ((64, SPAN), F32), ((ROWS, 128), F32), ((DEV, 128), F32)],
        (home_at, arrived, leaf_inverse, leaf_below, leaf_rows),
        [V((ROWS, PAD), BF16), V((PAD, 256), BF16), V((PATH, SPAN), BF16), V((SPAN, 128), BF16)],
        1,
    )
    pushed = exchange(pushed, S2)
    (paths,) = call(
        separator_kernel,
        [((DEV * S3, 128), F32)],
        (half, pushed, sep_inverse, sep_parent),
        (),
        1,
    )
    paths = exchange(paths, S3)
    (returning,) = call(
        backward_kernel,
        [((DEV * S4, 128), F32)],
        (home_at, paths, leaf_inverse, leaf_below, leaf_rows, leaf_solved, tree, idx, own_gram),
        [
            V((64, PATH), F32),
            V((128, PATH), BF16),
            V((PATH, SPAN), BF16),
            V((PAD, PAD), BF16),
            V((128, PAD), BF16),
            V((PAD, 256), BF16),
        ],
        1,
    )
    returned = exchange(returning, S4)
    (sums,) = call(total_kernel, [((DEV * 2, 128), F32)], (returned,))
    sums = exchange(sums, 2)
    (solved,) = call(
        unpack_kernel,
        [((64, ROWS), F32)],
        (key.reshape(ROWS, 1), returned),
        [V((ROWS, PAD), BF16), V((PAD, 128), BF16)],
    )
    return tuple(
        call(
            finish_kernel,
            [((64, 64), F32), ((64, 64), F32), ((64, ROWS), F32)],
            (sums, solved, block_now, block_before, coupling),
            [V((192, 2 * PAD), BF16)],
        )
    )


def solution(mesh):
    placed = (
        P(None, AXES),
        P(None, AXES),
        P(),
        P(AXES),
        P(AXES),
        P(AXES, None, None),
        P(AXES, None, None),
        P(AXES, None),
        P(),
        P(),
    )
    return jax.shard_map(
        per_device,
        mesh=mesh,
        in_specs=placed,
        out_specs=(P(), P(), P(None, AXES)),
        check_vma=False,
    )
```

time: 704 us -> 162 us (0.23); the launches traced: 695 us -> 162 us
  blocking collectives: 242 us -> 20.6 us
  local copies, waits for them, and re-layouts: 185 us -> 5.93 us
  other arithmetic: 66.9 us -> 0 us
  waiting for transfers between devices: 111 us -> 46.8 us
  Pallas kernels: 0 us -> 61.9 us
  matrix products: 41.3 us -> 0 us
  between operations: 15 us -> 0.74 us
    gather x64 -> x0, local copies, waits for them, and re-layouts: 160 us -> none  [the longest x24 27.6 us: place_tables(): first_slot = jnp.searchsorted(ranked, device_ids, side='left')]
    psum x2 -> x0, blocking collectives: 126 us -> none  [the longest x1 63.1 us: per_device(): lax.psum(jnp.einsum('kn,jn->kj', block_now, solved_block, precision=HIGHE...]
    all_gather x6 -> x0, blocking collectives: 94.7 us -> none  [the longest x5 81.5 us: per_device(): lax.all_gather(-pending[:, path_slot], 'front', axis=1, tiled=True)]
    reduce_scatter x5 -> x0, waiting for transfers between devices: 92.1 us -> none  [the longest x4 67.9 us: per_device(): lax.psum_scatter(partial_update, 'front', scatter_dimension=1, tiled=True)]
    pallas_call x0 -> x8, Pallas kernels: none -> 61.9 us  [call(): pl.pallas_call(kernel, out_shape=[jax.ShapeDtypeStruct(shape, dtype) for...]
    dot_general x26 -> x0, matrix products: 39.9 us -> none  [the longest x4 7.73 us: per_device(): jnp.einsum('ij,kj->ki', link_columns, values, precision=HIGHEST)]
    all_to_all x1 -> x4, waiting for transfers between devices: 13.8 us -> 46.8 us  [exchange(): lax.all_to_all(x.reshape(DEV, 1, lines * 128), AXES, split_axis=0, concat...]
    sort x4 -> x0, other arithmetic: 23.8 us -> none  [the longest x2 12.3 us: place_tables(): ordering = jnp.argsort(sort_keys)]
  transfers between devices with their start and end apart: 10 -> 4, of which waited for: 8 -> 4; matrix products, arithmetic and copies ran while one was open for 7% -> 1% of each run, Pallas kernels for 0% -> 5%
where the time goes in v1:
time: 162 us
  Pallas kernels  61.9 us (38%)
  waiting for transfers between devices  46.8 us (29%)
  starting transfers between devices  25.7 us (16%)
  blocking collectives  20.6 us (13%)
  local copies, waits for them, and re-layouts  5.93 us (4%)
    pallas_call x8, Pallas kernels, call(): pl.pallas_call(kernel, out_shape=[jax.ShapeDtypeStruct(shape, dtype) for...  61.9 us
    all_to_all x4, waiting for transfers between devices, exchange(): lax.all_to_all(x.reshape(DEV, 1, lines * 128), AXES, split_axis=0, concat...  46.8 us
    all_to_all x4, starting transfers between devices, exchange(): lax.all_to_all(x.reshape(DEV, 1, lines * 128), AXES, split_axis=0, concat...  25.7 us
    all_to_all x1, blocking collectives, exchange(): lax.all_to_all(x.reshape(DEV, 1, lines * 128), AXES, split_axis=0, concat...  20.6 us
    unnamed x10, local copies, waits for them, and re-layouts  3.25 us
  transfers between devices with their start and end apart: 4, of which 4 were waited for; matrix products, arithmetic and copies ran while one was open for 1% of the time, Pallas kernels for 5%

profile of v1, /device:TPU:1, one launch (start us, length us, event | category | flops | bytes accessed | tf_op | source)
XLA Modules:
  0.0 161.6 jit_solution(11291420796210277895)
XLA Ops:
  0.6 1.3 reshape.50.vt_ref
  1.9 8.5 %shard_map.112 = (f32[2304,128]{1,0:T(8,128)}, s32[1,2080]{1,0:T(1,128)}) custom-call(s32[1,2080]{1,0:T(1,128)} %reshape.50.vt_ref, f32[64,2080]{1,0:T(8,128)} %now_ref.5, f32[64,2080]{1,0:T(8,128)} %before_ref.5), custom_call_target="tpu_custom_call" | custom-call | tf_op jit(solution)/shard_map/pallas_call | solution.py:427
  10.5 11.5 %all-to-all-start = ((f32[128,1,2304]{2,1,0:T(1,128)}), f32[128,1,2304]{2,1,0:T(1,128)S(1)}, u32[]{:S(2)}, u32[]{:S(2)}) async-start(f32[128,1,2304]{2,1,0:T(1,128)} %bitcast.20), calls=%async_computation | async-start | bytes 2359296 | tf_op jit(solution)/shard_map/all_to_all | solution.py:439
  22.0 20.4 %all-to-all-done = f32[128,1,2304]{2,1,0:T(1,128)S(1)} async-done(((f32[128,1,2304]{2,1,0:T(1,128)}), f32[128,1,2304]{2,1,0:T(1,128)S(1)}, u32[]{:S(2)}, u32[]{:S(2)}) %all-to-all-start) | async-done | bytes 1179680 | tf_op jit(solution)/shard_map/all_to_all | solution.py:439
  42.5 0.0 copy-start
  42.5 1.0 copy-done
  43.5 15.7 %shard_map.113 = (f32[1280,128]{1,0:T(8,128)}, f32[64,2048]{1,0:T(8,128)}, f32[2080,128]{1,0:T(8,128)}, f32[128,128]{1,0:T(8,128)}) custom-call(s32[1]{0:T(128)} %bitcast.home_ref, f32[2304,128]{1,0:T(8,128)} %bitcast.15, f32[8,256,256]{2,1,0:T(8,128)} %inv_ref.5, f32[8,256,256]{2,1,0:T(8,128)} %below_ref.3, s32[8,256]{1,0:T(8,128)} %rows_ref.3), custom_call_target="tpu_custom_call" | custom-call | tf_op jit(solution)/shard_map/pallas_call | solution.py:427
  59.2 4.7 %all-to-all-start.1 = ((f32[128,1,1280]{2,1,0:T(1,128)}), f32[128,1,1280]{2,1,0:T(1,128)S(1)}, u32[]{:S(2)}, u32[]{:S(2)}) async-start(f32[128,1,1280]{2,1,0:T(1,128)} %bitcast.21), calls=%async_computation.1 | async-start | bytes 1310720 | tf_op jit(solution)/shard_map/all_to_all | solution.py:439
  63.9 14.9 %all-to-all-done.1 = f32[128,1,1280]{2,1,0:T(1,128)S(1)} async-done(((f32[128,1,1280]{2,1,0:T(1,128)}), f32[128,1,1280]{2,1,0:T(1,128)S(1)}, u32[]{:S(2)}, u32[]{:S(2)}) %all-to-all-start.1) | async-done | bytes 655392 | tf_op jit(solution)/shard_map/all_to_all | solution.py:439
  78.8 0.0 copy-start.1
  78.8 0.8 copy-done.1
  79.7 8.9 %shard_map.114 = f32[640,128]{1,0:T(8,128)} custom-call(s32[1]{0:T(128)} %bitcast.1.half_ref, f32[1280,128]{1,0:T(8,128)} %bitcast.16, f32[16,256,256]{2,1,0:T(8,128)} %inv_ref.4, f32[15,256,256]{2,1,0:T(8,128)} %parent_ref.1), custom_call_target="tpu_custom_call" | custom-call | tf_op jit(solution)/shard_map/pallas_call | solution.py:427
  88.6 4.8 %all-to-all-start.2 = ((f32[128,1,640]{2,1,0:T(1,128)}), f32[128,1,640]{2,1,0:T(1,128)S(1)}, u32[]{:S(2)}, u32[]{:S(2)}) async-start(f32[128,1,640]{2,1,0:T(1,128)} %bitcast.19), calls=%async_computation.2 | async-start | bytes 655360 | tf_op jit(solution)/shard_map/all_to_all | solution.py:439
  93.3 2.4 %shard_map.115.gram_ref = f32[128,128]{1,0:T(8,128)} custom-call(f32[64,2080]{1,0:T(8,128)} %now_ref.5, f32[64,2080]{1,0:T(8,128)} %before_ref.5), custom_call_target="tpu_custom_call" | custom-call | tf_op jit(solution)/shard_map/pallas_call | solution.py:427
  95.7 9.1 %all-to-all-done.2 = f32[128,1,640]{2,1,0:T(1,128)S(1)} async-done(((f32[128,1,640]{2,1,0:T(1,128)}), f32[128,1,640]{2,1,0:T(1,128)S(1)}, u32[]{:S(2)}, u32[]{:S(2)}) %all-to-all-start.2) | async-done | bytes 327712 | tf_op jit(solution)/shard_map/all_to_all | solution.py:439
  104.8 0.0 copy-start.2
  104.8 0.7 copy-done.2
  105.5 9.2 %shard_map.116 = f32[1280,128]{1,0:T(8,128)} custom-call(s32[1]{0:T(128)} %bitcast.home_ref, f32[640,128]{1,0:T(8,128)} %bitcast.18, f32[8,256,256]{2,1,0:T(8,128)} %inv_ref.5, f32[8,256,256]{2,1,0:T(8,128)} %below_ref.3, s32[8,256]{1,0:T(8,128)} %rows_ref.3, f32[64,2048]{1,0:T(8,128)} %get-tuple-element.11.solved_ref, ...), custom_call_target="tpu_custom_call" | custom-call | tf_op jit(solution)/shard_map/pallas_call | solution.py:427
  114.7 0.0 copy-start.4
  114.7 20.6 %all_to_all.25 = f32[128,1,1280]{2,1,0:T(1,128)} all-to-all(f32[128,1,1280]{2,1,0:T(1,128)} %bitcast.17), channel_id=1, replica_groups=mesh['leaf'=16,'front'=8] {'leaf','front'}, dimensions={0} | all-to-all | bytes 1310720 | tf_op jit(solution)/shard_map/all_to_all | solution.py:439
  135.3 1.8 %shard_map.117 = f32[256,128]{1,0:T(8,128)} custom-call(f32[1280,128]{1,0:T(8,128)} %bitcast.13), custom_call_target="tpu_custom_call" | custom-call | tf_op jit(solution)/shard_map/pallas_call | solution.py:427
  137.1 4.8 %all-to-all-start.4 = ((f32[128,1,256]{2,1,0:T(1,128)}), f32[128,1,256]{2,1,0:T(1,128)S(1)}, u32[]{:S(2)}, u32[]{:S(2)}) async-start(f32[128,1,256]{2,1,0:T(1,128)} %bitcast.23), calls=%async_computation.4 | async-start | bytes 262144 | tf_op jit(solution)/shard_map/all_to_all | solution.py:439
  141.8 0.0 copy-done.4
  141.8 1.4 copy.18.key_ref
  143.2 6.2 %shard_map.118.solved_ref = f32[64,2080]{1,0:T(8,128)} custom-call(s32[2080,1]{1,0:T(8,128)} %copy.18.key_ref, f32[1280,128]{1,0:T(8,128)} %bitcast.14), custom_call_target="tpu_custom_call" | custom-call | tf_op jit(solution)/shard_map/pallas_call | solution.py:427
  149.4 2.4 %all-to-all-done.4 = f32[128,1,256]{2,1,0:T(1,128)S(1)} async-done(((f32[128,1,256]{2,1,0:T(1,128)}), f32[128,1,256]{2,1,0:T(1,128)S(1)}, u32[]{:S(2)}, u32[]{:S(2)}) %all-to-all-start.4) | async-done | bytes 131104 | tf_op jit(solution)/shard_map/all_to_all | solution.py:439
  151.8 0.0 copy-start.3
  151.8 0.6 copy-done.3
  152.4 9.2 %shard_map.119 = (f32[64,64]{1,0:T(8,128)}, f32[64,64]{1,0:T(8,128)}, f32[64,2080]{1,0:T(8,128)}) custom-call(f32[256,128]{1,0:T(8,128)} %bitcast.22, f32[64,2080]{1,0:T(8,128)} %shard_map.118.solved_ref, f32[64,2080]{1,0:T(8,128)} %now_ref.5, f32[64,2080]{1,0:T(8,128)} %before_ref.5, f32[64,64]{1,0:T(8,128)} %coupling_ref.1), custom_call_target="tpu_custom_call" | custom-call | tf_op jit(solution)/shard_map/pallas_call | solution.py:427
Async XLA Ops:
  10.5 32.0 %all-to-all-start = ((f32[128,1,2304]{2,1,0:T(1,128)}), f32[128,1,2304]{2,1,0:T(1,128)S(1)}, u32[]{:S(2)}, u32[]{:S(2)}) async-start(f32[128,1,2304]{2,1,0:T(1,128)} %bitcast.20), calls=%async_computation | async-start | bytes 2359296 | tf_op jit(solution)/shard_map/all_to_all | solution.py:439
  42.5 1.0 copy-start
  59.2 19.6 %all-to-all-start.1 = ((f32[128,1,1280]{2,1,0:T(1,128)}), f32[128,1,1280]{2,1,0:T(1,128)S(1)}, u32[]{:S(2)}, u32[]{:S(2)}) async-start(f32[128,1,1280]{2,1,0:T(1,128)} %bitcast.21), calls=%async_computation.1 | async-start | bytes 1310720 | tf_op jit(solution)/shard_map/all_to_all | solution.py:439
  78.8 0.8 copy-start.1
  88.6 16.2 %all-to-all-start.2 = ((f32[128,1,640]{2,1,0:T(1,128)}), f32[128,1,640]{2,1,0:T(1,128)S(1)}, u32[]{:S(2)}, u32[]{:S(2)}) async-start(f32[128,1,640]{2,1,0:T(1,128)} %bitcast.19), calls=%async_computation.2 | async-start | bytes 655360 | tf_op jit(solution)/shard_map/all_to_all | solution.py:439
  104.8 0.7 copy-start.2
  114.7 27.1 %copy-start.4 = (s32[1,2080]{1,0:T(1,128)S(1)}, s32[1,2080]{1,0:T(1,128)}, u32[]{:S(2)}) copy-start(s32[1,2080]{1,0:T(1,128)} %get-tuple-element.14) | copy-start | bytes 24964
  137.1 14.7 %all-to-all-start.4 = ((f32[128,1,256]{2,1,0:T(1,128)}), f32[128,1,256]{2,1,0:T(1,128)S(1)}, u32[]{:S(2)}, u32[]{:S(2)}) async-start(f32[128,1,256]{2,1,0:T(1,128)} %bitcast.23), calls=%async_computation.4 | async-start | bytes 262144 | tf_op jit(solution)/shard_map/all_to_all | solution.py:439
  151.8 0.7 copy-start.3

commit v2 on v1

v2 whole, which is shorter than its diff:
```python
import jax
import jax.numpy as jnp
from jax import lax
from jax.experimental import pallas as pl
from jax.experimental.pallas import tpu as pltpu
from jax.sharding import PartitionSpec as P

F32 = jnp.float32
BF16 = jnp.bfloat16
HIGHEST = lax.Precision.HIGHEST
AXES = ("leaf", "front")
DEV = 128
CAP = 17
ROWS = 2080
PAD = 2176
VEC = 64
LEAF = 256
NLEAF = 8
SPAN = 2048
GROUPS = 16
FRONT = 8
SHARE = 32
LEVELS = 5
PATH = 1280
S1 = 18
S2 = 10
S3 = 5
S4 = 10
MIB = 1024 * 1024


def nn(a, b):
    return lax.dot_general(a, b, (((1,), (0,)), ((), ())), preferred_element_type=F32)


def nt(a, b):
    return lax.dot_general(a, b, (((1,), (1,)), ((), ())), preferred_element_type=F32)


def tn(a, b):
    return lax.dot_general(a, b, (((0,), (0,)), ((), ())), preferred_element_type=F32)


def nn32(a, b):
    return lax.dot_general(
        a, b, (((1,), (0,)), ((), ())), preferred_element_type=F32, precision=HIGHEST
    )


def nt32(a, b):
    return lax.dot_general(
        a, b, (((1,), (1,)), ((), ())), preferred_element_type=F32, precision=HIGHEST
    )


def split(x):
    hi = x.astype(BF16)
    lo = (x - hi.astype(F32)).astype(BF16)
    return hi, lo


def iota(shape, dim):
    return lax.broadcasted_iota(jnp.int32, shape, dim)


I16 = jnp.int16


def onehot(mask):
    return jnp.where(mask, jnp.ones((), BF16), jnp.zeros((), BF16))


def onehot32(mask):
    return jnp.where(mask, 1.0, 0.0).astype(BF16)


def mark_row(row, height, start):
    width = row.shape[1]
    wide = jnp.broadcast_to(row, (16, width)).astype(I16)
    wide = jnp.concatenate([wide] * (height // 16), axis=0)
    return onehot(wide == (iota((height, width), 0) + start).astype(I16))


def mark_column(column, width):
    height = column.shape[0]
    wide = jnp.broadcast_to(column, (height, 128)).astype(I16)
    wide = jnp.concatenate([wide] * (width // 128), axis=1)
    return onehot(wide == iota((height, width), 1).astype(I16))


def stacked(x):
    hi, lo = split(x)
    return jnp.concatenate([hi, lo], axis=0)


def both(x):
    return x + pltpu.roll(x, 64, 1)


def folded(x):
    half = x.shape[0] // 2
    return x[0:half] + x[half:]


def pack_kernel(vt_ref, now_ref, before_ref, out_ref, key_ref, dest, member, value, mark):
    dest[...] = jnp.full((8, PAD), -1, jnp.int32)
    dest[0:1, 0:ROWS] = vt_ref[...]
    target = dest[0:1, :]
    bucket = ((target.astype(F32) + 0.5) * (1.0 / ROWS)).astype(jnp.int32)
    bucket = jnp.where(target < 0, -1, bucket)
    place = target - bucket * ROWS
    member[...] = mark_row(bucket, DEV, 0)
    value[...] = jnp.zeros((4 * VEC, PAD), BF16)
    now_hi, now_lo = split(now_ref[...])
    bef_hi, bef_lo = split(before_ref[...])
    value[0:64, 0:ROWS] = now_hi
    value[64:128, 0:ROWS] = bef_hi
    value[128:192, 0:ROWS] = now_lo
    value[192:256, 0:ROWS] = bef_lo
    before = onehot32(
        (iota((128, 256), 0) < iota((128, 256), 1)) | (iota((128, 256), 1) >= 128)
    )
    carry = jnp.zeros((DEV, 128), F32)
    ranks = []
    for b in range(CAP):
        part = member[:, b * 128 : (b + 1) * 128]
        counts = nn(part, before)
        ranks.append(
            jnp.sum(part.astype(F32) * (counts[:, 0:128] + carry), axis=0, keepdims=True)
        )
        carry = carry + counts[:, 128:256]
    rank = jnp.concatenate(ranks, axis=1).astype(jnp.int32)
    key = jnp.where(target < 0, -1, rank * DEV + bucket)
    key_ref[...] = key
    for k in range(CAP):
        mark[k * DEV : (k + 1) * DEV, :] = mark_row(key, DEV, k * DEV)
    block = nt(mark[...], value[...])
    block = block[:, 0:128] + block[:, 128:256]
    for k in range(CAP):
        out_ref[pl.ds(k, DEV, stride=S1), :] = block[k * DEV : (k + 1) * DEV]
    ranked = jnp.broadcast_to(rank, (32, PAD)) == iota((32, PAD), 0)
    high = place // 64
    marks = jnp.concatenate(
        [
            jnp.where(ranked, jnp.broadcast_to(high, (32, PAD)).astype(F32), 0.0),
            jnp.where(ranked, jnp.broadcast_to(place - high * 64, (32, PAD)).astype(F32), 0.0),
            jnp.zeros((64, PAD), F32),
        ],
        axis=0,
    ).astype(BF16)
    found = nt(member[...], marks)
    where = found * 64.0 + pltpu.roll(found, 96, 1)
    lane = iota((DEV, 128), 1)
    filled = (lane.astype(F32) < carry) & (lane < CAP)
    out_ref[pl.ds(CAP, DEV, stride=S1), :] = jnp.where(filled, where, -1.0)


def forward_kernel(
    home_ref,
    recv_ref,
    inv_ref,
    below_ref,
    rows_ref,
    out_ref,
    solved_ref,
    tree_ref,
    mark,
    value,
    moved,
    update,
):
    idx = recv_ref[pl.ds(CAP, DEV, stride=S1), :].astype(jnp.int32)
    for k in range(CAP):
        got = recv_ref[pl.ds(k, DEV, stride=S1), :].T
        value[:, k * DEV : (k + 1) * DEV] = stacked(got[0:64])
        mark[k * DEV : (k + 1) * DEV, :] = mark_column(idx[:, k : k + 1], PAD)
    tree_ref[...] = folded(nn(value[...], mark[...]))
    rows = rows_ref[...].astype(F32).T.astype(jnp.int32)
    for q in range(NLEAF):
        cols = slice(q * LEAF, (q + 1) * LEAF)
        hi, lo = split(inv_ref[q])
        source = stacked(tree_ref[:, cols])
        solved = folded(nt(source, hi) + nt(source, lo))
        solved_ref[:, cols] = solved
        hi, lo = split(below_ref[q])
        solved = stacked(solved)
        update[:, cols] = stacked(folded(nt(solved, hi) + nt(solved, lo)))
        moved[cols, :] = mark_column(rows[:, q : q + 1], PATH)
    pushed = folded(nn(update[...], moved[...]))
    start = home_ref[0]
    own = pltpu.roll(tree_ref[:, SPAN:PAD], start % 128, 1)
    for j in range(S2):
        chunk = jnp.where(start // 128 == j, own, 0.0) - pushed[:, j * 128 : (j + 1) * 128]
        out_ref[pl.ds(j, DEV, stride=S2), :] = jnp.concatenate([chunk, chunk], axis=0)


def side_kernel(recv_ref, tree_ref, other_ref, gram_ref, mark, value):
    idx = recv_ref[pl.ds(CAP, DEV, stride=S1), :].astype(jnp.int32)
    for k in range(CAP):
        got = recv_ref[pl.ds(k, DEV, stride=S1), :].T
        value[:, k * DEV : (k + 1) * DEV] = stacked(got[64:128])
        mark[k * DEV : (k + 1) * DEV, :] = mark_column(idx[:, k : k + 1], PAD)
    before = folded(nn(value[...], mark[...]))
    hi, lo = split(tree_ref[...])
    other_ref[0:64, :] = hi
    other_ref[128:192, :] = lo
    hi, lo = split(before)
    other_ref[64:128, :] = hi
    other_ref[192:256, :] = lo
    gram = folded(nt(other_ref[...], other_ref[...]))
    gram_ref[...] = gram[:, 0:128] + gram[:, 128:256]


def prepare_kernel(inv_ref, parent_ref, square_ref, link_ref):
    for s in range(GROUPS):
        hi, lo = split(inv_ref[s])
        square_ref[s] = tn(hi, hi) + (tn(hi, lo) + tn(lo, hi))
        if s > 0:
            up, down = split(parent_ref[s - 1])
            link_ref[s - 1] = nn(up, hi) + (nn(up, lo) + nn(down, hi))


def to_row(column, eye):
    top = jnp.sum(jnp.where(eye, column[0:128], 0.0), axis=0, keepdims=True)
    bottom = jnp.sum(jnp.where(eye, column[128:256], 0.0), axis=0, keepdims=True)
    return jnp.concatenate([top, bottom], axis=1)


def to_column(row, eye):
    top = jnp.sum(jnp.where(eye, row[:, 0:128], 0.0), axis=1, keepdims=True)
    bottom = jnp.sum(jnp.where(eye, row[:, 128:256], 0.0), axis=1, keepdims=True)
    return jnp.concatenate([top, bottom], axis=0)


def apply(matrix, row, eye):
    product = matrix * row
    return to_row(jnp.sum(product[:, 0:128] + product[:, 128:256], axis=1, keepdims=True), eye)


def apply_t(matrix, row, eye):
    return jnp.sum(matrix * to_column(row, eye), axis=0, keepdims=True)


def separator_kernel(half_ref, recv_ref, square_ref, link_ref, out_ref):
    eye = iota((128, 128), 0) == iota((128, 128), 1)
    source = {}
    for height in range(1, LEVELS + 1):
        count = max(GROUPS >> height, 1)
        first = count if height < LEVELS else 0
        span = DEV // count
        left = recv_ref[pl.ds(2 * height - 2, DEV, stride=S2), :]
        right = recv_ref[pl.ds(2 * height - 1, DEV, stride=S2), :]
        for c in range(count):
            at = slice(c * span, (c + 1) * span)
            source[first + c] = jnp.concatenate(
                [
                    jnp.sum(left[at], axis=0, keepdims=True),
                    jnp.sum(right[at], axis=0, keepdims=True),
                ],
                axis=1,
            )
    for height in range(2, LEVELS + 1):
        count = max(GROUPS >> height, 1)
        first = count if height < LEVELS else 0
        for s in range(first, first + count):
            for c in (1,) if s == 0 else (2 * s, 2 * s + 1):
                source[s] = source[s] - apply(link_ref[c - 1], source[c], eye)
    back = {}
    for s in range(GROUPS):
        back[s] = apply_t(square_ref[s], source[s], eye)
        if s > 0:
            back[s] = back[s] - apply_t(link_ref[s - 1], back[s // 2], eye)
    upper = half_ref[0] == 1
    for jj in range(S3):
        lines = []
        for g in range(GROUPS):
            ends = []
            for j in (jj, S3 + jj):
                s = (GROUPS + g) >> (j // 2 + 1)
                ends.append(back[s][:, (j % 2) * 128 : (j % 2) * 128 + 128])
            line = jnp.where(upper, ends[1], ends[0])
            lines.append(jnp.broadcast_to(line, (FRONT, 128)))
        out_ref[pl.ds(jj, DEV, stride=S3), :] = jnp.concatenate(lines, axis=0)


def backward_kernel(
    home_ref,
    recv_ref,
    arrived_ref,
    inv_ref,
    below_ref,
    rows_ref,
    solved_ref,
    other_ref,
    gram_ref,
    out_ref,
    known,
    parts,
    moved,
    mark,
    result,
):
    for q in range(NLEAF):
        moved[:, q * LEAF : (q + 1) * LEAF] = mark_row(rows_ref[q : q + 1, :], PATH, 0)
    for h in range(2):
        for jj in range(S3):
            j = h * S3 + jj
            chunk = recv_ref[pl.ds(h * 64 * S3 + jj, 64, stride=S3), :]
            known[:, j * 128 : (j + 1) * 128] = chunk
            parts[:, j * 128 : (j + 1) * 128] = stacked(chunk)
    picked = folded(nn(parts[...], moved[...]))
    start = home_ref[0]
    tile = pl.multiple_of((start // 128) * 128, 128)
    home = pltpu.roll(known[:, pl.ds(tile, 128)], (128 - start % 128) % 128, 1)
    home = jnp.where(iota((64, 128), 1) < SHARE, home, 0.0)
    result[:, SPAN:PAD] = stacked(home)
    for q in range(NLEAF):
        cols = slice(q * LEAF, (q + 1) * LEAF)
        hi, lo = split(below_ref[q])
        rows = stacked(picked[:, cols])
        source = stacked(solved_ref[:, cols] - folded(nn(rows, hi) + nn(rows, lo)))
        hi, lo = split(inv_ref[q])
        result[:, cols] = stacked(folded(nn(source, hi) + nn(source, lo)))
    cross = folded(nt(result[...], other_ref[...]))
    cross = cross[:, 0:128] + cross[:, 128:256]
    square = both(folded(nt(result[...], result[...])))
    slots = arrived_ref[pl.ds(CAP, DEV, stride=S1), :].T.astype(jnp.int32)
    for k in range(CAP):
        mark[:, k * DEV : (k + 1) * DEV] = mark_row(slots[k : k + 1, :], PAD, 0)
    packed = folded(nn(result[...], mark[...]))
    for j in range(8):
        pair = [packed[:, k * DEV : (k + 1) * DEV] for k in (2 * j, 2 * j + 1)]
        out_ref[pl.ds(j, DEV, stride=S4), :] = jnp.concatenate(pair, axis=0).T
    last = packed[:, 16 * DEV : 17 * DEV]
    last = jnp.concatenate([last, last], axis=0).T
    late = jnp.concatenate([square, gram_ref[64:128, :]], axis=0)
    out_ref[pl.ds(8, DEV, stride=S4), :] = jnp.where(iota((DEV, 128), 1) < 64, last, late)
    out_ref[pl.ds(9, DEV, stride=S4), :] = jnp.concatenate([cross, gram_ref[0:64, :]], axis=0)


def total_kernel(recv_ref, out_ref):
    first = jnp.sum(recv_ref[pl.ds(9, DEV, stride=S4), :], axis=0, keepdims=True)
    second = jnp.sum(recv_ref[pl.ds(8, DEV, stride=S4), :], axis=0, keepdims=True)
    out_ref[pl.ds(0, DEV, stride=2), :] = jnp.broadcast_to(first, (DEV, 128))
    out_ref[pl.ds(1, DEV, stride=2), :] = jnp.broadcast_to(second, (DEV, 128))


def unpack_kernel(key_ref, recv_ref, out_ref, mark, value):
    for k in range(CAP):
        mark[k * DEV : (k + 1) * DEV, :] = mark_row(key_ref[...], DEV, k * DEV)
    for j in range(9):
        got = recv_ref[pl.ds(j, DEV, stride=S4), :].T
        value[:, 2 * j * DEV : (2 * j + 1) * DEV] = stacked(got[0:64])
        if j < 8:
            value[:, (2 * j + 1) * DEV : (2 * j + 2) * DEV] = stacked(got[64:128])
    out_ref[...] = folded(nn(value[...], mark[...]))[:, 0:ROWS]


def finish_kernel(
    recv_ref, solved_ref, now_ref, before_ref, coupling_ref, proj_ref, factor_ref, next_ref, value
):
    first = recv_ref[pl.ds(0, DEV, stride=2), :]
    second = recv_ref[pl.ds(1, DEV, stride=2), :]
    count = 1.0 / (ROWS * DEV)
    s_b = first[0:64, 0:64] * count
    s_a = first[0:64, 64:128] * count
    b_b = first[64:128, 0:64] * count
    b_a = first[64:128, 64:128] * count
    s_s = second[0:64, 64:128] * count
    a_a = second[64:128, 64:128] * count
    coupling = coupling_ref[...]
    proj_ref[...] = s_b.T
    line_s = s_s - nt32(s_b, s_b) - nt32(coupling, s_a)
    line_b = s_b - nn32(s_b, b_b) - nt32(coupling, b_a)
    line_a = s_a - nn32(s_b, b_a) - nn32(coupling, a_a)
    gram = line_s - nt32(line_b, s_b) - nt32(line_a, coupling)
    eye = iota((64, 64), 0) == iota((64, 64), 1)
    work = jnp.concatenate([gram, jnp.where(eye, 1.0, 0.0)], axis=1)
    done = []
    for b in range(8):
        height = 64 - 8 * b
        at = 8 * b
        columns = [
            jnp.broadcast_to(work[:, at + c : at + c + 1], (height, 128)) for c in range(8)
        ]
        below = iota((height, 128), 0)
        for c in range(8):
            ratio = jnp.where(below > c, columns[c] * (1.0 / columns[c][c : c + 1, :]), 0.0)
            work = work - ratio * work[c : c + 1, :]
            for e in range(c + 1, 8):
                columns[e] = columns[e] - ratio * columns[e][c : c + 1, :]
        done.append(work[0:8])
        work = work[8:]
    work = jnp.concatenate(done, axis=0)
    scale = lax.rsqrt(jnp.sum(jnp.where(eye, work[:, 0:64], 0.0), axis=1, keepdims=True))
    work = work * scale
    factor_ref[...] = jnp.where(iota((64, 64), 0) <= iota((64, 64), 1), work[:, 0:64], 0.0)
    inverse = work[:, 64:128]
    weight = jnp.concatenate(
        [inverse, -nn32(inverse, s_b), -nn32(inverse, coupling)], axis=1
    )
    hi, lo = split(weight)
    weight = jnp.concatenate([hi, lo], axis=0)
    for b, ref in enumerate((solved_ref, now_ref, before_ref)):
        hi, lo = split(ref[...])
        value[b * 64 : (b + 1) * 64, 0:ROWS] = hi
        value[b * 64 : (b + 1) * 64, PAD : PAD + ROWS] = lo
    high = nn(weight, value[:, 0:ROWS])
    low = nn(weight, value[:, PAD : PAD + ROWS])
    total = high + low
    next_ref[...] = total[0:64] + total[64:128]


def vmem(count):
    return [pl.BlockSpec(memory_space=pltpu.VMEM)] * count


def call(kernel, outs, operands, scratch=(), scalars=0, limit=24, micros=4):
    return pl.pallas_call(
        kernel,
        out_shape=[jax.ShapeDtypeStruct(shape, dtype) for shape, dtype in outs],
        in_specs=[pl.BlockSpec(memory_space=pltpu.SMEM)] * scalars
        + vmem(len(operands) - scalars),
        out_specs=vmem(len(outs)),
        scratch_shapes=list(scratch),
        cost_estimate=pl.CostEstimate(
            flops=micros * 1000000000, bytes_accessed=micros * 3000000, transcendentals=0
        ),
        compiler_params=pltpu.CompilerParams(vmem_limit_bytes=limit * MIB),
    )(*operands)


def exchange(x, lines):
    return lax.all_to_all(
        x.reshape(DEV, 1, lines * 128), AXES, split_axis=0, concat_axis=0, tiled=True
    ).reshape(DEV * lines, 128)


def per_device(
    block_now,
    block_before,
    coupling,
    vertex_to_tree,
    tree_to_vertex,
    leaf_inverse,
    leaf_below,
    leaf_rows,
    sep_inverse,
    sep_parent,
):
    my_group = lax.axis_index("leaf")
    my_front = lax.axis_index("front")
    home_slot = jnp.zeros((), jnp.int32)
    for bit in range(LEVELS - 1):
        home_slot = home_slot + (my_group % (2 << bit) == 0).astype(jnp.int32)
    home_at = (home_slot * LEAF + my_front * SHARE).astype(jnp.int32).reshape(1)
    half = (my_group // 8).astype(jnp.int32).reshape(1)
    V = pltpu.VMEM
    packed, key = call(
        pack_kernel,
        [((DEV * S1, 128), F32), ((1, PAD), jnp.int32)],
        (vertex_to_tree.reshape(1, ROWS), block_now, block_before),
        [V((8, PAD), jnp.int32), V((DEV, PAD), BF16), V((256, PAD), BF16), V((PAD, PAD), BF16)],
    )
    arrived = exchange(packed, S1)
    square, link = call(
        prepare_kernel,
        [((GROUPS, LEAF, LEAF), F32), ((GROUPS - 1, LEAF, LEAF), F32)],
        (sep_inverse, sep_parent),
    )
    pushed, leaf_solved, tree = call(
        forward_kernel,
        [((DEV * S2, 128), F32), ((64, SPAN), F32), ((64, PAD), F32)],
        (home_at, arrived, leaf_inverse, leaf_below, leaf_rows),
        [V((PAD, PAD), BF16), V((128, PAD), BF16), V((SPAN, PATH), BF16), V((128, SPAN), BF16)],
        1,
    )
    pushed = exchange(pushed, S2)
    other, gram = call(
        side_kernel,
        [((256, PAD), BF16), ((128, 128), F32)],
        (arrived, tree),
        [V((PAD, PAD), BF16), V((128, PAD), BF16)],
    )
    (paths,) = call(
        separator_kernel,
        [((DEV * S3, 128), F32)],
        (half, pushed, square, link),
        (),
        1,
    )
    paths = exchange(paths, S3)
    (returning,) = call(
        backward_kernel,
        [((DEV * S4, 128), F32)],
        (
            home_at,
            paths,
            arrived,
            leaf_inverse,
            leaf_below,
            leaf_rows,
            leaf_solved,
            other,
            gram,
        ),
        [
            V((64, PATH), F32),
            V((128, PATH), BF16),
            V((PATH, SPAN), BF16),
            V((PAD, PAD), BF16),
            V((128, PAD), BF16),
        ],
        1,
    )
    returned = exchange(returning, S4)
    (sums,) = call(total_kernel, [((DEV * 2, 128), F32)], (returned,), micros=1)
    sums = exchange(sums, 2)
    (solved,) = call(
        unpack_kernel,
        [((64, ROWS), F32)],
        (key, returned),
        [V((PAD, PAD), BF16), V((128, PAD), BF16)],
    )
    return tuple(
        call(
            finish_kernel,
            [((64, 64), F32), ((64, 64), F32), ((64, ROWS), F32)],
            (sums, solved, block_now, block_before, coupling),
            [V((192, 2 * PAD), BF16)],
        )
    )


def solution(mesh):
    placed = (
        P(None, AXES),
        P(None, AXES),
        P(),
        P(AXES),
        P(AXES),
        P(AXES, None, None),
        P(AXES, None, None),
        P(AXES, None),
        P(),
        P(),
    )
    return jax.shard_map(
        per_device,
        mesh=mesh,
        in_specs=placed,
        out_specs=(P(), P(), P(None, AXES)),
        check_vma=False,
    )
```

time: 162 us -> 141 us (0.87)
  Pallas kernels: 61.9 us -> 29.6 us
  local copies, waits for them, and re-layouts: 5.93 us -> 22.7 us
  waiting for transfers between devices: 46.8 us -> 40 us
  starting transfers between devices: 25.7 us -> 27.4 us
    pallas_call x8 -> x9, Pallas kernels: 61.9 us -> 29.6 us  [call(): pl.pallas_call(kernel, out_shape=[jax.ShapeDtypeStruct(shape, dtype) for...]
    unnamed x10 -> x40, local copies, waits for them, and re-layouts: 3.25 us -> 22 us
    all_to_all x4, waiting for transfers between devices: 46.8 us -> 40 us  [exchange(): lax.all_to_all(x.reshape(DEV, 1, lines * 128), AXES, split_axis=0, concat...]
    all_to_all x4, starting transfers between devices: 25.7 us -> 27.4 us  [exchange(): lax.all_to_all(x.reshape(DEV, 1, lines * 128), AXES, split_axis=0, concat...]
  transfers between devices with their start and end apart: 4 -> 4, of which waited for: 4 -> 4; matrix products, arithmetic and copies ran while one was open for 1% -> 0% of each run, Pallas kernels for 5% -> 5%
where the time goes in v2:
time: 141 us; the launch traced here: 140 us
  waiting for transfers between devices  40 us (28%)
  Pallas kernels  29.6 us (21%)
  starting transfers between devices  27.4 us (19%)
  local copies, waits for them, and re-layouts  22.7 us (16%)
  blocking collectives  19.5 us (14%)
    all_to_all x4, waiting for transfers between devices, exchange(): lax.all_to_all(x.reshape(DEV, 1, lines * 128), AXES, split_axis=0, concat...  40 us
    pallas_call x9, Pallas kernels, call(): pl.pallas_call(kernel, out_shape=[jax.ShapeDtypeStruct(shape, dtype) for...  29.6 us
    all_to_all x4, starting transfers between devices, exchange(): lax.all_to_all(x.reshape(DEV, 1, lines * 128), AXES, split_axis=0, concat...  27.4 us
    unnamed x40, local copies, waits for them, and re-layouts  22 us
    all_to_all x1, blocking collectives, exchange(): lax.all_to_all(x.reshape(DEV, 1, lines * 128), AXES, split_axis=0, concat...  19.5 us
  transfers between devices with their start and end apart: 4, of which 4 were waited for; matrix products, arithmetic and copies ran while one was open for 0% of the time, Pallas kernels for 5%

profile of v2, /device:TPU:1, one launch (start us, length us, event | category | flops | bytes accessed | tf_op | source)
XLA Modules:
  0.0 140.1 jit_solution(13518173626695649604)
XLA Ops:
  0.6 0.7 reshape.47.vt_ref
  1.3 1.1 copy-done.6
  2.4 1.1 copy-done.8
  3.5 4.5 %shard_map.112 = (f32[2304,128]{1,0:T(8,128)}, s32[1,2176]{1,0:T(1,128)S(1)}) custom-call(s32[1,2080]{1,0:T(1,128)S(1)} %reshape.47.vt_ref, f32[64,2080]{1,0:T(8,128)S(1)} %copy-done.6, f32[64,2080]{1,0:T(8,128)S(1)} %copy-done.8), custom_call_target="tpu_custom_call" | custom-call | flops 4000000000 | bytes 12000000 | tf_op jit(solution)/shard_map/pallas_call | solution.py:419
  7.9 11.5 %all-to-all-start = ((f32[128,1,2304]{2,1,0:T(1,128)}), f32[128,1,2304]{2,1,0:T(1,128)S(1)}, u32[]{:S(2)}, u32[]{:S(2)}) async-start(f32[128,1,2304]{2,1,0:T(1,128)} %bitcast.2), calls=%async_computation | async-start | bytes 2359296 | tf_op jit(solution)/shard_map/all_to_all | solution.py:434
  19.5 20.4 %all-to-all-done = f32[128,1,2304]{2,1,0:T(1,128)S(1)} async-done(((f32[128,1,2304]{2,1,0:T(1,128)}), f32[128,1,2304]{2,1,0:T(1,128)S(1)}, u32[]{:S(2)}, u32[]{:S(2)}) %all-to-all-start) | async-done | bytes 1179680 | tf_op jit(solution)/shard_map/all_to_all | solution.py:434
  39.9 1.6 %copy-done.4 = f32[8,256,256]{2,1,0:T(8,128)S(1)} copy-done((f32[8,256,256]{2,1,0:T(8,128)S(1)}, f32[8,256,256]{2,1,0:T(8,128)}, u32[]{:S(2)}) %copy-start.4) | copy-done | bytes 2097176
  41.5 5.0 %shard_map.113 = (f32[1280,128]{1,0:T(8,128)}, f32[64,2048]{1,0:T(8,128)S(1)}, f32[64,2176]{1,0:T(8,128)S(1)}) custom-call(s32[1]{0:T(128)} %bitcast.home_ref, f32[2304,128]{1,0:T(8,128)S(1)} %bitcast.12, f32[8,256,256]{2,1,0:T(8,128)S(1)} %copy-done.2, f32[8,256,256]{2,1,0:T(8,128)S(1)} %copy-done.4, s32[8,256]{1,0:T(8,128)S(1)} %copy-done.11), custom_call_target="tpu_custom_call" | custom-call | flops 4000000000 | bytes 12000000 | tf_op jit(solution)/shard_map/pallas_call | solution.py:419
  46.5 0.8 copy-done.16
  47.3 0.8 copy-done.18
  48.1 4.7 %all-to-all-start.1 = ((f32[128,1,1280]{2,1,0:T(1,128)}), f32[128,1,1280]{2,1,0:T(1,128)S(1)}, u32[]{:S(2)}, u32[]{:S(2)}) async-start(f32[128,1,1280]{2,1,0:T(1,128)} %bitcast.4), calls=%async_computation.1 | async-start | bytes 1310720 | tf_op jit(solution)/shard_map/all_to_all | solution.py:434
  52.8 2.2 %copy-done = f32[16,256,256]{2,1,0:T(8,128)S(1)} copy-done((f32[16,256,256]{2,1,0:T(8,128)S(1)}, f32[16,256,256]{2,1,0:T(8,128)}, u32[]{:S(2)}) %copy-start) | copy-done | bytes 4194328
  55.0 2.1 %copy-done.1 = f32[15,256,256]{2,1,0:T(8,128)S(1)} copy-done((f32[15,256,256]{2,1,0:T(8,128)S(1)}, f32[15,256,256]{2,1,0:T(8,128)}, u32[]{:S(2)}) %copy-start.1) | copy-done | bytes 3932184
  57.1 3.4 %shard_map.114 = (f32[16,256,256]{2,1,0:T(8,128)S(1)}, f32[15,256,256]{2,1,0:T(8,128)S(1)}) custom-call(f32[16,256,256]{2,1,0:T(8,128)S(1)} %copy-done, f32[15,256,256]{2,1,0:T(8,128)S(1)} %copy-done.1), custom_call_target="tpu_custom_call" | custom-call | flops 4000000000 | bytes 12000000 | tf_op jit(solution)/shard_map/pallas_call | solution.py:419
  60.5 2.0 %copy-done.12 = f32[16,256,256]{2,1,0:T(8,128)} copy-done((f32[16,256,256]{2,1,0:T(8,128)}, f32[16,256,256]{2,1,0:T(8,128)S(1)}, u32[]{:S(2)}) %copy-start.12) | copy-done | bytes 4194328
  62.5 1.9 %copy-done.14 = f32[15,256,256]{2,1,0:T(8,128)} copy-done((f32[15,256,256]{2,1,0:T(8,128)}, f32[15,256,256]{2,1,0:T(8,128)S(1)}, u32[]{:S(2)}) %copy-start.14) | copy-done | bytes 3932184
  64.4 3.4 %all-to-all-done.1 = f32[128,1,1280]{2,1,0:T(1,128)S(1)} async-done(((f32[128,1,1280]{2,1,0:T(1,128)}), f32[128,1,1280]{2,1,0:T(1,128)S(1)}, u32[]{:S(2)}, u32[]{:S(2)}) %all-to-all-start.1) | async-done | bytes 655392 | tf_op jit(solution)/shard_map/all_to_all | solution.py:434
  67.8 2.2 %copy-done.13 = f32[16,256,256]{2,1,0:T(8,128)S(1)} copy-done((f32[16,256,256]{2,1,0:T(8,128)S(1)}, f32[16,256,256]{2,1,0:T(8,128)}, u32[]{:S(2)}) %copy-start.13) | copy-done | bytes 4194328
  70.0 2.1 %copy-done.15 = f32[15,256,256]{2,1,0:T(8,128)S(1)} copy-done((f32[15,256,256]{2,1,0:T(8,128)S(1)}, f32[15,256,256]{2,1,0:T(8,128)}, u32[]{:S(2)}) %copy-start.15) | copy-done | bytes 3932184
  72.1 3.4 %shard_map.115 = f32[640,128]{1,0:T(8,128)} custom-call(s32[1]{0:T(128)} %bitcast.1.half_ref, f32[1280,128]{1,0:T(8,128)S(1)} %bitcast.15, f32[16,256,256]{2,1,0:T(8,128)S(1)} %copy-done.13, f32[15,256,256]{2,1,0:T(8,128)S(1)} %copy-done.15), custom_call_target="tpu_custom_call" | custom-call | flops 4000000000 | bytes 12000000 | tf_op jit(solution)/shard_map/pallas_call | solution.py:419
  75.4 6.4 %all-to-all-start.2 = ((f32[128,1,640]{2,1,0:T(1,128)}), f32[128,1,640]{2,1,0:T(1,128)S(1)}, u32[]{:S(2)}, u32[]{:S(2)}) async-start(f32[128,1,640]{2,1,0:T(1,128)} %bitcast.6), calls=%async_computation.2 | async-start | bytes 655360 | tf_op jit(solution)/shard_map/all_to_all | solution.py:434
  81.9 1.0 copy-done.19
  82.9 2.4 %shard_map.116 = (bf16[256,2176]{1,0:T(8,128)(2,1)S(1)}, f32[128,128]{1,0:T(8,128)S(1)}) custom-call(f32[2304,128]{1,0:T(8,128)S(1)} %bitcast.13, f32[64,2176]{1,0:T(8,128)S(1)} %copy-done.19), custom_call_target="tpu_custom_call" | custom-call | flops 4000000000 | bytes 12000000 | tf_op jit(solution)/shard_map/pallas_call | solution.py:419
  85.3 8.0 %all-to-all-done.2 = f32[128,1,640]{2,1,0:T(1,128)S(1)} async-done(((f32[128,1,640]{2,1,0:T(1,128)}), f32[128,1,640]{2,1,0:T(1,128)S(1)}, u32[]{:S(2)}, u32[]{:S(2)}) %all-to-all-start.2) | async-done | bytes 327712 | tf_op jit(solution)/shard_map/all_to_all | solution.py:434
  93.3 1.6 %copy-done.3 = f32[8,256,256]{2,1,0:T(8,128)S(1)} copy-done((f32[8,256,256]{2,1,0:T(8,128)S(1)}, f32[8,256,256]{2,1,0:T(8,128)}, u32[]{:S(2)}) %copy-start.3) | copy-done | bytes 2097176
  94.9 1.6 %copy-done.5 = f32[8,256,256]{2,1,0:T(8,128)S(1)} copy-done((f32[8,256,256]{2,1,0:T(8,128)S(1)}, f32[8,256,256]{2,1,0:T(8,128)}, u32[]{:S(2)}) %copy-start.5) | copy-done | bytes 2097176
  96.5 4.2 %shard_map.117 = f32[1280,128]{1,0:T(8,128)S(1)} custom-call(s32[1]{0:T(128)} %bitcast.home_ref, f32[640,128]{1,0:T(8,128)S(1)} %bitcast.19, f32[2304,128]{1,0:T(8,128)S(1)} %bitcast.14, f32[8,256,256]{2,1,0:T(8,128)S(1)} %copy-done.3, f32[8,256,256]{2,1,0:T(8,128)S(1)} %copy-done.5, s32[8,256]{1,0:T(8,128)S(1)} %copy-done.11, f32[64,2048]{1,0:T(8,128)S(1)} %copy-done.17, ...), custom_call_target="tpu_custom_call" | custom-call | flops 4000000000 | bytes 12000000 | tf_op jit(solution)/shard_map/pallas_call | solution.py:419
  100.7 19.5 %all_to_all.25 = f32[128,1,1280]{2,1,0:T(1,128)S(1)} all-to-all(f32[128,1,1280]{2,1,0:T(1,128)S(1)} %bitcast.18), channel_id=1, replica_groups=mesh['leaf'=16,'front'=8] {'leaf','front'}, dimensions={0} | all-to-all | bytes 1310720 | tf_op jit(solution)/shard_map/all_to_all | solution.py:434
  120.9 4.8 %all-to-all-start.4 = ((f32[128,1,256]{2,1,0:T(1,128)}), f32[128,1,256]{2,1,0:T(1,128)S(1)}, u32[]{:S(2)}, u32[]{:S(2)}) async-start(f32[128,1,256]{2,1,0:T(1,128)} %bitcast.10), calls=%async_computation.4 | async-start | bytes 262144 | tf_op jit(solution)/shard_map/all_to_all | solution.py:434
  125.7 1.7 %shard_map.119.solved_ref = f32[64,2080]{1,0:T(8,128)S(1)} custom-call(s32[1,2176]{1,0:T(1,128)S(1)} %get-tuple-element.20.key_ref, f32[1280,128]{1,0:T(8,128)S(1)} %bitcast.17), custom_call_target="tpu_custom_call" | custom-call | flops 4000000000 | bytes 12000000 | tf_op jit(solution)/shard_map/pallas_call | solution.py:419
  127.4 8.2 %all-to-all-done.4 = f32[128,1,256]{2,1,0:T(1,128)S(1)} async-done(((f32[128,1,256]{2,1,0:T(1,128)}), f32[128,1,256]{2,1,0:T(1,128)S(1)}, u32[]{:S(2)}, u32[]{:S(2)}) %all-to-all-start.4) | async-done | bytes 131104 | tf_op jit(solution)/shard_map/all_to_all | solution.py:434
  135.6 4.5 %shard_map.120 = (f32[64,64]{1,0:T(8,128)}, f32[64,64]{1,0:T(8,128)}, f32[64,2080]{1,0:T(8,128)}) custom-call(f32[256,128]{1,0:T(8,128)S(1)} %bitcast.20, f32[64,2080]{1,0:T(8,128)S(1)} %shard_map.119.solved_ref, f32[64,2080]{1,0:T(8,128)S(1)} %copy-done.7, f32[64,2080]{1,0:T(8,128)S(1)} %copy-done.9, f32[64,64]{1,0:T(8,128)S(1)} %copy-done.10), custom_call_target="tpu_custom_call" | custom-call | flops 4000000000 | bytes 12000000 | tf_op jit(solution)/shard_map/pallas_call | solution.py:419
  (27 shorter events, 0.7 us)
Async XLA Ops:
  1.3 1.1 copy-start.6
  2.4 1.1 copy-start.8
  7.9 32.0 %copy-start.2 = (f32[8,256,256]{2,1,0:T(8,128)S(1)}, f32[8,256,256]{2,1,0:T(8,128)}, u32[]{:S(2)}) copy-start(f32[8,256,256]{2,1,0:T(8,128)} %inv_ref.5) | copy-start | bytes 6291460
  7.9 32.0 %copy-start.11 = (s32[8,256]{1,0:T(8,128)S(1)}, s32[8,256]{1,0:T(8,128)}, u32[]{:S(2)}) copy-start(s32[8,256]{1,0:T(8,128)} %rows_ref.3) | copy-start | bytes 24580
  7.9 32.0 %all-to-all-start = ((f32[128,1,2304]{2,1,0:T(1,128)}), f32[128,1,2304]{2,1,0:T(1,128)S(1)}, u32[]{:S(2)}, u32[]{:S(2)}) async-start(f32[128,1,2304]{2,1,0:T(1,128)} %bitcast.2), calls=%async_computation | async-start | bytes 2359296 | tf_op jit(solution)/shard_map/all_to_all | solution.py:434
  39.9 1.6 %copy-start.4 = (f32[8,256,256]{2,1,0:T(8,128)S(1)}, f32[8,256,256]{2,1,0:T(8,128)}, u32[]{:S(2)}) copy-start(f32[8,256,256]{2,1,0:T(8,128)} %below_ref.3) | copy-start | bytes 6291460
  46.5 0.8 copy-start.16
  47.3 0.8 copy-start.18
  48.1 19.6 %all-to-all-start.1 = ((f32[128,1,1280]{2,1,0:T(1,128)}), f32[128,1,1280]{2,1,0:T(1,128)S(1)}, u32[]{:S(2)}, u32[]{:S(2)}) async-start(f32[128,1,1280]{2,1,0:T(1,128)} %bitcast.4), calls=%async_computation.1 | async-start | bytes 1310720 | tf_op jit(solution)/shard_map/all_to_all | solution.py:434
  52.8 2.2 %copy-start = (f32[16,256,256]{2,1,0:T(8,128)S(1)}, f32[16,256,256]{2,1,0:T(8,128)}, u32[]{:S(2)}) copy-start(f32[16,256,256]{2,1,0:T(8,128)} %inv_ref.4) | copy-start | bytes 12582916
  55.0 2.1 %copy-start.1 = (f32[15,256,256]{2,1,0:T(8,128)S(1)}, f32[15,256,256]{2,1,0:T(8,128)}, u32[]{:S(2)}) copy-start(f32[15,256,256]{2,1,0:T(8,128)} %parent_ref.1) | copy-start | bytes 11796484
  60.5 2.0 %copy-start.12 = (f32[16,256,256]{2,1,0:T(8,128)}, f32[16,256,256]{2,1,0:T(8,128)S(1)}, u32[]{:S(2)}) copy-start(f32[16,256,256]{2,1,0:T(8,128)S(1)} %get-tuple-element.14.square_ref) | copy-start | bytes 12582916
  62.5 1.9 %copy-start.14 = (f32[15,256,256]{2,1,0:T(8,128)}, f32[15,256,256]{2,1,0:T(8,128)S(1)}, u32[]{:S(2)}) copy-start(f32[15,256,256]{2,1,0:T(8,128)S(1)} %get-tuple-element.15.link_ref) | copy-start | bytes 11796484
  67.8 2.2 %copy-start.13 = (f32[16,256,256]{2,1,0:T(8,128)S(1)}, f32[16,256,256]{2,1,0:T(8,128)}, u32[]{:S(2)}) copy-start(f32[16,256,256]{2,1,0:T(8,128)} %copy-done.12) | copy-start | bytes 12582916
  70.0 2.1 %copy-start.15 = (f32[15,256,256]{2,1,0:T(8,128)S(1)}, f32[15,256,256]{2,1,0:T(8,128)}, u32[]{:S(2)}) copy-start(f32[15,256,256]{2,1,0:T(8,128)} %copy-done.14) | copy-start | bytes 11796484
  75.4 17.9 %all-to-all-start.2 = ((f32[128,1,640]{2,1,0:T(1,128)}), f32[128,1,640]{2,1,0:T(1,128)S(1)}, u32[]{:S(2)}, u32[]{:S(2)}) async-start(f32[128,1,640]{2,1,0:T(1,128)} %bitcast.6), calls=%async_computation.2 | async-start | bytes 655360 | tf_op jit(solution)/shard_map/all_to_all | solution.py:434
  81.9 1.1 copy-start.19
  82.9 10.4 %copy-start.17 = (f32[64,2048]{1,0:T(8,128)S(1)}, f32[64,2048]{1,0:T(8,128)}, u32[]{:S(2)}) copy-start(f32[64,2048]{1,0:T(8,128)} %copy-done.16) | copy-start | bytes 1572868
  93.3 1.6 %copy-start.3 = (f32[8,256,256]{2,1,0:T(8,128)S(1)}, f32[8,256,256]{2,1,0:T(8,128)}, u32[]{:S(2)}) copy-start(f32[8,256,256]{2,1,0:T(8,128)} %inv_ref.5) | copy-start | bytes 6291460
  94.9 1.6 %copy-start.5 = (f32[8,256,256]{2,1,0:T(8,128)S(1)}, f32[8,256,256]{2,1,0:T(8,128)}, u32[]{:S(2)}) copy-start(f32[8,256,256]{2,1,0:T(8,128)} %below_ref.3) | copy-start | bytes 6291460
  120.9 14.7 %all-to-all-start.4 = ((f32[128,1,256]{2,1,0:T(1,128)}), f32[128,1,256]{2,1,0:T(1,128)S(1)}, u32[]{:S(2)}, u32[]{:S(2)}) async-start(f32[128,1,256]{2,1,0:T(1,128)} %bitcast.10), calls=%async_computation.4 | async-start | bytes 262144 | tf_op jit(solution)/shard_map/all_to_all | solution.py:434
  125.6 10.0 %copy-start.7 = (f32[64,2080]{1,0:T(8,128)S(1)}, f32[64,2080]{1,0:T(8,128)}, u32[]{:S(2)}) copy-start(f32[64,2080]{1,0:T(8,128)} %now_ref.3) | copy-start | bytes 1597444
  125.6 9.9 %copy-start.9 = (f32[64,2080]{1,0:T(8,128)S(1)}, f32[64,2080]{1,0:T(8,128)}, u32[]{:S(2)}) copy-start(f32[64,2080]{1,0:T(8,128)} %before_ref.3) | copy-start | bytes 1597444
  125.7 9.9 %copy-start.10 = (f32[64,64]{1,0:T(8,128)S(1)}, f32[64,64]{1,0:T(8,128)}, u32[]{:S(2)}) copy-start(f32[64,64]{1,0:T(8,128)} %coupling_ref.1) | copy-start | bytes 49156

commit v3 on v2

--- a/solution.py
+++ b/solution.py
@@ -102,7 +102,16 @@
     return x[0:half] + x[half:]
 
 
-def pack_kernel(vt_ref, now_ref, before_ref, out_ref, key_ref, dest, member, value, mark):
+def fetch(source, target, sem):
+    copy = pltpu.make_async_copy(source, target, sem)
+    copy.start()
+    return copy
+
+
+def pack_kernel(
+    vt_ref, now_hbm, before_hbm, out_ref, key_ref, dest, member, value, mark, now, before, sems
+):
+    loads = [fetch(now_hbm, now, sems.at[0]), fetch(before_hbm, before, sems.at[1])]
     dest[...] = jnp.full((8, PAD), -1, jnp.int32)
     dest[0:1, 0:ROWS] = vt_ref[...]
     target = dest[0:1, :]
@@ -110,21 +119,14 @@
     bucket = jnp.where(target < 0, -1, bucket)
     place = target - bucket * ROWS
     member[...] = mark_row(bucket, DEV, 0)
-    value[...] = jnp.zeros((4 * VEC, PAD), BF16)
-    now_hi, now_lo = split(now_ref[...])
-    bef_hi, bef_lo = split(before_ref[...])
-    value[0:64, 0:ROWS] = now_hi
-    value[64:128, 0:ROWS] = bef_hi
-    value[128:192, 0:ROWS] = now_lo
-    value[192:256, 0:ROWS] = bef_lo
-    before = onehot32(
+    earlier = onehot32(
         (iota((128, 256), 0) < iota((128, 256), 1)) | (iota((128, 256), 1) >= 128)
     )
     carry = jnp.zeros((DEV, 128), F32)
     ranks = []
     for b in range(CAP):
         part = member[:, b * 128 : (b + 1) * 128]
-        counts = nn(part, before)
+        counts = nn(part, earlier)
         ranks.append(
             jnp.sum(part.astype(F32) * (counts[:, 0:128] + carry), axis=0, keepdims=True)
         )
@@ -134,6 +136,15 @@
     key_ref[...] = key
     for k in range(CAP):
         mark[k * DEV : (k + 1) * DEV, :] = mark_row(key, DEV, k * DEV)
+    for load in loads:
+        load.wait()
+    value[:, SPAN:PAD] = jnp.zeros((4 * VEC, PAD - SPAN), BF16)
+    now_hi, now_lo = split(now[...])
+    bef_hi, bef_lo = split(before[...])
+    value[0:64, 0:ROWS] = now_hi
+    value[64:128, 0:ROWS] = bef_hi
+    value[128:192, 0:ROWS] = now_lo
+    value[192:256, 0:ROWS] = bef_lo
     block = nt(mark[...], value[...])
     block = block[:, 0:128] + block[:, 128:256]
     for k in range(CAP):
@@ -158,66 +169,111 @@
 def forward_kernel(
     home_ref,
     recv_ref,
-    inv_ref,
-    below_ref,
     rows_ref,
+    inv_hbm,
+    below_hbm,
+    ready_hbm,
     out_ref,
-    solved_ref,
-    tree_ref,
+    solved_hbm,
+    tree_hbm,
     mark,
     value,
     moved,
     update,
+    inv_ref,
+    below_ref,
+    solved_ref,
+    tree_ref,
+    sems,
 ):
+    inv_loads = [
+        fetch(inv_hbm.at[q], inv_ref.at[q], sems.at[q]) for q in range(NLEAF)
+    ]
+    below_loads = [
+        fetch(below_hbm.at[q], below_ref.at[q], sems.at[NLEAF + q]) for q in range(NLEAF)
+    ]
     idx = recv_ref[pl.ds(CAP, DEV, stride=S1), :].astype(jnp.int32)
     for k in range(CAP):
         got = recv_ref[pl.ds(k, DEV, stride=S1), :].T
         value[:, k * DEV : (k + 1) * DEV] = stacked(got[0:64])
         mark[k * DEV : (k + 1) * DEV, :] = mark_column(idx[:, k : k + 1], PAD)
     tree_ref[...] = folded(nn(value[...], mark[...]))
+    stores = [fetch(tree_ref, tree_hbm, sems.at[2 * NLEAF])]
     rows = rows_ref[...].astype(F32).T.astype(jnp.int32)
     for q in range(NLEAF):
         cols = slice(q * LEAF, (q + 1) * LEAF)
+        inv_loads[q].wait()
         hi, lo = split(inv_ref[q])
         source = stacked(tree_ref[:, cols])
         solved = folded(nt(source, hi) + nt(source, lo))
         solved_ref[:, cols] = solved
+        below_loads[q].wait()
         hi, lo = split(below_ref[q])
         solved = stacked(solved)
         update[:, cols] = stacked(folded(nt(solved, hi) + nt(solved, lo)))
         moved[cols, :] = mark_column(rows[:, q : q + 1], PATH)
+    stores.append(fetch(solved_ref, solved_hbm, sems.at[2 * NLEAF + 1]))
     pushed = folded(nn(update[...], moved[...]))
     start = home_ref[0]
     own = pltpu.roll(tree_ref[:, SPAN:PAD], start % 128, 1)
     for j in range(S2):
         chunk = jnp.where(start // 128 == j, own, 0.0) - pushed[:, j * 128 : (j + 1) * 128]
         out_ref[pl.ds(j, DEV, stride=S2), :] = jnp.concatenate([chunk, chunk], axis=0)
-
-
-def side_kernel(recv_ref, tree_ref, other_ref, gram_ref, mark, value):
-    idx = recv_ref[pl.ds(CAP, DEV, stride=S1), :].astype(jnp.int32)
+    for store in stores:
+        store.wait()
+
+
+def side_kernel(
+    recv_ref, tree_hbm, other_hbm, idx_ref, gram_ref, mark, value, tree_ref, other_ref, sems
+):
+    load = fetch(tree_hbm, tree_ref, sems.at[0])
+    where = recv_ref[pl.ds(CAP, DEV, stride=S1), :]
+    idx_ref[...] = where.T
+    idx = where.astype(jnp.int32)
     for k in range(CAP):
         got = recv_ref[pl.ds(k, DEV, stride=S1), :].T
         value[:, k * DEV : (k + 1) * DEV] = stacked(got[64:128])
         mark[k * DEV : (k + 1) * DEV, :] = mark_column(idx[:, k : k + 1], PAD)
     before = folded(nn(value[...], mark[...]))
+    load.wait()
     hi, lo = split(tree_ref[...])
     other_ref[0:64, :] = hi
     other_ref[128:192, :] = lo
     hi, lo = split(before)
     other_ref[64:128, :] = hi
     other_ref[192:256, :] = lo
+    store = fetch(other_ref, other_hbm, sems.at[1])
     gram = folded(nt(other_ref[...], other_ref[...]))
     gram_ref[...] = gram[:, 0:128] + gram[:, 128:256]
-
-
-def prepare_kernel(inv_ref, parent_ref, square_ref, link_ref):
+    store.wait()
+
+
+def prepare_kernel(
+    inv_hbm, parent_hbm, square_hbm, link_hbm, inv_ref, parent_ref, square_ref, link_ref, sems
+):
+    inv_loads = []
+    parent_loads = []
+    stores = []
     for s in range(GROUPS):
+        inv_loads.append(fetch(inv_hbm.at[s], inv_ref.at[s], sems.at[s]))
+        if s > 0:
+            at = s - 1
+            parent_loads.append(
+                fetch(parent_hbm.at[at], parent_ref.at[at], sems.at[GROUPS + at])
+            )
+    for s in range(GROUPS):
+        inv_loads[s].wait()
         hi, lo = split(inv_ref[s])
         square_ref[s] = tn(hi, hi) + (tn(hi, lo) + tn(lo, hi))
+        stores.append(fetch(square_ref.at[s], square_hbm.at[s], sems.at[2 * GROUPS + s]))
         if s > 0:
-            up, down = split(parent_ref[s - 1])
-            link_ref[s - 1] = nn(up, hi) + (nn(up, lo) + nn(down, hi))
+            at = s - 1
+            parent_loads[at].wait()
+            up, down = split(parent_ref[at])
+            link_ref[at] = nn(up, hi) + (nn(up, lo) + nn(down, hi))
+            stores.append(fetch(link_ref.at[at], link_hbm.at[at], sems.at[3 * GROUPS + at]))
+    for store in stores:
+        store.wait()
 
 
 def to_row(column, eye):
@@ -241,7 +297,15 @@
     return jnp.sum(matrix * to_column(row, eye), axis=0, keepdims=True)
 
 
-def separator_kernel(half_ref, recv_ref, square_ref, link_ref, out_ref):
+def separator_kernel(
+    half_ref, recv_ref, square_hbm, link_hbm, out_ref, square_ref, link_ref, sems
+):
+    loads = {}
+    for at in range(GROUPS - 2, -1, -1):
+        loads[at] = fetch(link_hbm.at[at], link_ref.at[at], sems.at[at])
+    square_loads = [
+        fetch(square_hbm.at[s], square_ref.at[s], sems.at[GROUPS + s]) for s in range(GROUPS)
+    ]
     eye = iota((128, 128), 0) == iota((128, 128), 1)
     source = {}
     for height in range(1, LEVELS + 1):
@@ -264,9 +328,11 @@
         first = count if height < LEVELS else 0
         for s in range(first, first + count):
             for c in (1,) if s == 0 else (2 * s, 2 * s + 1):
+                loads[c - 1].wait()
                 source[s] = source[s] - apply(link_ref[c - 1], source[c], eye)
     back = {}
     for s in range(GROUPS):
+        square_loads[s].wait()
         back[s] = apply_t(square_ref[s], source[s], eye)
         if s > 0:
             back[s] = back[s] - apply_t(link_ref[s - 1], back[s // 2], eye)
@@ -286,20 +352,32 @@
 def backward_kernel(
     home_ref,
     recv_ref,
-    arrived_ref,
-    inv_ref,
-    below_ref,
     rows_ref,
-    solved_ref,
-    other_ref,
+    idx_ref,
     gram_ref,
+    inv_hbm,
+    below_hbm,
+    solved_hbm,
+    other_hbm,
     out_ref,
     known,
     parts,
     moved,
     mark,
     result,
+    inv_ref,
+    below_ref,
+    solved_ref,
+    other_ref,
+    sems,
 ):
+    loads = [fetch(solved_hbm, solved_ref, sems.at[2 * NLEAF])]
+    below_loads = []
+    inv_loads = []
+    for q in range(NLEAF):
+        below_loads.append(fetch(below_hbm.at[q], below_ref.at[q], sems.at[q]))
+        inv_loads.append(fetch(inv_hbm.at[q], inv_ref.at[q], sems.at[NLEAF + q]))
+    loads.append(fetch(other_hbm, other_ref, sems.at[2 * NLEAF + 1]))
     for q in range(NLEAF):
         moved[:, q * LEAF : (q + 1) * LEAF] = mark_row(rows_ref[q : q + 1, :], PATH, 0)
     for h in range(2):
@@ -316,15 +394,20 @@
     result[:, SPAN:PAD] = stacked(home)
     for q in range(NLEAF):
         cols = slice(q * LEAF, (q + 1) * LEAF)
+        if q == 0:
+            loads[0].wait()
+        below_loads[q].wait()
         hi, lo = split(below_ref[q])
         rows = stacked(picked[:, cols])
         source = stacked(solved_ref[:, cols] - folded(nn(rows, hi) + nn(rows, lo)))
+        inv_loads[q].wait()
         hi, lo = split(inv_ref[q])
         result[:, cols] = stacked(folded(nn(source, hi) + nn(source, lo)))
+    loads[1].wait()
     cross = folded(nt(result[...], other_ref[...]))
     cross = cross[:, 0:128] + cross[:, 128:256]
     square = both(folded(nt(result[...], result[...])))
-    slots = arrived_ref[pl.ds(CAP, DEV, stride=S1), :].T.astype(jnp.int32)
+    slots = idx_ref[...].astype(jnp.int32)
     for k in range(CAP):
         mark[:, k * DEV : (k + 1) * DEV] = mark_row(slots[k : k + 1, :], PAD, 0)
     packed = folded(nn(result[...], mark[...]))
@@ -357,8 +440,20 @@
 
 
 def finish_kernel(
-    recv_ref, solved_ref, now_ref, before_ref, coupling_ref, proj_ref, factor_ref, next_ref, value
+    recv_ref,
+    solved_ref,
+    coupling_ref,
+    now_hbm,
+    before_hbm,
+    proj_ref,
+    factor_ref,
+    next_ref,
+    value,
+    now_ref,
+    before_ref,
+    sems,
 ):
+    loads = [fetch(now_hbm, now_ref, sems.at[0]), fetch(before_hbm, before_ref, sems.at[1])]
     first = recv_ref[pl.ds(0, DEV, stride=2), :]
     second = recv_ref[pl.ds(1, DEV, stride=2), :]
     count = 1.0 / (ROWS * DEV)
@@ -401,6 +496,8 @@
     )
     hi, lo = split(weight)
     weight = jnp.concatenate([hi, lo], axis=0)
+    for load in loads:
+        load.wait()
     for b, ref in enumerate((solved_ref, now_ref, before_ref)):
         hi, lo = split(ref[...])
         value[b * 64 : (b + 1) * 64, 0:ROWS] = hi
@@ -415,13 +512,17 @@
     return [pl.BlockSpec(memory_space=pltpu.VMEM)] * count
 
 
-def call(kernel, outs, operands, scratch=(), scalars=0, limit=24, micros=4):
+def call(kernel, outs, operands, scratch=(), scalars=0, far=0, far_outs=(), limit=52, micros=4):
+    kinds = [pltpu.SMEM] * scalars + [pltpu.VMEM] * (len(operands) - scalars - far)
+    kinds += [pltpu.HBM] * far
     return pl.pallas_call(
         kernel,
         out_shape=[jax.ShapeDtypeStruct(shape, dtype) for shape, dtype in outs],
-        in_specs=[pl.BlockSpec(memory_space=pltpu.SMEM)] * scalars
-        + vmem(len(operands) - scalars),
-        out_specs=vmem(len(outs)),
+        in_specs=[pl.BlockSpec(memory_space=kind) for kind in kinds],
+        out_specs=[
+            pl.BlockSpec(memory_space=pltpu.HBM if i in far_outs else pltpu.VMEM)
+            for i in range(len(outs))
+        ],
         scratch_shapes=list(scratch),
         cost_estimate=pl.CostEstimate(
             flops=micros * 1000000000, bytes_accessed=micros * 3000000, transcendentals=0
@@ -456,38 +557,84 @@
     home_at = (home_slot * LEAF + my_front * SHARE).astype(jnp.int32).reshape(1)
     half = (my_group // 8).astype(jnp.int32).reshape(1)
     V = pltpu.VMEM
+    S = pltpu.SemaphoreType.DMA
     packed, key = call(
         pack_kernel,
         [((DEV * S1, 128), F32), ((1, PAD), jnp.int32)],
         (vertex_to_tree.reshape(1, ROWS), block_now, block_before),
-        [V((8, PAD), jnp.int32), V((DEV, PAD), BF16), V((256, PAD), BF16), V((PAD, PAD), BF16)],
+        [
+            V((8, PAD), jnp.int32),
+            V((DEV, PAD), BF16),
+            V((256, PAD), BF16),
+            V((PAD, PAD), BF16),
+            V((64, ROWS), F32),
+            V((64, ROWS), F32),
+            S((2,)),
+        ],
+        far=2,
+        limit=58,
     )
     arrived = exchange(packed, S1)
     square, link = call(
         prepare_kernel,
         [((GROUPS, LEAF, LEAF), F32), ((GROUPS - 1, LEAF, LEAF), F32)],
         (sep_inverse, sep_parent),
+        [
+            V((GROUPS, LEAF, LEAF), F32),
+            V((GROUPS - 1, LEAF, LEAF), F32),
+            V((GROUPS, LEAF, LEAF), F32),
+            V((GROUPS - 1, LEAF, LEAF), F32),
+            S((4 * GROUPS,)),
+        ],
+        far=2,
+        far_outs=(0, 1),
     )
     pushed, leaf_solved, tree = call(
         forward_kernel,
         [((DEV * S2, 128), F32), ((64, SPAN), F32), ((64, PAD), F32)],
-        (home_at, arrived, leaf_inverse, leaf_below, leaf_rows),
-        [V((PAD, PAD), BF16), V((128, PAD), BF16), V((SPAN, PATH), BF16), V((128, SPAN), BF16)],
+        (home_at, arrived, leaf_rows, leaf_inverse, leaf_below, link),
+        [
+            V((PAD, PAD), BF16),
+            V((128, PAD), BF16),
+            V((SPAN, PATH), BF16),
+            V((128, SPAN), BF16),
+            V((NLEAF, LEAF, LEAF), F32),
+            V((NLEAF, LEAF, LEAF), F32),
+            V((64, SPAN), F32),
+            V((64, PAD), F32),
+            S((2 * NLEAF + 2,)),
+        ],
         1,
+        far=3,
+        limit=50,
+        far_outs=(1, 2),
     )
     pushed = exchange(pushed, S2)
-    other, gram = call(
+    other, idx, gram = call(
         side_kernel,
-        [((256, PAD), BF16), ((128, 128), F32)],
+        [((256, PAD), BF16), ((128, 128), F32), ((128, 128), F32)],
         (arrived, tree),
-        [V((PAD, PAD), BF16), V((128, PAD), BF16)],
+        [
+            V((PAD, PAD), BF16),
+            V((128, PAD), BF16),
+            V((64, PAD), F32),
+            V((256, PAD), BF16),
+            S((2,)),
+        ],
+        far=1,
+        far_outs=(0,),
     )
     (paths,) = call(
         separator_kernel,
         [((DEV * S3, 128), F32)],
         (half, pushed, square, link),
-        (),
+        [
+            V((GROUPS, LEAF, LEAF), F32),
+            V((GROUPS - 1, LEAF, LEAF), F32),
+            S((2 * GROUPS,)),
+        ],
         1,
+        far=2,
     )
     paths = exchange(paths, S3)
     (returning,) = call(
@@ -496,13 +643,13 @@
         (
             home_at,
             paths,
-            arrived,
+            leaf_rows,
+            idx,
+            gram,
             leaf_inverse,
             leaf_below,
-            leaf_rows,
             leaf_solved,
             other,
-            gram,
         ),
         [
             V((64, PATH), F32),
@@ -510,8 +657,14 @@
             V((PATH, SPAN), BF16),
             V((PAD, PAD), BF16),
             V((128, PAD), BF16),
+            V((NLEAF, LEAF, LEAF), F32),
+            V((NLEAF, LEAF, LEAF), F32),
+            V((64, SPAN), F32),
+            V((256, PAD), BF16),
+            S((2 * NLEAF + 2,)),
         ],
         1,
+        far=4,
     )
     returned = exchange(returning, S4)
     (sums,) = call(total_kernel, [((DEV * 2, 128), F32)], (returned,), micros=1)
@@ -526,8 +679,9 @@
         call(
             finish_kernel,
             [((64, 64), F32), ((64, 64), F32), ((64, ROWS), F32)],
-            (sums, solved, block_now, block_before, coupling),
-            [V((192, 2 * PAD), BF16)],
+            (sums, solved, coupling, block_now, block_before),
+            [V((192, 2 * PAD), BF16), V((64, ROWS), F32), V((64, ROWS), F32), S((2,))],
+            far=2,
         )
     )
 

time: 141 us -> 141 us (level)
  Pallas kernels: 29.6 us -> 55.6 us
  local copies, waits for them, and re-layouts: 22.7 us -> 2.36 us
  waiting for transfers between devices: 40 us -> 36.3 us
  starting transfers between devices: 27.4 us -> 25.7 us
    pallas_call x9, Pallas kernels: 29.6 us -> 55.6 us  [call(): pl.pallas_call(kernel, out_shape=[jax.ShapeDtypeStruct(shape, dtype) for...]
    unnamed x40 -> x14, local copies, waits for them, and re-layouts: 22 us -> 1.05 us
    all_to_all x4, waiting for transfers between devices: 40 us -> 36.3 us  [exchange(): lax.all_to_all(x.reshape(DEV, 1, lines * 128), AXES, split_axis=0, concat...]
    all_to_all x4, starting transfers between devices: 27.4 us -> 25.7 us  [exchange(): lax.all_to_all(x.reshape(DEV, 1, lines * 128), AXES, split_axis=0, concat...]
  transfers between devices with their start and end apart: 4 -> 4, of which waited for: 4 -> 4; matrix products, arithmetic and copies ran while one was open for 0% -> 0% of each run, Pallas kernels for 5% -> 14%
where the time goes in v3:
time: 141 us
  Pallas kernels  55.6 us (39%)
  waiting for transfers between devices  36.3 us (26%)
  starting transfers between devices  25.7 us (18%)
  blocking collectives  19.5 us (14%)
  local copies, waits for them, and re-layouts  2.36 us (2%)
    pallas_call x9, Pallas kernels, call(): pl.pallas_call(kernel, out_shape=[jax.ShapeDtypeStruct(shape, dtype) for...  55.6 us
    all_to_all x4, waiting for transfers between devices, exchange(): lax.all_to_all(x.reshape(DEV, 1, lines * 128), AXES, split_axis=0, concat...  36.3 us
    all_to_all x4, starting transfers between devices, exchange(): lax.all_to_all(x.reshape(DEV, 1, lines * 128), AXES, split_axis=0, concat...  25.7 us
    all_to_all x1, blocking collectives, exchange(): lax.all_to_all(x.reshape(DEV, 1, lines * 128), AXES, split_axis=0, concat...  19.5 us
  transfers between devices with their start and end apart: 4, of which 4 were waited for; matrix products, arithmetic and copies ran while one was open for 0% of the time, Pallas kernels for 14%

profile of v3, /device:TPU:1, one launch (start us, length us, event | category | flops | bytes accessed | tf_op | source)
XLA Modules:
  0.0 140.6 jit_solution(6189170417096013324)
XLA Ops:
  0.6 1.3 reshape.47.vt_ref
  1.9 6.4 %shard_map.112 = (f32[2304,128]{1,0:T(8,128)}, s32[1,2176]{1,0:T(1,128)}) custom-call(s32[1,2080]{1,0:T(1,128)} %reshape.47.vt_ref, f32[64,2080]{1,0:T(8,128)} %now_hbm.3, f32[64,2080]{1,0:T(8,128)} %before_hbm.3), custom_call_target="tpu_custom_call" | custom-call | flops 4000000000 | bytes 12000000 | tf_op jit(solution)/shard_map/pallas_call | solution.py:518
  8.4 11.5 %all-to-all-start = ((f32[128,1,2304]{2,1,0:T(1,128)}), f32[128,1,2304]{2,1,0:T(1,128)S(1)}, u32[]{:S(2)}, u32[]{:S(2)}) async-start(f32[128,1,2304]{2,1,0:T(1,128)} %bitcast.20), calls=%async_computation | async-start | bytes 2359296 | tf_op jit(solution)/shard_map/all_to_all | solution.py:535
  20.0 0.0 copy-start.4
  20.0 13.5 %shard_map.113 = (f32[16,256,256]{2,1,0:T(8,128)}, f32[15,256,256]{2,1,0:T(8,128)}) custom-call(f32[16,256,256]{2,1,0:T(8,128)} %inv_hbm.3, f32[15,256,256]{2,1,0:T(8,128)} %parent_hbm.1), custom_call_target="tpu_custom_call" | custom-call | flops 4000000000 | bytes 12000000 | tf_op jit(solution)/shard_map/pallas_call | solution.py:518
  33.5 6.9 %all-to-all-done = f32[128,1,2304]{2,1,0:T(1,128)S(1)} async-done(((f32[128,1,2304]{2,1,0:T(1,128)}), f32[128,1,2304]{2,1,0:T(1,128)S(1)}, u32[]{:S(2)}, u32[]{:S(2)}) %all-to-all-start) | async-done | bytes 1179680 | tf_op jit(solution)/shard_map/all_to_all | solution.py:535
  40.4 0.0 copy-start
  40.4 0.0 copy-done.4
  40.4 8.9 %shard_map.114 = (f32[1280,128]{1,0:T(8,128)}, f32[64,2048]{1,0:T(8,128)S(1)}, f32[64,2176]{1,0:T(8,128)S(1)}) custom-call(s32[1]{0:T(128)} %bitcast.home_ref, f32[2304,128]{1,0:T(8,128)S(1)} %bitcast.12, s32[8,256]{1,0:T(8,128)S(1)} %copy-done.4, f32[8,256,256]{2,1,0:T(8,128)} %inv_hbm.5, f32[8,256,256]{2,1,0:T(8,128)} %below_hbm.3, ...), custom_call_target="tpu_custom_call" | custom-call | flops 4000000000 | bytes 12000000 | tf_op jit(solution)/shard_map/pallas_call | solution.py:518
  49.3 0.0 copy-done
  49.3 4.7 %all-to-all-start.1 = ((f32[128,1,1280]{2,1,0:T(1,128)}), f32[128,1,1280]{2,1,0:T(1,128)S(1)}, u32[]{:S(2)}, u32[]{:S(2)}) async-start(f32[128,1,1280]{2,1,0:T(1,128)} %bitcast.4), calls=%async_computation.1 | async-start | bytes 1310720 | tf_op jit(solution)/shard_map/all_to_all | solution.py:535
  54.0 14.9 %all-to-all-done.1 = f32[128,1,1280]{2,1,0:T(1,128)S(1)} async-done(((f32[128,1,1280]{2,1,0:T(1,128)}), f32[128,1,1280]{2,1,0:T(1,128)S(1)}, u32[]{:S(2)}, u32[]{:S(2)}) %all-to-all-start.1) | async-done | bytes 655392 | tf_op jit(solution)/shard_map/all_to_all | solution.py:535
  69.0 7.7 %shard_map.115 = f32[640,128]{1,0:T(8,128)} custom-call(s32[1]{0:T(128)} %bitcast.1.half_ref, f32[1280,128]{1,0:T(8,128)S(1)} %bitcast.14, f32[16,256,256]{2,1,0:T(8,128)} %get-tuple-element.16.square_hbm, f32[15,256,256]{2,1,0:T(8,128)} %get-tuple-element.14.ready_hbm.link_hbm), custom_call_target="tpu_custom_call" | custom-call | flops 4000000000 | bytes 12000000 | tf_op jit(solution)/shard_map/pallas_call | solution.py:518
  76.7 4.8 %all-to-all-start.2 = ((f32[128,1,640]{2,1,0:T(1,128)}), f32[128,1,640]{2,1,0:T(1,128)S(1)}, u32[]{:S(2)}, u32[]{:S(2)}) async-start(f32[128,1,640]{2,1,0:T(1,128)} %bitcast.6), calls=%async_computation.2 | async-start | bytes 655360 | tf_op jit(solution)/shard_map/all_to_all | solution.py:535
  81.4 4.3 %shard_map.116 = (bf16[256,2176]{1,0:T(8,128)(2,1)S(1)}, f32[128,128]{1,0:T(8,128)S(1)}, f32[128,128]{1,0:T(8,128)S(1)}) custom-call(f32[2304,128]{1,0:T(8,128)} %bitcast.13, f32[64,2176]{1,0:T(8,128)S(1)} %get-tuple-element.17.tree_hbm), custom_call_target="tpu_custom_call" | custom-call | flops 4000000000 | bytes 12000000 | tf_op jit(solution)/shard_map/pallas_call | solution.py:518
  85.7 0.0 copy-start.5
  85.7 1.0 copy-done.5
  86.7 6.1 %all-to-all-done.2 = f32[128,1,640]{2,1,0:T(1,128)S(1)} async-done(((f32[128,1,640]{2,1,0:T(1,128)}), f32[128,1,640]{2,1,0:T(1,128)S(1)}, u32[]{:S(2)}, u32[]{:S(2)}) %all-to-all-start.2) | async-done | bytes 327712 | tf_op jit(solution)/shard_map/all_to_all | solution.py:535
  92.9 7.7 %shard_map.117 = f32[1280,128]{1,0:T(8,128)S(1)} custom-call(s32[1]{0:T(128)} %bitcast.home_ref, f32[640,128]{1,0:T(8,128)S(1)} %bitcast.18, s32[8,256]{1,0:T(8,128)S(1)} %copy-done.4, f32[128,128]{1,0:T(8,128)S(1)} %get-tuple-element.18.idx_ref, f32[128,128]{1,0:T(8,128)S(1)} %get-tuple-element.19.gram_ref, f32[8,256,256]{2,1,0:T(8,128)} %inv_hbm.5, ...), custom_call_target="tpu_custom_call" | custom-call | flops 4000000000 | bytes 12000000 | tf_op jit(solution)/shard_map/pallas_call | solution.py:518
  100.6 19.5 %all_to_all.25 = f32[128,1,1280]{2,1,0:T(1,128)S(1)} all-to-all(f32[128,1,1280]{2,1,0:T(1,128)S(1)} %bitcast.17), channel_id=1, replica_groups=mesh['leaf'=16,'front'=8] {'leaf','front'}, dimensions={0} | all-to-all | bytes 1310720 | tf_op jit(solution)/shard_map/all_to_all | solution.py:535
  120.1 0.7 shard_map.118
  120.8 4.8 %all-to-all-start.4 = ((f32[128,1,256]{2,1,0:T(1,128)}), f32[128,1,256]{2,1,0:T(1,128)S(1)}, u32[]{:S(2)}, u32[]{:S(2)}) async-start(f32[128,1,256]{2,1,0:T(1,128)} %bitcast.10), calls=%async_computation.4 | async-start | bytes 262144 | tf_op jit(solution)/shard_map/all_to_all | solution.py:535
  125.6 0.0 copy-done.6
  125.6 0.0 copy-start.1
  125.6 0.0 copy-start.2
  125.6 0.0 copy-start.3
  125.6 1.7 %shard_map.119.solved_ref = f32[64,2080]{1,0:T(8,128)S(1)} custom-call(s32[1,2176]{1,0:T(1,128)S(1)} %copy-done.6, f32[1280,128]{1,0:T(8,128)S(1)} %bitcast.16), custom_call_target="tpu_custom_call" | custom-call | flops 4000000000 | bytes 12000000 | tf_op jit(solution)/shard_map/pallas_call | solution.py:518
  127.3 8.4 %all-to-all-done.4 = f32[128,1,256]{2,1,0:T(1,128)S(1)} async-done(((f32[128,1,256]{2,1,0:T(1,128)}), f32[128,1,256]{2,1,0:T(1,128)S(1)}, u32[]{:S(2)}, u32[]{:S(2)}) %all-to-all-start.4) | async-done | bytes 131104 | tf_op jit(solution)/shard_map/all_to_all | solution.py:535
  135.6 0.0 copy-done.1
  135.7 0.0 copy-done.2
  135.7 0.0 copy-done.3
  135.7 4.7 %shard_map.120 = (f32[64,64]{1,0:T(8,128)}, f32[64,64]{1,0:T(8,128)}, f32[64,2080]{1,0:T(8,128)}) custom-call(f32[256,128]{1,0:T(8,128)S(1)} %bitcast.19, f32[64,2080]{1,0:T(8,128)S(1)} %shard_map.119.solved_ref, f32[64,64]{1,0:T(8,128)S(1)} %copy-done.3, f32[64,2080]{1,0:T(8,128)S(1)} %copy-done.1, f32[64,2080]{1,0:T(8,128)S(1)} %copy-done.2), custom_call_target="tpu_custom_call" | custom-call | flops 4000000000 | bytes 12000000 | tf_op jit(solution)/shard_map/pallas_call | solution.py:518
  (1 shorter events, 0.0 us)
Async XLA Ops:
  8.4 32.0 %all-to-all-start = ((f32[128,1,2304]{2,1,0:T(1,128)}), f32[128,1,2304]{2,1,0:T(1,128)S(1)}, u32[]{:S(2)}, u32[]{:S(2)}) async-start(f32[128,1,2304]{2,1,0:T(1,128)} %bitcast.20), calls=%async_computation | async-start | bytes 2359296 | tf_op jit(solution)/shard_map/all_to_all | solution.py:535
  20.0 20.4 %copy-start.4 = (s32[8,256]{1,0:T(8,128)S(1)}, s32[8,256]{1,0:T(8,128)}, u32[]{:S(2)}) copy-start(s32[8,256]{1,0:T(8,128)} %rows_ref.3) | copy-start | bytes 24580
  40.4 8.9 %copy-start = (f32[128,1,2304]{2,1,0:T(1,128)}, f32[128,1,2304]{2,1,0:T(1,128)S(1)}, u32[]{:S(2)}) copy-start(f32[128,1,2304]{2,1,0:T(1,128)S(1)} %all-to-all-done) | copy-start | bytes 3538948
  49.3 19.6 %all-to-all-start.1 = ((f32[128,1,1280]{2,1,0:T(1,128)}), f32[128,1,1280]{2,1,0:T(1,128)S(1)}, u32[]{:S(2)}, u32[]{:S(2)}) async-start(f32[128,1,1280]{2,1,0:T(1,128)} %bitcast.4), calls=%async_computation.1 | async-start | bytes 1310720 | tf_op jit(solution)/shard_map/all_to_all | solution.py:535
  76.7 16.2 %all-to-all-start.2 = ((f32[128,1,640]{2,1,0:T(1,128)}), f32[128,1,640]{2,1,0:T(1,128)S(1)}, u32[]{:S(2)}, u32[]{:S(2)}) async-start(f32[128,1,640]{2,1,0:T(1,128)} %bitcast.6), calls=%async_computation.2 | async-start | bytes 655360 | tf_op jit(solution)/shard_map/all_to_all | solution.py:535
  85.7 1.0 copy-start.5
  120.1 5.5 %copy-start.6 = (s32[1,2176]{1,0:T(1,128)S(1)}, s32[1,2176]{1,0:T(1,128)}, u32[]{:S(2)}) copy-start(s32[1,2176]{1,0:T(1,128)} %get-tuple-element.22.key_ref) | copy-start | bytes 26116
  120.8 14.9 %all-to-all-start.4 = ((f32[128,1,256]{2,1,0:T(1,128)}), f32[128,1,256]{2,1,0:T(1,128)S(1)}, u32[]{:S(2)}, u32[]{:S(2)}) async-start(f32[128,1,256]{2,1,0:T(1,128)} %bitcast.10), calls=%async_computation.4 | async-start | bytes 262144 | tf_op jit(solution)/shard_map/all_to_all | solution.py:535
  125.6 10.1 %copy-start.1 = (f32[64,2080]{1,0:T(8,128)S(1)}, f32[64,2080]{1,0:T(8,128)}, u32[]{:S(2)}) copy-start(f32[64,2080]{1,0:T(8,128)} %now_hbm.3) | copy-start | bytes 1597444
  125.6 10.1 %copy-start.2 = (f32[64,2080]{1,0:T(8,128)S(1)}, f32[64,2080]{1,0:T(8,128)}, u32[]{:S(2)}) copy-start(f32[64,2080]{1,0:T(8,128)} %before_hbm.3) | copy-start | bytes 1597444
  125.6 10.1 %copy-start.3 = (f32[64,64]{1,0:T(8,128)S(1)}, f32[64,64]{1,0:T(8,128)}, u32[]{:S(2)}) copy-start(f32[64,64]{1,0:T(8,128)} %coupling_ref.1) | copy-start | bytes 49156

commit v4 on v3

--- a/solution.py
+++ b/solution.py
@@ -113,7 +113,7 @@
 ):
     loads = [fetch(now_hbm, now, sems.at[0]), fetch(before_hbm, before, sems.at[1])]
     dest[...] = jnp.full((8, PAD), -1, jnp.int32)
-    dest[0:1, 0:ROWS] = vt_ref[...]
+    dest[0:1, 0:ROWS] = vt_ref[...].reshape(1, ROWS)
     target = dest[0:1, :]
     bucket = ((target.astype(F32) + 0.5) * (1.0 / ROWS)).astype(jnp.int32)
     bucket = jnp.where(target < 0, -1, bucket)
@@ -133,9 +133,6 @@
         carry = carry + counts[:, 128:256]
     rank = jnp.concatenate(ranks, axis=1).astype(jnp.int32)
     key = jnp.where(target < 0, -1, rank * DEV + bucket)
-    key_ref[...] = key
-    for k in range(CAP):
-        mark[k * DEV : (k + 1) * DEV, :] = mark_row(key, DEV, k * DEV)
     for load in loads:
         load.wait()
     value[:, SPAN:PAD] = jnp.zeros((4 * VEC, PAD - SPAN), BF16)
@@ -145,6 +142,9 @@
     value[64:128, 0:ROWS] = bef_hi
     value[128:192, 0:ROWS] = now_lo
     value[192:256, 0:ROWS] = bef_lo
+    key_ref[...] = key
+    for k in range(CAP):
+        mark[k * DEV : (k + 1) * DEV, :] = mark_row(key, DEV, k * DEV)
     block = nt(mark[...], value[...])
     block = block[:, 0:128] + block[:, 128:256]
     for k in range(CAP):
@@ -200,14 +200,14 @@
     tree_ref[...] = folded(nn(value[...], mark[...]))
     stores = [fetch(tree_ref, tree_hbm, sems.at[2 * NLEAF])]
     rows = rows_ref[...].astype(F32).T.astype(jnp.int32)
+    for load in inv_loads + below_loads:
+        load.wait()
     for q in range(NLEAF):
         cols = slice(q * LEAF, (q + 1) * LEAF)
-        inv_loads[q].wait()
         hi, lo = split(inv_ref[q])
         source = stacked(tree_ref[:, cols])
         solved = folded(nt(source, hi) + nt(source, lo))
         solved_ref[:, cols] = solved
-        below_loads[q].wait()
         hi, lo = split(below_ref[q])
         solved = stacked(solved)
         update[:, cols] = stacked(folded(nt(solved, hi) + nt(solved, lo)))
@@ -261,17 +261,22 @@
             parent_loads.append(
                 fetch(parent_hbm.at[at], parent_ref.at[at], sems.at[GROUPS + at])
             )
-    for s in range(GROUPS):
-        inv_loads[s].wait()
-        hi, lo = split(inv_ref[s])
-        square_ref[s] = tn(hi, hi) + (tn(hi, lo) + tn(lo, hi))
-        stores.append(fetch(square_ref.at[s], square_hbm.at[s], sems.at[2 * GROUPS + s]))
-        if s > 0:
-            at = s - 1
-            parent_loads[at].wait()
-            up, down = split(parent_ref[at])
-            link_ref[at] = nn(up, hi) + (nn(up, lo) + nn(down, hi))
-            stores.append(fetch(link_ref.at[at], link_hbm.at[at], sems.at[3 * GROUPS + at]))
+    for first in (0, GROUPS // 2):
+        for s in range(first, first + GROUPS // 2):
+            inv_loads[s].wait()
+            if s > 0:
+                parent_loads[s - 1].wait()
+        for s in range(first, first + GROUPS // 2):
+            hi, lo = split(inv_ref[s])
+            square_ref[s] = tn(hi, hi) + (tn(hi, lo) + tn(lo, hi))
+            if s > 0:
+                up, down = split(parent_ref[s - 1])
+                link_ref[s - 1] = nn(up, hi) + (nn(up, lo) + nn(down, hi))
+        for s in range(first, first + GROUPS // 2):
+            stores.append(fetch(square_ref.at[s], square_hbm.at[s], sems.at[2 * GROUPS + s]))
+            if s > 0:
+                at = s - 1
+                stores.append(fetch(link_ref.at[at], link_hbm.at[at], sems.at[3 * GROUPS + at]))
     for store in stores:
         store.wait()
 
@@ -326,13 +331,19 @@
     for height in range(2, LEVELS + 1):
         count = max(GROUPS >> height, 1)
         first = count if height < LEVELS else 0
+        if height == 2:
+            for at in range(7, 15):
+                loads[at].wait()
+        if height == 3:
+            for at in range(7):
+                loads[at].wait()
         for s in range(first, first + count):
             for c in (1,) if s == 0 else (2 * s, 2 * s + 1):
-                loads[c - 1].wait()
                 source[s] = source[s] - apply(link_ref[c - 1], source[c], eye)
+    for load in square_loads:
+        load.wait()
     back = {}
     for s in range(GROUPS):
-        square_loads[s].wait()
         back[s] = apply_t(square_ref[s], source[s], eye)
         if s > 0:
             back[s] = back[s] - apply_t(link_ref[s - 1], back[s // 2], eye)
@@ -387,6 +398,8 @@
             known[:, j * 128 : (j + 1) * 128] = chunk
             parts[:, j * 128 : (j + 1) * 128] = stacked(chunk)
     picked = folded(nn(parts[...], moved[...]))
+    for load in loads + below_loads + inv_loads:
+        load.wait()
     start = home_ref[0]
     tile = pl.multiple_of((start // 128) * 128, 128)
     home = pltpu.roll(known[:, pl.ds(tile, 128)], (128 - start % 128) % 128, 1)
@@ -394,16 +407,11 @@
     result[:, SPAN:PAD] = stacked(home)
     for q in range(NLEAF):
         cols = slice(q * LEAF, (q + 1) * LEAF)
-        if q == 0:
-            loads[0].wait()
-        below_loads[q].wait()
         hi, lo = split(below_ref[q])
         rows = stacked(picked[:, cols])
         source = stacked(solved_ref[:, cols] - folded(nn(rows, hi) + nn(rows, lo)))
-        inv_loads[q].wait()
         hi, lo = split(inv_ref[q])
         result[:, cols] = stacked(folded(nn(source, hi) + nn(source, lo)))
-    loads[1].wait()
     cross = folded(nt(result[...], other_ref[...]))
     cross = cross[:, 0:128] + cross[:, 128:256]
     square = both(folded(nt(result[...], result[...])))
@@ -561,7 +569,7 @@
     packed, key = call(
         pack_kernel,
         [((DEV * S1, 128), F32), ((1, PAD), jnp.int32)],
-        (vertex_to_tree.reshape(1, ROWS), block_now, block_before),
+        (vertex_to_tree, block_now, block_before),
         [
             V((8, PAD), jnp.int32),
             V((DEV, PAD), BF16),

time: 141 us -> 134 us (0.950)
  Pallas kernels: 55.6 us -> 45.1 us
  waiting for transfers between devices: 36.3 us -> 41.5 us
    pallas_call x9, Pallas kernels: 55.6 us -> 45.1 us  [call(): pl.pallas_call(kernel, out_shape=[jax.ShapeDtypeStruct(shape, dtype) for...]
    all_to_all x4, waiting for transfers between devices: 36.3 us -> 41.5 us  [exchange(): lax.all_to_all(x.reshape(DEV, 1, lines * 128), AXES, split_axis=0, concat...]
  transfers between devices with their start and end apart: 4 -> 4, of which waited for: 4 -> 4; matrix products, arithmetic and copies ran while one was open for 0% -> 0% of each run, Pallas kernels for 14% -> 11%
where the time goes in v4:
time: 134 us
  Pallas kernels  45.1 us (34%)
  waiting for transfers between devices  41.5 us (31%)
  starting transfers between devices  25.7 us (19%)
  blocking collectives  19.5 us (15%)
    pallas_call x9, Pallas kernels, call(): pl.pallas_call(kernel, out_shape=[jax.ShapeDtypeStruct(shape, dtype) for...  45.1 us
    all_to_all x4, waiting for transfers between devices, exchange(): lax.all_to_all(x.reshape(DEV, 1, lines * 128), AXES, split_axis=0, concat...  41.5 us
    all_to_all x4, starting transfers between devices, exchange(): lax.all_to_all(x.reshape(DEV, 1, lines * 128), AXES, split_axis=0, concat...  25.7 us
    all_to_all x1, blocking collectives, exchange(): lax.all_to_all(x.reshape(DEV, 1, lines * 128), AXES, split_axis=0, concat...  19.5 us
  transfers between devices with their start and end apart: 4, of which 4 were waited for; matrix products, arithmetic and copies ran while one was open for 0% of the time, Pallas kernels for 11%

profile of v4, /device:TPU:1, one launch (start us, length us, event | category | flops | bytes accessed | tf_op | source)
XLA Modules:
  0.0 133.9 jit_solution(5397187051810297926)
XLA Ops:
  0.6 6.1 %shard_map.112 = (f32[2304,128]{1,0:T(8,128)}, s32[1,2176]{1,0:T(1,128)}) custom-call(s32[2080]{0:T(1024)} %vt_ref.1, f32[64,2080]{1,0:T(8,128)} %now_hbm.3, f32[64,2080]{1,0:T(8,128)} %before_hbm.3), custom_call_target="tpu_custom_call" | custom-call | flops 4000000000 | bytes 12000000 | tf_op jit(solution)/shard_map/pallas_call | solution.py:526
  6.7 11.5 %all-to-all-start = ((f32[128,1,2304]{2,1,0:T(1,128)}), f32[128,1,2304]{2,1,0:T(1,128)S(1)}, u32[]{:S(2)}, u32[]{:S(2)}) async-start(f32[128,1,2304]{2,1,0:T(1,128)} %bitcast.20), calls=%async_computation | async-start | bytes 2359296 | tf_op jit(solution)/shard_map/all_to_all | solution.py:543
  18.3 0.0 copy-start.4
  18.3 8.2 %shard_map.113 = (f32[16,256,256]{2,1,0:T(8,128)}, f32[15,256,256]{2,1,0:T(8,128)}) custom-call(f32[16,256,256]{2,1,0:T(8,128)} %inv_hbm.3, f32[15,256,256]{2,1,0:T(8,128)} %parent_hbm.1), custom_call_target="tpu_custom_call" | custom-call | flops 4000000000 | bytes 12000000 | tf_op jit(solution)/shard_map/pallas_call | solution.py:526
  26.5 12.2 %all-to-all-done = f32[128,1,2304]{2,1,0:T(1,128)S(1)} async-done(((f32[128,1,2304]{2,1,0:T(1,128)}), f32[128,1,2304]{2,1,0:T(1,128)S(1)}, u32[]{:S(2)}, u32[]{:S(2)}) %all-to-all-start) | async-done | bytes 1179680 | tf_op jit(solution)/shard_map/all_to_all | solution.py:543
  38.7 0.0 copy-start
  38.7 0.0 copy-done.4
  38.7 6.5 %shard_map.114 = (f32[1280,128]{1,0:T(8,128)}, f32[64,2048]{1,0:T(8,128)S(1)}, f32[64,2176]{1,0:T(8,128)S(1)}) custom-call(s32[1]{0:T(128)} %bitcast.home_ref, f32[2304,128]{1,0:T(8,128)S(1)} %bitcast.12, s32[8,256]{1,0:T(8,128)S(1)} %copy-done.4, f32[8,256,256]{2,1,0:T(8,128)} %inv_hbm.5, f32[8,256,256]{2,1,0:T(8,128)} %below_hbm.3, ...), custom_call_target="tpu_custom_call" | custom-call | flops 4000000000 | bytes 12000000 | tf_op jit(solution)/shard_map/pallas_call | solution.py:526
  45.3 0.0 copy-done
  45.3 4.7 %all-to-all-start.1 = ((f32[128,1,1280]{2,1,0:T(1,128)}), f32[128,1,1280]{2,1,0:T(1,128)S(1)}, u32[]{:S(2)}, u32[]{:S(2)}) async-start(f32[128,1,1280]{2,1,0:T(1,128)} %bitcast.4), calls=%async_computation.1 | async-start | bytes 1310720 | tf_op jit(solution)/shard_map/all_to_all | solution.py:543
  50.0 15.0 %all-to-all-done.1 = f32[128,1,1280]{2,1,0:T(1,128)S(1)} async-done(((f32[128,1,1280]{2,1,0:T(1,128)}), f32[128,1,1280]{2,1,0:T(1,128)S(1)}, u32[]{:S(2)}, u32[]{:S(2)}) %all-to-all-start.1) | async-done | bytes 655392 | tf_op jit(solution)/shard_map/all_to_all | solution.py:543
  64.9 6.2 %shard_map.115 = f32[640,128]{1,0:T(8,128)} custom-call(s32[1]{0:T(128)} %bitcast.1.half_ref, f32[1280,128]{1,0:T(8,128)S(1)} %bitcast.14, f32[16,256,256]{2,1,0:T(8,128)} %get-tuple-element.16.square_hbm, f32[15,256,256]{2,1,0:T(8,128)} %get-tuple-element.14.ready_hbm.link_hbm), custom_call_target="tpu_custom_call" | custom-call | flops 4000000000 | bytes 12000000 | tf_op jit(solution)/shard_map/pallas_call | solution.py:526
  71.1 4.8 %all-to-all-start.2 = ((f32[128,1,640]{2,1,0:T(1,128)}), f32[128,1,640]{2,1,0:T(1,128)S(1)}, u32[]{:S(2)}, u32[]{:S(2)}) async-start(f32[128,1,640]{2,1,0:T(1,128)} %bitcast.6), calls=%async_computation.2 | async-start | bytes 655360 | tf_op jit(solution)/shard_map/all_to_all | solution.py:543
  75.9 4.3 %shard_map.116 = (bf16[256,2176]{1,0:T(8,128)(2,1)S(1)}, f32[128,128]{1,0:T(8,128)S(1)}, f32[128,128]{1,0:T(8,128)S(1)}) custom-call(f32[2304,128]{1,0:T(8,128)} %bitcast.13, f32[64,2176]{1,0:T(8,128)S(1)} %get-tuple-element.17.tree_hbm), custom_call_target="tpu_custom_call" | custom-call | flops 4000000000 | bytes 12000000 | tf_op jit(solution)/shard_map/pallas_call | solution.py:526
  80.2 0.0 copy-start.5
  80.2 1.0 copy-done.5
  81.2 6.1 %all-to-all-done.2 = f32[128,1,640]{2,1,0:T(1,128)S(1)} async-done(((f32[128,1,640]{2,1,0:T(1,128)}), f32[128,1,640]{2,1,0:T(1,128)S(1)}, u32[]{:S(2)}, u32[]{:S(2)}) %all-to-all-start.2) | async-done | bytes 327712 | tf_op jit(solution)/shard_map/all_to_all | solution.py:543
  87.3 6.7 %shard_map.117 = f32[1280,128]{1,0:T(8,128)S(1)} custom-call(s32[1]{0:T(128)} %bitcast.home_ref, f32[640,128]{1,0:T(8,128)S(1)} %bitcast.18, s32[8,256]{1,0:T(8,128)S(1)} %copy-done.4, f32[128,128]{1,0:T(8,128)S(1)} %get-tuple-element.18.idx_ref, f32[128,128]{1,0:T(8,128)S(1)} %get-tuple-element.19.gram_ref, f32[8,256,256]{2,1,0:T(8,128)} %inv_hbm.5, ...), custom_call_target="tpu_custom_call" | custom-call | flops 4000000000 | bytes 12000000 | tf_op jit(solution)/shard_map/pallas_call | solution.py:526
  94.1 19.5 %all_to_all.25 = f32[128,1,1280]{2,1,0:T(1,128)S(1)} all-to-all(f32[128,1,1280]{2,1,0:T(1,128)S(1)} %bitcast.17), channel_id=1, replica_groups=mesh['leaf'=16,'front'=8] {'leaf','front'}, dimensions={0} | all-to-all | bytes 1310720 | tf_op jit(solution)/shard_map/all_to_all | solution.py:543
  113.6 0.0 copy-start.6
  113.6 0.7 shard_map.118
  114.2 4.8 %all-to-all-start.4 = ((f32[128,1,256]{2,1,0:T(1,128)}), f32[128,1,256]{2,1,0:T(1,128)S(1)}, u32[]{:S(2)}, u32[]{:S(2)}) async-start(f32[128,1,256]{2,1,0:T(1,128)} %bitcast.10), calls=%async_computation.4 | async-start | bytes 262144 | tf_op jit(solution)/shard_map/all_to_all | solution.py:543
  119.0 0.0 copy-done.6
  119.0 0.0 copy-start.1
  119.0 0.0 copy-start.2
  119.0 0.0 copy-start.3
  119.1 1.7 %shard_map.119.solved_ref = f32[64,2080]{1,0:T(8,128)S(1)} custom-call(s32[1,2176]{1,0:T(1,128)S(1)} %copy-done.6, f32[1280,128]{1,0:T(8,128)S(1)} %bitcast.16), custom_call_target="tpu_custom_call" | custom-call | flops 4000000000 | bytes 12000000 | tf_op jit(solution)/shard_map/pallas_call | solution.py:526
  120.7 8.2 %all-to-all-done.4 = f32[128,1,256]{2,1,0:T(1,128)S(1)} async-done(((f32[128,1,256]{2,1,0:T(1,128)}), f32[128,1,256]{2,1,0:T(1,128)S(1)}, u32[]{:S(2)}, u32[]{:S(2)}) %all-to-all-start.4) | async-done | bytes 131104 | tf_op jit(solution)/shard_map/all_to_all | solution.py:543
  129.0 0.0 copy-done.1
  129.0 0.0 copy-done.2
  129.0 0.0 copy-done.3
  129.0 4.7 %shard_map.120 = (f32[64,64]{1,0:T(8,128)}, f32[64,64]{1,0:T(8,128)}, f32[64,2080]{1,0:T(8,128)}) custom-call(f32[256,128]{1,0:T(8,128)S(1)} %bitcast.19, f32[64,2080]{1,0:T(8,128)S(1)} %shard_map.119.solved_ref, f32[64,64]{1,0:T(8,128)S(1)} %copy-done.3, f32[64,2080]{1,0:T(8,128)S(1)} %copy-done.1, f32[64,2080]{1,0:T(8,128)S(1)} %copy-done.2), custom_call_target="tpu_custom_call" | custom-call | flops 4000000000 | bytes 12000000 | tf_op jit(solution)/shard_map/pallas_call | solution.py:526
Async XLA Ops:
  6.7 32.0 %all-to-all-start = ((f32[128,1,2304]{2,1,0:T(1,128)}), f32[128,1,2304]{2,1,0:T(1,128)S(1)}, u32[]{:S(2)}, u32[]{:S(2)}) async-start(f32[128,1,2304]{2,1,0:T(1,128)} %bitcast.20), calls=%async_computation | async-start | bytes 2359296 | tf_op jit(solution)/shard_map/all_to_all | solution.py:543
  18.3 20.4 %copy-start.4 = (s32[8,256]{1,0:T(8,128)S(1)}, s32[8,256]{1,0:T(8,128)}, u32[]{:S(2)}) copy-start(s32[8,256]{1,0:T(8,128)} %rows_ref.3) | copy-start | bytes 24580
  38.7 6.6 %copy-start = (f32[128,1,2304]{2,1,0:T(1,128)}, f32[128,1,2304]{2,1,0:T(1,128)S(1)}, u32[]{:S(2)}) copy-start(f32[128,1,2304]{2,1,0:T(1,128)S(1)} %all-to-all-done) | copy-start | bytes 3538948
  45.3 19.7 %all-to-all-start.1 = ((f32[128,1,1280]{2,1,0:T(1,128)}), f32[128,1,1280]{2,1,0:T(1,128)S(1)}, u32[]{:S(2)}, u32[]{:S(2)}) async-start(f32[128,1,1280]{2,1,0:T(1,128)} %bitcast.4), calls=%async_computation.1 | async-start | bytes 1310720 | tf_op jit(solution)/shard_map/all_to_all | solution.py:543
  71.1 16.2 %all-to-all-start.2 = ((f32[128,1,640]{2,1,0:T(1,128)}), f32[128,1,640]{2,1,0:T(1,128)S(1)}, u32[]{:S(2)}, u32[]{:S(2)}) async-start(f32[128,1,640]{2,1,0:T(1,128)} %bitcast.6), calls=%async_computation.2 | async-start | bytes 655360 | tf_op jit(solution)/shard_map/all_to_all | solution.py:543
  80.2 1.0 copy-start.5
  113.6 5.5 %copy-start.6 = (s32[1,2176]{1,0:T(1,128)S(1)}, s32[1,2176]{1,0:T(1,128)}, u32[]{:S(2)}) copy-start(s32[1,2176]{1,0:T(1,128)} %get-tuple-element.22.key_ref) | copy-start | bytes 26116
  114.2 14.7 %all-to-all-start.4 = ((f32[128,1,256]{2,1,0:T(1,128)}), f32[128,1,256]{2,1,0:T(1,128)S(1)}, u32[]{:S(2)}, u32[]{:S(2)}) async-start(f32[128,1,256]{2,1,0:T(1,128)} %bitcast.10), calls=%async_computation.4 | async-start | bytes 262144 | tf_op jit(solution)/shard_map/all_to_all | solution.py:543
  119.0 9.9 %copy-start.1 = (f32[64,2080]{1,0:T(8,128)S(1)}, f32[64,2080]{1,0:T(8,128)}, u32[]{:S(2)}) copy-start(f32[64,2080]{1,0:T(8,128)} %now_hbm.3) | copy-start | bytes 1597444
  119.0 9.9 %copy-start.2 = (f32[64,2080]{1,0:T(8,128)S(1)}, f32[64,2080]{1,0:T(8,128)}, u32[]{:S(2)}) copy-start(f32[64,2080]{1,0:T(8,128)} %before_hbm.3) | copy-start | bytes 1597444
  119.0 9.9 %copy-start.3 = (f32[64,64]{1,0:T(8,128)S(1)}, f32[64,64]{1,0:T(8,128)}, u32[]{:S(2)}) copy-start(f32[64,64]{1,0:T(8,128)} %coupling_ref.1) | copy-start | bytes 49156

commit v5 on v4

--- a/solution.py
+++ b/solution.py
@@ -3,12 +3,15 @@
 from jax import lax
 from jax.experimental import pallas as pl
 from jax.experimental.pallas import tpu as pltpu
+from jax.sharding import Mesh
 from jax.sharding import PartitionSpec as P
 
 F32 = jnp.float32
 BF16 = jnp.bfloat16
 HIGHEST = lax.Precision.HIGHEST
-AXES = ("leaf", "front")
+AXES = ("half", "group", "front")
+NEAR = ("group", "front")
+HALF = 64
 DEV = 128
 CAP = 17
 ROWS = 2080
@@ -24,7 +27,7 @@
 PATH = 1280
 S1 = 18
 S2 = 10
-S3 = 5
+S3 = 10
 S4 = 10
 MIB = 1024 * 1024
 
@@ -200,6 +203,8 @@
     tree_ref[...] = folded(nn(value[...], mark[...]))
     stores = [fetch(tree_ref, tree_hbm, sems.at[2 * NLEAF])]
     rows = rows_ref[...].astype(F32).T.astype(jnp.int32)
+    for q in range(NLEAF):
+        moved[q * LEAF : (q + 1) * LEAF, :] = mark_column(rows[:, q : q + 1], PATH)
     for load in inv_loads + below_loads:
         load.wait()
     for q in range(NLEAF):
@@ -211,14 +216,13 @@
         hi, lo = split(below_ref[q])
         solved = stacked(solved)
         update[:, cols] = stacked(folded(nt(solved, hi) + nt(solved, lo)))
-        moved[cols, :] = mark_column(rows[:, q : q + 1], PATH)
     stores.append(fetch(solved_ref, solved_hbm, sems.at[2 * NLEAF + 1]))
     pushed = folded(nn(update[...], moved[...]))
     start = home_ref[0]
     own = pltpu.roll(tree_ref[:, SPAN:PAD], start % 128, 1)
     for j in range(S2):
         chunk = jnp.where(start // 128 == j, own, 0.0) - pushed[:, j * 128 : (j + 1) * 128]
-        out_ref[pl.ds(j, DEV, stride=S2), :] = jnp.concatenate([chunk, chunk], axis=0)
+        out_ref[pl.ds(j, HALF, stride=S2), :] = chunk
     for store in stores:
         store.wait()
 
@@ -302,62 +306,90 @@
     return jnp.sum(matrix * to_column(row, eye), axis=0, keepdims=True)
 
 
-def separator_kernel(
-    half_ref, recv_ref, square_hbm, link_hbm, out_ref, square_ref, link_ref, sems
-):
-    loads = {}
-    for at in range(GROUPS - 2, -1, -1):
-        loads[at] = fetch(link_hbm.at[at], link_ref.at[at], sems.at[at])
-    square_loads = [
-        fetch(square_hbm.at[s], square_ref.at[s], sems.at[GROUPS + s]) for s in range(GROUPS)
+def local_links(half):
+    return [7 + 4 * half + c for c in range(4)] + [3 + 2 * half + c for c in range(2)] + [1 + half]
+
+
+def up_kernel(half_ref, recv_ref, link_hbm, ready_hbm, top_ref, source_ref, link_ref, sems):
+    half = half_ref[0]
+    loads = [
+        fetch(link_hbm.at[at], link_ref.at[i], sems.at[i])
+        for i, at in enumerate(local_links(half))
     ]
     eye = iota((128, 128), 0) == iota((128, 128), 1)
-    source = {}
+    sums = []
     for height in range(1, LEVELS + 1):
-        count = max(GROUPS >> height, 1)
-        first = count if height < LEVELS else 0
-        span = DEV // count
-        left = recv_ref[pl.ds(2 * height - 2, DEV, stride=S2), :]
-        right = recv_ref[pl.ds(2 * height - 1, DEV, stride=S2), :]
+        count = max(8 >> height, 1)
+        span = HALF // count
+        left = recv_ref[pl.ds(2 * height - 2, HALF, stride=S2), :]
+        right = recv_ref[pl.ds(2 * height - 1, HALF, stride=S2), :]
         for c in range(count):
             at = slice(c * span, (c + 1) * span)
-            source[first + c] = jnp.concatenate(
-                [
-                    jnp.sum(left[at], axis=0, keepdims=True),
-                    jnp.sum(right[at], axis=0, keepdims=True),
-                ],
-                axis=1,
-            )
-    for height in range(2, LEVELS + 1):
-        count = max(GROUPS >> height, 1)
-        first = count if height < LEVELS else 0
-        if height == 2:
-            for at in range(7, 15):
-                loads[at].wait()
-        if height == 3:
-            for at in range(7):
-                loads[at].wait()
-        for s in range(first, first + count):
-            for c in (1,) if s == 0 else (2 * s, 2 * s + 1):
-                source[s] = source[s] - apply(link_ref[c - 1], source[c], eye)
-    for load in square_loads:
+            ends = [jnp.sum(part[at], axis=0, keepdims=True) for part in (left, right)]
+            sums.append(jnp.concatenate(ends, axis=1))
+    for load in loads:
         load.wait()
-    back = {}
-    for s in range(GROUPS):
-        back[s] = apply_t(square_ref[s], source[s], eye)
-        if s > 0:
-            back[s] = back[s] - apply_t(link_ref[s - 1], back[s // 2], eye)
-    upper = half_ref[0] == 1
-    for jj in range(S3):
+    for i in range(7):
+        to = 4 + i // 2 if i < 4 else (6 if i < 6 else 7)
+        sums[to] = sums[to] - apply(link_ref[i], sums[i], eye)
+    top_ref[...] = jnp.concatenate(sums[7:9] + [jnp.zeros((6, LEAF), F32)], axis=0)
+    source_ref[...] = jnp.concatenate(sums[0:7] + [jnp.zeros((1, LEAF), F32)], axis=0)
+
+
+def square_kernel(half_ref, source_ref, square_hbm, out_ref, square_ref, sems):
+    half = half_ref[0]
+    loads = [
+        fetch(square_hbm.at[at + 1], square_ref.at[i], sems.at[i])
+        for i, at in enumerate(local_links(half))
+    ]
+    eye = iota((128, 128), 0) == iota((128, 128), 1)
+    for load in loads:
+        load.wait()
+    lines = [apply_t(square_ref[i], source_ref[i : i + 1, :], eye) for i in range(7)]
+    out_ref[...] = jnp.concatenate(lines + [jnp.zeros((1, LEAF), F32)], axis=0)
+
+
+def down_kernel(
+    half_ref,
+    top_ref,
+    other_ref,
+    line_ref,
+    square_hbm,
+    link_hbm,
+    out_ref,
+    square_ref,
+    link_ref,
+    sems,
+):
+    half = half_ref[0]
+    first = [
+        fetch(link_hbm.at[0], link_ref.at[7], sems.at[7]),
+        fetch(square_hbm.at[0], square_ref.at[0], sems.at[8]),
+        fetch(square_hbm.at[1], square_ref.at[1], sems.at[9]),
+    ]
+    links = local_links(half)
+    loads = [fetch(link_hbm.at[links[i]], link_ref.at[i], sems.at[i]) for i in range(6, -1, -1)]
+    eye = iota((128, 128), 0) == iota((128, 128), 1)
+    total = top_ref[...] + other_ref[...]
+    below = total[0:1]
+    for load in first:
+        load.wait()
+    root = total[1:2] - apply(link_ref[7], below, eye)
+    root = apply_t(square_ref[0], root, eye)
+    below = apply_t(square_ref[1], below, eye) - apply_t(link_ref[7], root, eye)
+    for load in loads:
+        load.wait()
+    line = line_ref[...]
+    third = line[6:7] - apply_t(link_ref[6], below, eye)
+    second = [line[4 + c : 5 + c] - apply_t(link_ref[4 + c], third, eye) for c in range(2)]
+    lowest = [line[c : c + 1] - apply_t(link_ref[c], second[c // 2], eye) for c in range(4)]
+    for j in range(S3):
         lines = []
-        for g in range(GROUPS):
-            ends = []
-            for j in (jj, S3 + jj):
-                s = (GROUPS + g) >> (j // 2 + 1)
-                ends.append(back[s][:, (j % 2) * 128 : (j % 2) * 128 + 128])
-            line = jnp.where(upper, ends[1], ends[0])
-            lines.append(jnp.broadcast_to(line, (FRONT, 128)))
-        out_ref[pl.ds(jj, DEV, stride=S3), :] = jnp.concatenate(lines, axis=0)
+        for g in range(8):
+            value = (lowest[g // 2], second[g // 4], third, below, root)[j // 2]
+            value = value[:, (j % 2) * 128 : (j % 2) * 128 + 128]
+            lines.append(jnp.broadcast_to(value, (FRONT, 128)))
+        out_ref[pl.ds(j, HALF, stride=S3), :] = jnp.concatenate(lines, axis=0)
 
 
 def backward_kernel(
@@ -391,13 +423,14 @@
     loads.append(fetch(other_hbm, other_ref, sems.at[2 * NLEAF + 1]))
     for q in range(NLEAF):
         moved[:, q * LEAF : (q + 1) * LEAF] = mark_row(rows_ref[q : q + 1, :], PATH, 0)
-    for h in range(2):
-        for jj in range(S3):
-            j = h * S3 + jj
-            chunk = recv_ref[pl.ds(h * 64 * S3 + jj, 64, stride=S3), :]
-            known[:, j * 128 : (j + 1) * 128] = chunk
-            parts[:, j * 128 : (j + 1) * 128] = stacked(chunk)
+    for j in range(S3):
+        chunk = recv_ref[pl.ds(j, HALF, stride=S3), :]
+        known[:, j * 128 : (j + 1) * 128] = chunk
+        parts[:, j * 128 : (j + 1) * 128] = stacked(chunk)
     picked = folded(nn(parts[...], moved[...]))
+    slots = idx_ref[...].astype(jnp.int32)
+    for k in range(CAP):
+        mark[:, k * DEV : (k + 1) * DEV] = mark_row(slots[k : k + 1, :], PAD, 0)
     for load in loads + below_loads + inv_loads:
         load.wait()
     start = home_ref[0]
@@ -415,9 +448,6 @@
     cross = folded(nt(result[...], other_ref[...]))
     cross = cross[:, 0:128] + cross[:, 128:256]
     square = both(folded(nt(result[...], result[...])))
-    slots = idx_ref[...].astype(jnp.int32)
-    for k in range(CAP):
-        mark[:, k * DEV : (k + 1) * DEV] = mark_row(slots[k : k + 1, :], PAD, 0)
     packed = folded(nn(result[...], mark[...]))
     for j in range(8):
         pair = [packed[:, k * DEV : (k + 1) * DEV] for k in (2 * j, 2 * j + 1)]
@@ -539,10 +569,11 @@
     )(*operands)
 
 
-def exchange(x, lines):
+def exchange(x, lines, axes=AXES):
+    peers = x.shape[0] // lines
     return lax.all_to_all(
-        x.reshape(DEV, 1, lines * 128), AXES, split_axis=0, concat_axis=0, tiled=True
-    ).reshape(DEV * lines, 128)
+        x.reshape(peers, 1, lines * 128), axes, split_axis=0, concat_axis=0, tiled=True
+    ).reshape(peers * lines, 128)
 
 
 def per_device(
@@ -557,13 +588,14 @@
     sep_inverse,
     sep_parent,
 ):
-    my_group = lax.axis_index("leaf")
+    my_half = lax.axis_index("half")
+    my_group = my_half * 8 + lax.axis_index("group")
     my_front = lax.axis_index("front")
     home_slot = jnp.zeros((), jnp.int32)
     for bit in range(LEVELS - 1):
         home_slot = home_slot + (my_group % (2 << bit) == 0).astype(jnp.int32)
     home_at = (home_slot * LEAF + my_front * SHARE).astype(jnp.int32).reshape(1)
-    half = (my_group // 8).astype(jnp.int32).reshape(1)
+    half = my_half.astype(jnp.int32).reshape(1)
     V = pltpu.VMEM
     S = pltpu.SemaphoreType.DMA
     packed, key = call(
@@ -599,7 +631,7 @@
     )
     pushed, leaf_solved, tree = call(
         forward_kernel,
-        [((DEV * S2, 128), F32), ((64, SPAN), F32), ((64, PAD), F32)],
+        [((HALF * S2, 128), F32), ((64, SPAN), F32), ((64, PAD), F32)],
         (home_at, arrived, leaf_rows, leaf_inverse, leaf_below, link),
         [
             V((PAD, PAD), BF16),
@@ -617,7 +649,7 @@
         limit=50,
         far_outs=(1, 2),
     )
-    pushed = exchange(pushed, S2)
+    pushed = exchange(pushed, S2, NEAR)
     other, idx, gram = call(
         side_kernel,
         [((256, PAD), BF16), ((128, 128), F32), ((128, 128), F32)],
@@ -632,19 +664,34 @@
         far=1,
         far_outs=(0,),
     )
-    (paths,) = call(
-        separator_kernel,
-        [((DEV * S3, 128), F32)],
-        (half, pushed, square, link),
-        [
-            V((GROUPS, LEAF, LEAF), F32),
-            V((GROUPS - 1, LEAF, LEAF), F32),
-            S((2 * GROUPS,)),
-        ],
+    small = ((8, LEAF), F32)
+    top, source = call(
+        up_kernel,
+        [small, small],
+        (half, pushed, link, other),
+        [V((7, LEAF, LEAF), F32), S((7,))],
         1,
         far=2,
     )
-    paths = exchange(paths, S3)
+    other_top = lax.ppermute(top, "half", [(0, 1), (1, 0)])
+    (line,) = call(
+        square_kernel,
+        [small],
+        (half, source, square),
+        [V((7, LEAF, LEAF), F32), S((7,))],
+        1,
+        far=1,
+        micros=2,
+    )
+    (paths,) = call(
+        down_kernel,
+        [((HALF * S3, 128), F32)],
+        (half, top, other_top, line, square, link),
+        [V((2, LEAF, LEAF), F32), V((8, LEAF, LEAF), F32), S((10,))],
+        1,
+        far=2,
+    )
+    paths = exchange(paths, S3, NEAR)
     (returning,) = call(
         backward_kernel,
         [((DEV * S4, 128), F32)],
@@ -707,9 +754,10 @@
         P(),
         P(),
     )
+    split_mesh = Mesh(mesh.devices.reshape(2, 8, 8), AXES)
     return jax.shard_map(
         per_device,
-        mesh=mesh,
+        mesh=split_mesh,
         in_specs=placed,
         out_specs=(P(), P(), P(None, AXES)),
         check_vma=False,

time: 134 us -> 132 us (0.985)
  blocking collectives: 19.5 us -> 35 us
  waiting for transfers between devices: 41.5 us -> 27 us
  starting transfers between devices: 25.7 us -> 23.3 us
    all_to_all x1 -> x2, blocking collectives: 19.5 us -> 35 us  [exchange(): lax.all_to_all(x.reshape(peers, 1, lines * 128), axes, split_axis=0, conc...]
    all_to_all x4 -> x3, waiting for transfers between devices: 41.5 us -> 26.6 us  [exchange(): lax.all_to_all(x.reshape(peers, 1, lines * 128), axes, split_axis=0, conc...]
    all_to_all x4 -> x3, starting transfers between devices: 25.7 us -> 21.5 us  [exchange(): lax.all_to_all(x.reshape(peers, 1, lines * 128), axes, split_axis=0, conc...]
    ppermute x0 -> x1, starting transfers between devices: none -> 1.78 us  [per_device(): other_top = lax.ppermute(top, 'half', [(0, 1), (1, 0)])]
    pallas_call x9 -> x11, Pallas kernels: 45.1 us -> 45.5 us  [call(): pl.pallas_call(kernel, out_shape=[jax.ShapeDtypeStruct(shape, dtype) for...]
  transfers between devices with their start and end apart: 4 -> 4, of which waited for: 4 -> 4; matrix products, arithmetic and copies ran while one was open for 0% -> 0% of each run, Pallas kernels for 11% -> 12%
where the time goes in v5:
time: 132 us
  Pallas kernels  45.5 us (34%)
  blocking collectives  35 us (27%)
  waiting for transfers between devices  27 us (20%)
  starting transfers between devices  23.3 us (18%)
    pallas_call x11, Pallas kernels, call(): pl.pallas_call(kernel, out_shape=[jax.ShapeDtypeStruct(shape, dtype) for...  45.5 us
    all_to_all x2, blocking collectives, exchange(): lax.all_to_all(x.reshape(peers, 1, lines * 128), axes, split_axis=0, conc...  35 us
    all_to_all x3, waiting for transfers between devices, exchange(): lax.all_to_all(x.reshape(peers, 1, lines * 128), axes, split_axis=0, conc...  26.6 us
    all_to_all x3, starting transfers between devices, exchange(): lax.all_to_all(x.reshape(peers, 1, lines * 128), axes, split_axis=0, conc...  21.5 us
  transfers between devices with their start and end apart: 4, of which 4 were waited for; matrix products, arithmetic and copies ran while one was open for 0% of the time, Pallas kernels for 12%

profile of v5, /device:TPU:1, one launch (start us, length us, event | category | flops | bytes accessed | tf_op | source)
XLA Modules:
  0.0 131.9 jit_solution(818506509026864048)
XLA Ops:
  0.6 6.1 %shard_map.112 = (f32[2304,128]{1,0:T(8,128)}, s32[1,2176]{1,0:T(1,128)}) custom-call(s32[2080]{0:T(1024)} %vt_ref.1, f32[64,2080]{1,0:T(8,128)} %now_hbm.3, f32[64,2080]{1,0:T(8,128)} %before_hbm.3), custom_call_target="tpu_custom_call" | custom-call | flops 4000000000 | bytes 12000000 | tf_op jit(solution)/shard_map/pallas_call | solution.py:556
  6.7 11.5 %all-to-all-start = ((f32[128,1,2304]{2,1,0:T(1,128)}), f32[128,1,2304]{2,1,0:T(1,128)S(1)}, u32[]{:S(2)}, u32[]{:S(2)}) async-start(f32[128,1,2304]{2,1,0:T(1,128)} %bitcast.21), calls=%async_computation | async-start | bytes 2359296 | tf_op jit(solution)/shard_map/all_to_all | solution.py:574
  18.3 0.0 copy-start.4
  18.3 8.2 %shard_map.113 = (f32[16,256,256]{2,1,0:T(8,128)}, f32[15,256,256]{2,1,0:T(8,128)}) custom-call(f32[16,256,256]{2,1,0:T(8,128)} %inv_hbm.3, f32[15,256,256]{2,1,0:T(8,128)} %parent_hbm.1), custom_call_target="tpu_custom_call" | custom-call | flops 4000000000 | bytes 12000000 | tf_op jit(solution)/shard_map/pallas_call | solution.py:556
  26.5 12.2 %all-to-all-done = f32[128,1,2304]{2,1,0:T(1,128)S(1)} async-done(((f32[128,1,2304]{2,1,0:T(1,128)}), f32[128,1,2304]{2,1,0:T(1,128)S(1)}, u32[]{:S(2)}, u32[]{:S(2)}) %all-to-all-start) | async-done | bytes 1179680 | tf_op jit(solution)/shard_map/all_to_all | solution.py:574
  38.7 0.0 copy-done.4
  38.7 6.4 %shard_map.114 = (f32[640,128]{1,0:T(8,128)}, f32[64,2048]{1,0:T(8,128)S(1)}, f32[64,2176]{1,0:T(8,128)S(1)}) custom-call(s32[1]{0:T(128)} %bitcast.home_ref, f32[2304,128]{1,0:T(8,128)S(1)} %bitcast.12, s32[8,256]{1,0:T(8,128)S(1)} %copy-done.4, f32[8,256,256]{2,1,0:T(8,128)} %inv_hbm.5, f32[8,256,256]{2,1,0:T(8,128)} %below_hbm.3, ...), custom_call_target="tpu_custom_call" | custom-call | flops 4000000000 | bytes 12000000 | tf_op jit(solution)/shard_map/pallas_call | solution.py:556
  45.1 0.0 copy-done
  45.2 5.2 %all-to-all-start.1 = ((f32[64,1,1280]{2,1,0:T(1,128)}), f32[64,1,1280]{2,1,0:T(1,128)S(1)}, u32[]{:S(2)}, u32[]{:S(2)}) async-start(f32[64,1,1280]{2,1,0:T(1,128)} %bitcast.4), calls=%async_computation.1 | async-start | bytes 655360 | tf_op jit(solution)/shard_map/all_to_all | solution.py:574
  50.4 4.3 %shard_map.115 = (bf16[256,2176]{1,0:T(8,128)(2,1)S(1)}, f32[128,128]{1,0:T(8,128)S(1)}, f32[128,128]{1,0:T(8,128)S(1)}) custom-call(f32[2304,128]{1,0:T(8,128)} %bitcast.13, f32[64,2176]{1,0:T(8,128)S(1)} %get-tuple-element.18.tree_hbm), custom_call_target="tpu_custom_call" | custom-call | flops 4000000000 | bytes 12000000 | tf_op jit(solution)/shard_map/pallas_call | solution.py:556
  54.7 0.0 copy-start.5
  54.7 6.1 %all-to-all-done.1 = f32[64,1,1280]{2,1,0:T(1,128)S(1)} async-done(((f32[64,1,1280]{2,1,0:T(1,128)}), f32[64,1,1280]{2,1,0:T(1,128)S(1)}, u32[]{:S(2)}, u32[]{:S(2)}) %all-to-all-start.1) | async-done | bytes 327712 | tf_op jit(solution)/shard_map/all_to_all | solution.py:574
  60.9 2.0 %shard_map.116 = (f32[8,256]{1,0:T(8,128)S(1)}, f32[8,256]{1,0:T(8,128)S(1)}) custom-call(s32[1]{0:T(128)} %bitcast.1.half_ref, f32[640,128]{1,0:T(8,128)S(1)} %bitcast.17, f32[15,256,256]{2,1,0:T(8,128)} %get-tuple-element.16.ready_hbm.link_hbm, bf16[256,2176]{1,0:T(8,128)(2,1)S(1)} %get-tuple-element.19.ready_hbm.other_hbm), custom_call_target="tpu_custom_call" | custom-call | flops 4000000000 | bytes 12000000 | tf_op jit(solution)/shard_map/pallas_call | solution.py:556
  62.8 0.0 copy-done.5
  62.8 1.8 %collective-permute-start = (f32[8,256]{1,0:T(8,128)S(1)}, f32[8,256]{1,0:T(8,128)S(1)}, u32[]{:S(2)}, u32[]{:S(2)}) collective-permute-start(f32[8,256]{1,0:T(8,128)S(1)} %get-tuple-element.20.top_ref), channel_id=1, source_target_pairs={{0,64},{64,0},{1,65},{65,1},{2,66},{66,2},{3,67},{67,3},{4,68},{68... | collective-permute-start | bytes 24584 | tf_op jit(solution)/shard_map/ppermute | solution.py:676
  64.6 2.1 %shard_map.117.line_ref = f32[8,256]{1,0:T(8,128)S(1)} custom-call(s32[1]{0:T(128)} %bitcast.1.half_ref, f32[8,256]{1,0:T(8,128)S(1)} %get-tuple-element.21.source_ref, f32[16,256,256]{2,1,0:T(8,128)} %get-tuple-element.22.square_hbm), custom_call_target="tpu_custom_call" | custom-call | flops 2000000000 | bytes 6000000 | tf_op jit(solution)/shard_map/pallas_call | solution.py:556
  66.7 0.4 collective-permute-done.other_ref
  67.2 2.4 %shard_map.118 = f32[640,128]{1,0:T(8,128)S(1)} custom-call(s32[1]{0:T(128)} %bitcast.1.half_ref, f32[8,256]{1,0:T(8,128)S(1)} %get-tuple-element.20.top_ref, f32[8,256]{1,0:T(8,128)S(1)} %collective-permute-done.other_ref, f32[8,256]{1,0:T(8,128)S(1)} %shard_map.117.line_ref, f32[16,256,256]{2,1,0:T(8,128)} %get-tuple-element.22.square_hbm, ...), custom_call_target="tpu_custom_call" | custom-call | flops 4000000000 | bytes 12000000 | tf_op jit(solution)/shard_map/pallas_call | solution.py:556
  69.5 15.8 %all_to_all.25 = f32[64,1,1280]{2,1,0:T(1,128)S(1)} all-to-all(f32[64,1,1280]{2,1,0:T(1,128)S(1)} %bitcast.19), channel_id=1, replica_groups=mesh['half'=2,'group'=8,'front'=8] {'group','front'}, dimensions={0} | all-to-all | bytes 655360 | tf_op jit(solution)/shard_map/all_to_all | solution.py:574
  85.3 7.0 %shard_map.119 = f32[1280,128]{1,0:T(8,128)S(1)} custom-call(s32[1]{0:T(128)} %bitcast.home_ref, f32[640,128]{1,0:T(8,128)S(1)} %bitcast.18, s32[8,256]{1,0:T(8,128)S(1)} %copy-done.4, f32[128,128]{1,0:T(8,128)S(1)} %get-tuple-element.23.idx_ref, f32[128,128]{1,0:T(8,128)S(1)} %get-tuple-element.24.gram_ref, f32[8,256,256]{2,1,0:T(8,128)} %inv_hbm.5, ...), custom_call_target="tpu_custom_call" | custom-call | flops 4000000000 | bytes 12000000 | tf_op jit(solution)/shard_map/pallas_call | solution.py:556
  92.4 19.1 %all_to_all.26 = f32[128,1,1280]{2,1,0:T(1,128)S(1)} all-to-all(f32[128,1,1280]{2,1,0:T(1,128)S(1)} %bitcast.16), channel_id=1, replica_groups=mesh['half'=2,'group'=8,'front'=8] {'half','group','front'}, dimensions={0} | all-to-all | bytes 1310720 | tf_op jit(solution)/shard_map/all_to_all | solution.py:574
  111.5 0.7 shard_map.120
  112.2 4.8 %all-to-all-start.4 = ((f32[128,1,256]{2,1,0:T(1,128)}), f32[128,1,256]{2,1,0:T(1,128)S(1)}, u32[]{:S(2)}, u32[]{:S(2)}) async-start(f32[128,1,256]{2,1,0:T(1,128)} %bitcast.10), calls=%async_computation.4 | async-start | bytes 262144 | tf_op jit(solution)/shard_map/all_to_all | solution.py:574
  117.0 0.0 copy-done.6
  117.0 0.0 copy-start.1
  117.0 0.0 copy-start.2
  117.0 0.0 copy-start.3
  117.0 1.7 %shard_map.121.solved_ref = f32[64,2080]{1,0:T(8,128)S(1)} custom-call(s32[1,2176]{1,0:T(1,128)S(1)} %copy-done.6, f32[1280,128]{1,0:T(8,128)S(1)} %bitcast.15), custom_call_target="tpu_custom_call" | custom-call | flops 4000000000 | bytes 12000000 | tf_op jit(solution)/shard_map/pallas_call | solution.py:556
  118.7 8.2 %all-to-all-done.4 = f32[128,1,256]{2,1,0:T(1,128)S(1)} async-done(((f32[128,1,256]{2,1,0:T(1,128)}), f32[128,1,256]{2,1,0:T(1,128)S(1)}, u32[]{:S(2)}, u32[]{:S(2)}) %all-to-all-start.4) | async-done | bytes 131104 | tf_op jit(solution)/shard_map/all_to_all | solution.py:574
  126.9 0.0 copy-done.1
  126.9 0.0 copy-done.3
  126.9 4.7 %shard_map.122 = (f32[64,64]{1,0:T(8,128)}, f32[64,64]{1,0:T(8,128)}, f32[64,2080]{1,0:T(8,128)}) custom-call(f32[256,128]{1,0:T(8,128)S(1)} %bitcast.20, f32[64,2080]{1,0:T(8,128)S(1)} %shard_map.121.solved_ref, f32[64,64]{1,0:T(8,128)S(1)} %copy-done.3, f32[64,2080]{1,0:T(8,128)S(1)} %copy-done.1, f32[64,2080]{1,0:T(8,128)S(1)} %copy-done.2), custom_call_target="tpu_custom_call" | custom-call | flops 4000000000 | bytes 12000000 | tf_op jit(solution)/shard_map/pallas_call | solution.py:556
  (3 shorter events, 0.0 us)
Async XLA Ops:
  6.7 32.0 %all-to-all-start = ((f32[128,1,2304]{2,1,0:T(1,128)}), f32[128,1,2304]{2,1,0:T(1,128)S(1)}, u32[]{:S(2)}, u32[]{:S(2)}) async-start(f32[128,1,2304]{2,1,0:T(1,128)} %bitcast.21), calls=%async_computation | async-start | bytes 2359296 | tf_op jit(solution)/shard_map/all_to_all | solution.py:574
  18.3 20.4 %copy-start.4 = (s32[8,256]{1,0:T(8,128)S(1)}, s32[8,256]{1,0:T(8,128)}, u32[]{:S(2)}) copy-start(s32[8,256]{1,0:T(8,128)} %rows_ref.3) | copy-start | bytes 24580
  38.7 6.5 %copy-start = (f32[128,1,2304]{2,1,0:T(1,128)}, f32[128,1,2304]{2,1,0:T(1,128)S(1)}, u32[]{:S(2)}) copy-start(f32[128,1,2304]{2,1,0:T(1,128)S(1)} %all-to-all-done) | copy-start | bytes 3538948
  45.2 15.7 %all-to-all-start.1 = ((f32[64,1,1280]{2,1,0:T(1,128)}), f32[64,1,1280]{2,1,0:T(1,128)S(1)}, u32[]{:S(2)}, u32[]{:S(2)}) async-start(f32[64,1,1280]{2,1,0:T(1,128)} %bitcast.4), calls=%async_computation.1 | async-start | bytes 655360 | tf_op jit(solution)/shard_map/all_to_all | solution.py:574
  54.7 8.1 %copy-start.5 = (bf16[256,2176]{1,0:T(8,128)(2,1)}, bf16[256,2176]{1,0:T(8,128)(2,1)S(1)}, u32[]{:S(2)}) copy-start(bf16[256,2176]{1,0:T(8,128)(2,1)S(1)} %get-tuple-element.19.ready_hbm.other_hbm) | copy-start | bytes 3342340
  62.8 4.3 %collective-permute-start = (f32[8,256]{1,0:T(8,128)S(1)}, f32[8,256]{1,0:T(8,128)S(1)}, u32[]{:S(2)}, u32[]{:S(2)}) collective-permute-start(f32[8,256]{1,0:T(8,128)S(1)} %get-tuple-element.20.top_ref), channel_id=1, source_target_pairs={{0,64},{64,0},{1,65},{65,1},{2,66},{66,2},{3,67},{67,3},{4,68},{68... | collective-permute-start | bytes 24584 | tf_op jit(solution)/shard_map/ppermute | solution.py:676
  111.5 5.5 %copy-start.6 = (s32[1,2176]{1,0:T(1,128)S(1)}, s32[1,2176]{1,0:T(1,128)}, u32[]{:S(2)}) copy-start(s32[1,2176]{1,0:T(1,128)} %get-tuple-element.26.key_ref) | copy-start | bytes 26116
  112.2 14.7 %all-to-all-start.4 = ((f32[128,1,256]{2,1,0:T(1,128)}), f32[128,1,256]{2,1,0:T(1,128)S(1)}, u32[]{:S(2)}, u32[]{:S(2)}) async-start(f32[128,1,256]{2,1,0:T(1,128)} %bitcast.10), calls=%async_computation.4 | async-start | bytes 262144 | tf_op jit(solution)/shard_map/all_to_all | solution.py:574
  117.0 9.9 %copy-start.1 = (f32[64,2080]{1,0:T(8,128)S(1)}, f32[64,2080]{1,0:T(8,128)}, u32[]{:S(2)}) copy-start(f32[64,2080]{1,0:T(8,128)} %now_hbm.3) | copy-start | bytes 1597444
  117.0 9.9 %copy-start.2 = (f32[64,2080]{1,0:T(8,128)S(1)}, f32[64,2080]{1,0:T(8,128)}, u32[]{:S(2)}) copy-start(f32[64,2080]{1,0:T(8,128)} %before_hbm.3) | copy-start | bytes 1597444
  117.0 9.9 %copy-start.3 = (f32[64,64]{1,0:T(8,128)S(1)}, f32[64,64]{1,0:T(8,128)}, u32[]{:S(2)}) copy-start(f32[64,64]{1,0:T(8,128)} %coupling_ref.1) | copy-start | bytes 49156

commit v6 on v5

--- a/solution.py
+++ b/solution.py
@@ -100,6 +100,10 @@
     return x + pltpu.roll(x, 64, 1)
 
 
+def crossed(x, half):
+    return jnp.where(half == 1, jnp.concatenate([x[32:64], x[0:32]], axis=0), x)
+
+
 def folded(x):
     half = x.shape[0] // 2
     return x[0:half] + x[half:]
@@ -136,6 +140,8 @@
         carry = carry + counts[:, 128:256]
     rank = jnp.concatenate(ranks, axis=1).astype(jnp.int32)
     key = jnp.where(target < 0, -1, rank * DEV + bucket)
+    for k in range(8):
+        mark[k * DEV : (k + 1) * DEV, :] = mark_row(key, DEV, k * DEV)
     for load in loads:
         load.wait()
     value[:, SPAN:PAD] = jnp.zeros((4 * VEC, PAD - SPAN), BF16)
@@ -146,7 +152,7 @@
     value[128:192, 0:ROWS] = now_lo
     value[192:256, 0:ROWS] = bef_lo
     key_ref[...] = key
-    for k in range(CAP):
+    for k in range(8, CAP):
         mark[k * DEV : (k + 1) * DEV, :] = mark_row(key, DEV, k * DEV)
     block = nt(mark[...], value[...])
     block = block[:, 0:128] + block[:, 128:256]
@@ -189,23 +195,18 @@
     tree_ref,
     sems,
 ):
-    inv_loads = [
-        fetch(inv_hbm.at[q], inv_ref.at[q], sems.at[q]) for q in range(NLEAF)
-    ]
-    below_loads = [
-        fetch(below_hbm.at[q], below_ref.at[q], sems.at[NLEAF + q]) for q in range(NLEAF)
-    ]
+    loads = [fetch(inv_hbm, inv_ref, sems.at[0]), fetch(below_hbm, below_ref, sems.at[1])]
     idx = recv_ref[pl.ds(CAP, DEV, stride=S1), :].astype(jnp.int32)
     for k in range(CAP):
         got = recv_ref[pl.ds(k, DEV, stride=S1), :].T
         value[:, k * DEV : (k + 1) * DEV] = stacked(got[0:64])
         mark[k * DEV : (k + 1) * DEV, :] = mark_column(idx[:, k : k + 1], PAD)
     tree_ref[...] = folded(nn(value[...], mark[...]))
-    stores = [fetch(tree_ref, tree_hbm, sems.at[2 * NLEAF])]
+    stores = [fetch(tree_ref, tree_hbm, sems.at[2])]
     rows = rows_ref[...].astype(F32).T.astype(jnp.int32)
     for q in range(NLEAF):
         moved[q * LEAF : (q + 1) * LEAF, :] = mark_column(rows[:, q : q + 1], PATH)
-    for load in inv_loads + below_loads:
+    for load in loads:
         load.wait()
     for q in range(NLEAF):
         cols = slice(q * LEAF, (q + 1) * LEAF)
@@ -216,13 +217,13 @@
         hi, lo = split(below_ref[q])
         solved = stacked(solved)
         update[:, cols] = stacked(folded(nt(solved, hi) + nt(solved, lo)))
-    stores.append(fetch(solved_ref, solved_hbm, sems.at[2 * NLEAF + 1]))
+    stores.append(fetch(solved_ref, solved_hbm, sems.at[3]))
     pushed = folded(nn(update[...], moved[...]))
     start = home_ref[0]
     own = pltpu.roll(tree_ref[:, SPAN:PAD], start % 128, 1)
     for j in range(S2):
         chunk = jnp.where(start // 128 == j, own, 0.0) - pushed[:, j * 128 : (j + 1) * 128]
-        out_ref[pl.ds(j, HALF, stride=S2), :] = chunk
+        out_ref[pl.ds(j, HALF, stride=S2), :] = crossed(chunk, home_ref[1])
     for store in stores:
         store.wait()
 
@@ -336,49 +337,34 @@
     source_ref[...] = jnp.concatenate(sums[0:7] + [jnp.zeros((1, LEAF), F32)], axis=0)
 
 
-def square_kernel(half_ref, source_ref, square_hbm, out_ref, square_ref, sems):
+def square_kernel(
+    half_ref, source_ref, square_hbm, link_hbm, out_ref, high_ref, square_ref, sems
+):
     half = half_ref[0]
     loads = [
         fetch(square_hbm.at[at + 1], square_ref.at[i], sems.at[i])
         for i, at in enumerate(local_links(half))
+    ]
+    high = [
+        fetch(square_hbm.at[0:2], high_ref.at[0:2], sems.at[7]),
+        fetch(link_hbm.at[0], high_ref.at[2], sems.at[8]),
     ]
     eye = iota((128, 128), 0) == iota((128, 128), 1)
     for load in loads:
         load.wait()
     lines = [apply_t(square_ref[i], source_ref[i : i + 1, :], eye) for i in range(7)]
     out_ref[...] = jnp.concatenate(lines + [jnp.zeros((1, LEAF), F32)], axis=0)
-
-
-def down_kernel(
-    half_ref,
-    top_ref,
-    other_ref,
-    line_ref,
-    square_hbm,
-    link_hbm,
-    out_ref,
-    square_ref,
-    link_ref,
-    sems,
-):
-    half = half_ref[0]
-    first = [
-        fetch(link_hbm.at[0], link_ref.at[7], sems.at[7]),
-        fetch(square_hbm.at[0], square_ref.at[0], sems.at[8]),
-        fetch(square_hbm.at[1], square_ref.at[1], sems.at[9]),
-    ]
-    links = local_links(half)
-    loads = [fetch(link_hbm.at[links[i]], link_ref.at[i], sems.at[i]) for i in range(6, -1, -1)]
+    for load in high:
+        load.wait()
+
+
+def down_kernel(top_ref, other_ref, line_ref, link_ref, high_ref, out_ref):
     eye = iota((128, 128), 0) == iota((128, 128), 1)
     total = top_ref[...] + other_ref[...]
     below = total[0:1]
-    for load in first:
-        load.wait()
-    root = total[1:2] - apply(link_ref[7], below, eye)
-    root = apply_t(square_ref[0], root, eye)
-    below = apply_t(square_ref[1], below, eye) - apply_t(link_ref[7], root, eye)
-    for load in loads:
-        load.wait()
+    root = total[1:2] - apply(high_ref[2], below, eye)
+    root = apply_t(high_ref[0], root, eye)
+    below = apply_t(high_ref[1], below, eye) - apply_t(high_ref[2], root, eye)
     line = line_ref[...]
     third = line[6:7] - apply_t(link_ref[6], below, eye)
     second = [line[4 + c : 5 + c] - apply_t(link_ref[4 + c], third, eye) for c in range(2)]
@@ -398,8 +384,8 @@
     rows_ref,
     idx_ref,
     gram_ref,
-    inv_hbm,
-    below_hbm,
+    inv_ref,
+    below_ref,
     solved_hbm,
     other_hbm,
     out_ref,
@@ -408,30 +394,19 @@
     moved,
     mark,
     result,
-    inv_ref,
-    below_ref,
     solved_ref,
     other_ref,
     sems,
 ):
-    loads = [fetch(solved_hbm, solved_ref, sems.at[2 * NLEAF])]
-    below_loads = []
-    inv_loads = []
-    for q in range(NLEAF):
-        below_loads.append(fetch(below_hbm.at[q], below_ref.at[q], sems.at[q]))
-        inv_loads.append(fetch(inv_hbm.at[q], inv_ref.at[q], sems.at[NLEAF + q]))
-    loads.append(fetch(other_hbm, other_ref, sems.at[2 * NLEAF + 1]))
+    loads = [fetch(solved_hbm, solved_ref, sems.at[0]), fetch(other_hbm, other_ref, sems.at[1])]
     for q in range(NLEAF):
         moved[:, q * LEAF : (q + 1) * LEAF] = mark_row(rows_ref[q : q + 1, :], PATH, 0)
     for j in range(S3):
-        chunk = recv_ref[pl.ds(j, HALF, stride=S3), :]
+        chunk = crossed(recv_ref[pl.ds(j, HALF, stride=S3), :], home_ref[1])
         known[:, j * 128 : (j + 1) * 128] = chunk
         parts[:, j * 128 : (j + 1) * 128] = stacked(chunk)
     picked = folded(nn(parts[...], moved[...]))
-    slots = idx_ref[...].astype(jnp.int32)
-    for k in range(CAP):
-        mark[:, k * DEV : (k + 1) * DEV] = mark_row(slots[k : k + 1, :], PAD, 0)
-    for load in loads + below_loads + inv_loads:
+    for load in loads:
         load.wait()
     start = home_ref[0]
     tile = pl.multiple_of((start // 128) * 128, 128)
@@ -448,6 +423,9 @@
     cross = folded(nt(result[...], other_ref[...]))
     cross = cross[:, 0:128] + cross[:, 128:256]
     square = both(folded(nt(result[...], result[...])))
+    slots = idx_ref[...].astype(jnp.int32)
+    for k in range(CAP):
+        mark[:, k * DEV : (k + 1) * DEV] = mark_row(slots[k : k + 1, :], PAD, 0)
     packed = folded(nn(result[...], mark[...]))
     for j in range(8):
         pair = [packed[:, k * DEV : (k + 1) * DEV] for k in (2 * j, 2 * j + 1)]
@@ -478,20 +456,8 @@
 
 
 def finish_kernel(
-    recv_ref,
-    solved_ref,
-    coupling_ref,
-    now_hbm,
-    before_hbm,
-    proj_ref,
-    factor_ref,
-    next_ref,
-    value,
-    now_ref,
-    before_ref,
-    sems,
+    recv_ref, solved_ref, now_ref, before_ref, coupling_ref, proj_ref, factor_ref, next_ref, value
 ):
-    loads = [fetch(now_hbm, now_ref, sems.at[0]), fetch(before_hbm, before_ref, sems.at[1])]
     first = recv_ref[pl.ds(0, DEV, stride=2), :]
     second = recv_ref[pl.ds(1, DEV, stride=2), :]
     count = 1.0 / (ROWS * DEV)
@@ -534,20 +500,12 @@
     )
     hi, lo = split(weight)
     weight = jnp.concatenate([hi, lo], axis=0)
-    for load in loads:
-        load.wait()
     for b, ref in enumerate((solved_ref, now_ref, before_ref)):
         hi, lo = split(ref[...])
         value[b * 64 : (b + 1) * 64, 0:ROWS] = hi
         value[b * 64 : (b + 1) * 64, PAD : PAD + ROWS] = lo
-    high = nn(weight, value[:, 0:ROWS])
-    low = nn(weight, value[:, PAD : PAD + ROWS])
-    total = high + low
-    next_ref[...] = total[0:64] + total[64:128]
-
-
-def vmem(count):
-    return [pl.BlockSpec(memory_space=pltpu.VMEM)] * count
+    total = nn(weight, value[:, 0:ROWS]) + nn(weight, value[:, PAD : PAD + ROWS])
+    next_ref[...] = folded(total)
 
 
 def call(kernel, outs, operands, scratch=(), scalars=0, far=0, far_outs=(), limit=52, micros=4):
@@ -594,7 +552,7 @@
     home_slot = jnp.zeros((), jnp.int32)
     for bit in range(LEVELS - 1):
         home_slot = home_slot + (my_group % (2 << bit) == 0).astype(jnp.int32)
-    home_at = (home_slot * LEAF + my_front * SHARE).astype(jnp.int32).reshape(1)
+    home_at = jnp.stack([home_slot * LEAF + my_front * SHARE, my_half]).astype(jnp.int32)
     half = my_half.astype(jnp.int32).reshape(1)
     V = pltpu.VMEM
     S = pltpu.SemaphoreType.DMA
@@ -642,7 +600,7 @@
             V((NLEAF, LEAF, LEAF), F32),
             V((64, SPAN), F32),
             V((64, PAD), F32),
-            S((2 * NLEAF + 2,)),
+            S((4,)),
         ],
         1,
         far=3,
@@ -665,31 +623,29 @@
         far_outs=(0,),
     )
     small = ((8, LEAF), F32)
-    top, source = call(
+    top, source, links = call(
         up_kernel,
-        [small, small],
+        [small, small, ((7, LEAF, LEAF), F32)],
         (half, pushed, link, other),
-        [V((7, LEAF, LEAF), F32), S((7,))],
+        [S((7,))],
         1,
         far=2,
     )
-    other_top = lax.ppermute(top, "half", [(0, 1), (1, 0)])
-    (line,) = call(
+    across = [(i, i ^ 12) for i in range(GROUPS)]
+    other_top = lax.ppermute(top, ("half", "group"), across)
+    line, high = call(
         square_kernel,
-        [small],
-        (half, source, square),
-        [V((7, LEAF, LEAF), F32), S((7,))],
+        [small, ((3, LEAF, LEAF), F32)],
+        (half, source, square, link),
+        [V((7, LEAF, LEAF), F32), S((9,))],
         1,
-        far=1,
+        far=2,
         micros=2,
     )
     (paths,) = call(
         down_kernel,
         [((HALF * S3, 128), F32)],
-        (half, top, other_top, line, square, link),
-        [V((2, LEAF, LEAF), F32), V((8, LEAF, LEAF), F32), S((10,))],
-        1,
-        far=2,
+        (top, other_top, line, links, high),
     )
     paths = exchange(paths, S3, NEAR)
     (returning,) = call(
@@ -712,14 +668,13 @@
             V((PATH, SPAN), BF16),
             V((PAD, PAD), BF16),
             V((128, PAD), BF16),
-            V((NLEAF, LEAF, LEAF), F32),
-            V((NLEAF, LEAF, LEAF), F32),
             V((64, SPAN), F32),
             V((256, PAD), BF16),
-            S((2 * NLEAF + 2,)),
+            S((2,)),
         ],
         1,
-        far=4,
+        far=2,
+        limit=46,
     )
     returned = exchange(returning, S4)
     (sums,) = call(total_kernel, [((DEV * 2, 128), F32)], (returned,), micros=1)
@@ -734,9 +689,8 @@
         call(
             finish_kernel,
             [((64, 64), F32), ((64, 64), F32), ((64, ROWS), F32)],
-            (sums, solved, coupling, block_now, block_before),
-            [V((192, 2 * PAD), BF16), V((64, ROWS), F32), V((64, ROWS), F32), S((2,))],
-            far=2,
+            (sums, solved, block_now, block_before, coupling),
+            [V((192, 2 * PAD), BF16)],
         )
     )
 

time: 132 us -> 132 us (level)
  no operation moved by 1% of the time
where the time goes in v6:
time: 132 us; the launch traced here: 131 us
  Pallas kernels  45.3 us (34%)
  blocking collectives  34.9 us (26%)
  waiting for transfers between devices  27.8 us (21%)
  starting transfers between devices  22.1 us (17%)
    pallas_call x11, Pallas kernels, call(): pl.pallas_call(kernel, out_shape=[jax.ShapeDtypeStruct(shape, dtype) for...  45.3 us
    all_to_all x2, blocking collectives, exchange(): lax.all_to_all(x.reshape(peers, 1, lines * 128), axes, split_axis=0, conc...  34.9 us
    all_to_all x3, waiting for transfers between devices, exchange(): lax.all_to_all(x.reshape(peers, 1, lines * 128), axes, split_axis=0, conc...  26.5 us
    all_to_all x3, starting transfers between devices, exchange(): lax.all_to_all(x.reshape(peers, 1, lines * 128), axes, split_axis=0, conc...  21.5 us
  transfers between devices with their start and end apart: 4, of which 4 were waited for; matrix products, arithmetic and copies ran while one was open for 0% of the time, Pallas kernels for 12%

profile of v6, /device:TPU:1, one launch (start us, length us, event | category | flops | bytes accessed | tf_op | source)
XLA Modules:
  0.0 131.2 jit_solution(13350636042161929712)
XLA Ops:
  0.6 6.1 %shard_map.112 = (f32[2304,128]{1,0:T(8,128)}, s32[1,2176]{1,0:T(1,128)}) custom-call(s32[2080]{0:T(1024)} %vt_ref.1, f32[64,2080]{1,0:T(8,128)} %now_ref.1, f32[64,2080]{1,0:T(8,128)} %before_ref.1), custom_call_target="tpu_custom_call" | custom-call | flops 4000000000 | bytes 12000000 | tf_op jit(solution)/shard_map/pallas_call | solution.py:514
  6.7 11.5 %all-to-all-start = ((f32[128,1,2304]{2,1,0:T(1,128)}), f32[128,1,2304]{2,1,0:T(1,128)S(1)}, u32[]{:S(2)}, u32[]{:S(2)}) async-start(f32[128,1,2304]{2,1,0:T(1,128)} %bitcast.21), calls=%async_computation | async-start | bytes 2359296 | tf_op jit(solution)/shard_map/all_to_all | solution.py:532
  18.3 0.1 pad_add_fusion.home_ref
  18.3 8.2 %shard_map.113 = (f32[16,256,256]{2,1,0:T(8,128)}, f32[15,256,256]{2,1,0:T(8,128)}) custom-call(f32[16,256,256]{2,1,0:T(8,128)} %inv_hbm.2, f32[15,256,256]{2,1,0:T(8,128)} %parent_hbm.1), custom_call_target="tpu_custom_call" | custom-call | flops 4000000000 | bytes 12000000 | tf_op jit(solution)/shard_map/pallas_call | solution.py:514
  26.5 12.2 %all-to-all-done = f32[128,1,2304]{2,1,0:T(1,128)S(1)} async-done(((f32[128,1,2304]{2,1,0:T(1,128)}), f32[128,1,2304]{2,1,0:T(1,128)S(1)}, u32[]{:S(2)}, u32[]{:S(2)}) %all-to-all-start) | async-done | bytes 1179680 | tf_op jit(solution)/shard_map/all_to_all | solution.py:532
  38.7 0.0 copy-done.6
  38.7 6.9 %shard_map.114 = (f32[640,128]{1,0:T(8,128)}, f32[64,2048]{1,0:T(8,128)S(1)}, f32[64,2176]{1,0:T(8,128)S(1)}) custom-call(s32[2]{0:T(128)S(1)} %pad_add_fusion.home_ref, f32[2304,128]{1,0:T(8,128)S(1)} %bitcast.12, s32[8,256]{1,0:T(8,128)S(1)} %copy-done.6, f32[8,256,256]{2,1,0:T(8,128)} %inv_ref.1, f32[8,256,256]{2,1,0:T(8,128)} %below_ref.1, ...), custom_call_target="tpu_custom_call" | custom-call | flops 4000000000 | bytes 12000000 | tf_op jit(solution)/shard_map/pallas_call | solution.py:514
  45.6 0.0 copy-done
  45.6 5.2 %all-to-all-start.1 = ((f32[64,1,1280]{2,1,0:T(1,128)}), f32[64,1,1280]{2,1,0:T(1,128)S(1)}, u32[]{:S(2)}, u32[]{:S(2)}) async-start(f32[64,1,1280]{2,1,0:T(1,128)} %bitcast.4), calls=%async_computation.1 | async-start | bytes 655360 | tf_op jit(solution)/shard_map/all_to_all | solution.py:532
  50.8 4.3 %shard_map.115 = (bf16[256,2176]{1,0:T(8,128)(2,1)S(1)}, f32[128,128]{1,0:T(8,128)S(1)}, f32[128,128]{1,0:T(8,128)S(1)}) custom-call(f32[2304,128]{1,0:T(8,128)} %bitcast.13, f32[64,2176]{1,0:T(8,128)S(1)} %get-tuple-element.21.tree_hbm), custom_call_target="tpu_custom_call" | custom-call | flops 4000000000 | bytes 12000000 | tf_op jit(solution)/shard_map/pallas_call | solution.py:514
  55.1 6.2 %all-to-all-done.1 = f32[64,1,1280]{2,1,0:T(1,128)S(1)} async-done(((f32[64,1,1280]{2,1,0:T(1,128)}), f32[64,1,1280]{2,1,0:T(1,128)S(1)}, u32[]{:S(2)}, u32[]{:S(2)}) %all-to-all-start.1) | async-done | bytes 327712 | tf_op jit(solution)/shard_map/all_to_all | solution.py:532
  61.3 3.2 %shard_map.116 = (f32[8,256]{1,0:T(8,128)S(1)}, f32[8,256]{1,0:T(8,128)S(1)}, f32[7,256,256]{2,1,0:T(8,128)}) custom-call(s32[1]{0:T(128)} %bitcast.1.half_ref, f32[640,128]{1,0:T(8,128)S(1)} %bitcast.17, f32[15,256,256]{2,1,0:T(8,128)} %get-tuple-element.19.ready_hbm.link_hbm, bf16[256,2176]{1,0:T(8,128)(2,1)S(1)} %get-tuple-element.22.ready_hbm.other_hbm), custom_call_target="tpu_custom_call" | custom-call | flops 4000000000 | bytes 12000000 | tf_op jit(solution)/shard_map/pallas_call | solution.py:514
  64.5 0.6 collective-permute-start
  65.1 2.1 %shard_map.117 = (f32[8,256]{1,0:T(8,128)S(1)}, f32[3,256,256]{2,1,0:T(8,128)S(1)}) custom-call(s32[1]{0:T(128)} %bitcast.1.half_ref, f32[8,256]{1,0:T(8,128)S(1)} %get-tuple-element.24.source_ref, f32[16,256,256]{2,1,0:T(8,128)} %get-tuple-element.25.square_hbm, f32[15,256,256]{2,1,0:T(8,128)} %get-tuple-element.19.ready_hbm.link_hbm), custom_call_target="tpu_custom_call" | custom-call | flops 2000000000 | bytes 6000000 | tf_op jit(solution)/shard_map/pallas_call | solution.py:514
  67.2 1.3 collective-permute-done.other_ref
  68.5 2.8 %shard_map.118 = f32[640,128]{1,0:T(8,128)S(1)} custom-call(f32[8,256]{1,0:T(8,128)S(1)} %get-tuple-element.23.top_ref, f32[8,256]{1,0:T(8,128)S(1)} %collective-permute-done.other_ref, f32[8,256]{1,0:T(8,128)S(1)} %get-tuple-element.26.line_ref, f32[7,256,256]{2,1,0:T(8,128)} %get-tuple-element.27.link_ref, f32[3,256,256]{2,1,0:T(8,128)S(1)} %get-tuple-element.28.high_ref), custom_call_target="tpu_custom_call" | custom-call | flops 4000000000 | bytes 12000000 | tf_op jit(solution)/shard_map/pallas_call | solution.py:514
  71.3 15.5 %all_to_all.25 = f32[64,1,1280]{2,1,0:T(1,128)S(1)} all-to-all(f32[64,1,1280]{2,1,0:T(1,128)S(1)} %bitcast.19), channel_id=1, replica_groups=mesh['half'=2,'group'=8,'front'=8] {'group','front'}, dimensions={0} | all-to-all | bytes 655360 | tf_op jit(solution)/shard_map/all_to_all | solution.py:532
  86.8 0.0 copy-done.1
  86.8 0.0 copy-done.2
  86.8 5.0 %shard_map.119 = f32[1280,128]{1,0:T(8,128)S(1)} custom-call(s32[2]{0:T(128)S(1)} %pad_add_fusion.home_ref, f32[640,128]{1,0:T(8,128)S(1)} %bitcast.18, s32[8,256]{1,0:T(8,128)S(1)} %copy-done.6, f32[128,128]{1,0:T(8,128)S(1)} %get-tuple-element.29.idx_ref, f32[128,128]{1,0:T(8,128)S(1)} %get-tuple-element.30.gram_ref, f32[8,256,256]{2,1,0:T(8,128)S(1)} %copy-done.1, ...), custom_call_target="tpu_custom_call" | custom-call | flops 4000000000 | bytes 12000000 | tf_op jit(solution)/shard_map/pallas_call | solution.py:514
  91.8 19.4 %all_to_all.26 = f32[128,1,1280]{2,1,0:T(1,128)S(1)} all-to-all(f32[128,1,1280]{2,1,0:T(1,128)S(1)} %bitcast.16), channel_id=1, replica_groups=mesh['half'=2,'group'=8,'front'=8] {'half','group','front'}, dimensions={0} | all-to-all | bytes 1310720 | tf_op jit(solution)/shard_map/all_to_all | solution.py:532
  111.3 0.7 shard_map.120
  111.9 4.8 %all-to-all-start.4 = ((f32[128,1,256]{2,1,0:T(1,128)}), f32[128,1,256]{2,1,0:T(1,128)S(1)}, u32[]{:S(2)}, u32[]{:S(2)}) async-start(f32[128,1,256]{2,1,0:T(1,128)} %bitcast.10), calls=%async_computation.4 | async-start | bytes 262144 | tf_op jit(solution)/shard_map/all_to_all | solution.py:532
  116.7 0.0 copy-done.7
  116.7 0.0 copy-start.3
  116.7 0.0 copy-start.4
  116.7 0.0 copy-start.5
  116.8 1.7 %shard_map.121.solved_ref = f32[64,2080]{1,0:T(8,128)S(1)} custom-call(s32[1,2176]{1,0:T(1,128)S(1)} %copy-done.7, f32[1280,128]{1,0:T(8,128)S(1)} %bitcast.15), custom_call_target="tpu_custom_call" | custom-call | flops 4000000000 | bytes 12000000 | tf_op jit(solution)/shard_map/pallas_call | solution.py:514
  118.4 8.2 %all-to-all-done.4 = f32[128,1,256]{2,1,0:T(1,128)S(1)} async-done(((f32[128,1,256]{2,1,0:T(1,128)}), f32[128,1,256]{2,1,0:T(1,128)S(1)}, u32[]{:S(2)}, u32[]{:S(2)}) %all-to-all-start.4) | async-done | bytes 131104 | tf_op jit(solution)/shard_map/all_to_all | solution.py:532
  126.7 0.0 copy-done.3
  126.7 0.0 copy-done.4
  126.7 4.5 %shard_map.122 = (f32[64,64]{1,0:T(8,128)}, f32[64,64]{1,0:T(8,128)}, f32[64,2080]{1,0:T(8,128)}) custom-call(f32[256,128]{1,0:T(8,128)S(1)} %bitcast.20, f32[64,2080]{1,0:T(8,128)S(1)} %shard_map.121.solved_ref, f32[64,2080]{1,0:T(8,128)S(1)} %copy-done.3, f32[64,2080]{1,0:T(8,128)S(1)} %copy-done.4, f32[64,64]{1,0:T(8,128)S(1)} %copy-done.5), custom_call_target="tpu_custom_call" | custom-call | flops 4000000000 | bytes 12000000 | tf_op jit(solution)/shard_map/pallas_call | solution.py:514
  (6 shorter events, 0.0 us)
Async XLA Ops:
  6.7 32.0 %all-to-all-start = ((f32[128,1,2304]{2,1,0:T(1,128)}), f32[128,1,2304]{2,1,0:T(1,128)S(1)}, u32[]{:S(2)}, u32[]{:S(2)}) async-start(f32[128,1,2304]{2,1,0:T(1,128)} %bitcast.21), calls=%async_computation | async-start | bytes 2359296 | tf_op jit(solution)/shard_map/all_to_all | solution.py:532
  18.3 20.4 %copy-start.6 = (s32[8,256]{1,0:T(8,128)S(1)}, s32[8,256]{1,0:T(8,128)}, u32[]{:S(2)}) copy-start(s32[8,256]{1,0:T(8,128)} %rows_ref.3) | copy-start | bytes 24580
  38.7 6.9 %copy-start = (f32[128,1,2304]{2,1,0:T(1,128)}, f32[128,1,2304]{2,1,0:T(1,128)S(1)}, u32[]{:S(2)}) copy-start(f32[128,1,2304]{2,1,0:T(1,128)S(1)} %all-to-all-done) | copy-start | bytes 3538948
  45.6 15.7 %all-to-all-start.1 = ((f32[64,1,1280]{2,1,0:T(1,128)}), f32[64,1,1280]{2,1,0:T(1,128)S(1)}, u32[]{:S(2)}, u32[]{:S(2)}) async-start(f32[64,1,1280]{2,1,0:T(1,128)} %bitcast.4), calls=%async_computation.1 | async-start | bytes 655360 | tf_op jit(solution)/shard_map/all_to_all | solution.py:532
  64.5 4.0 %collective-permute-start = (f32[8,256]{1,0:T(8,128)S(1)}, f32[8,256]{1,0:T(8,128)S(1)}, u32[]{:S(2)}, u32[]{:S(2)}) collective-permute-start(f32[8,256]{1,0:T(8,128)S(1)} %get-tuple-element.23.top_ref), channel_id=1, source_target_pairs={{0,96},{8,104},{16,112},{24,120},{32,64},{40,72},{48,80},{56,88},{... | collective-permute-start | bytes 24584 | tf_op jit(solution)/shard_map/ppermute | solution.py:635
  68.5 18.3 %copy-start.1 = (f32[8,256,256]{2,1,0:T(8,128)S(1)}, f32[8,256,256]{2,1,0:T(8,128)}, u32[]{:S(2)}) copy-start(f32[8,256,256]{2,1,0:T(8,128)} %inv_ref.1) | copy-start | bytes 6291460
  68.5 18.3 %copy-start.2 = (f32[8,256,256]{2,1,0:T(8,128)S(1)}, f32[8,256,256]{2,1,0:T(8,128)}, u32[]{:S(2)}) copy-start(f32[8,256,256]{2,1,0:T(8,128)} %below_ref.1) | copy-start | bytes 6291460
  111.3 5.5 %copy-start.7 = (s32[1,2176]{1,0:T(1,128)S(1)}, s32[1,2176]{1,0:T(1,128)}, u32[]{:S(2)}) copy-start(s32[1,2176]{1,0:T(1,128)} %get-tuple-element.32.key_ref) | copy-start | bytes 26116
  111.9 14.7 %all-to-all-start.4 = ((f32[128,1,256]{2,1,0:T(1,128)}), f32[128,1,256]{2,1,0:T(1,128)S(1)}, u32[]{:S(2)}, u32[]{:S(2)}) async-start(f32[128,1,256]{2,1,0:T(1,128)} %bitcast.10), calls=%async_computation.4 | async-start | bytes 262144 | tf_op jit(solution)/shard_map/all_to_all | solution.py:532
  116.7 9.9 %copy-start.3 = (f32[64,2080]{1,0:T(8,128)S(1)}, f32[64,2080]{1,0:T(8,128)}, u32[]{:S(2)}) copy-start(f32[64,2080]{1,0:T(8,128)} %now_ref.1) | copy-start | bytes 1597444
  116.7 9.9 %copy-start.4 = (f32[64,2080]{1,0:T(8,128)S(1)}, f32[64,2080]{1,0:T(8,128)}, u32[]{:S(2)}) copy-start(f32[64,2080]{1,0:T(8,128)} %before_ref.1) | copy-start | bytes 1597444
  116.7 9.9 %copy-start.5 = (f32[64,64]{1,0:T(8,128)S(1)}, f32[64,64]{1,0:T(8,128)}, u32[]{:S(2)}) copy-start(f32[64,64]{1,0:T(8,128)} %coupling_ref.1) | copy-start | bytes 49156

commit v7 on v6

--- a/solution.py
+++ b/solution.py
@@ -177,6 +177,7 @@
 
 def forward_kernel(
     home_ref,
+    half_ref,
     recv_ref,
     rows_ref,
     inv_hbm,
@@ -195,7 +196,10 @@
     tree_ref,
     sems,
 ):
-    loads = [fetch(inv_hbm, inv_ref, sems.at[0]), fetch(below_hbm, below_ref, sems.at[1])]
+    loads = []
+    for q in range(NLEAF):
+        loads.append(fetch(inv_hbm.at[q], inv_ref.at[q], sems.at[4 + q]))
+        loads.append(fetch(below_hbm.at[q], below_ref.at[q], sems.at[12 + q]))
     idx = recv_ref[pl.ds(CAP, DEV, stride=S1), :].astype(jnp.int32)
     for k in range(CAP):
         got = recv_ref[pl.ds(k, DEV, stride=S1), :].T
@@ -223,7 +227,7 @@
     own = pltpu.roll(tree_ref[:, SPAN:PAD], start % 128, 1)
     for j in range(S2):
         chunk = jnp.where(start // 128 == j, own, 0.0) - pushed[:, j * 128 : (j + 1) * 128]
-        out_ref[pl.ds(j, HALF, stride=S2), :] = crossed(chunk, home_ref[1])
+        out_ref[pl.ds(j, HALF, stride=S2), :] = crossed(chunk, half_ref[0])
     for store in stores:
         store.wait()
 
@@ -380,6 +384,7 @@
 
 def backward_kernel(
     home_ref,
+    half_ref,
     recv_ref,
     rows_ref,
     idx_ref,
@@ -402,7 +407,7 @@
     for q in range(NLEAF):
         moved[:, q * LEAF : (q + 1) * LEAF] = mark_row(rows_ref[q : q + 1, :], PATH, 0)
     for j in range(S3):
-        chunk = crossed(recv_ref[pl.ds(j, HALF, stride=S3), :], home_ref[1])
+        chunk = crossed(recv_ref[pl.ds(j, HALF, stride=S3), :], half_ref[0])
         known[:, j * 128 : (j + 1) * 128] = chunk
         parts[:, j * 128 : (j + 1) * 128] = stacked(chunk)
     picked = folded(nn(parts[...], moved[...]))
@@ -476,20 +481,20 @@
     eye = iota((64, 64), 0) == iota((64, 64), 1)
     work = jnp.concatenate([gram, jnp.where(eye, 1.0, 0.0)], axis=1)
     done = []
-    for b in range(8):
-        height = 64 - 8 * b
-        at = 8 * b
+    for b in range(4):
+        height = 64 - 16 * b
+        at = 16 * b
         columns = [
-            jnp.broadcast_to(work[:, at + c : at + c + 1], (height, 128)) for c in range(8)
+            jnp.broadcast_to(work[:, at + c : at + c + 1], (height, 128)) for c in range(16)
         ]
         below = iota((height, 128), 0)
-        for c in range(8):
+        for c in range(16):
             ratio = jnp.where(below > c, columns[c] * (1.0 / columns[c][c : c + 1, :]), 0.0)
             work = work - ratio * work[c : c + 1, :]
-            for e in range(c + 1, 8):
+            for e in range(c + 1, 16):
                 columns[e] = columns[e] - ratio * columns[e][c : c + 1, :]
-        done.append(work[0:8])
-        work = work[8:]
+        done.append(work[0:16])
+        work = work[16:]
     work = jnp.concatenate(done, axis=0)
     scale = lax.rsqrt(jnp.sum(jnp.where(eye, work[:, 0:64], 0.0), axis=1, keepdims=True))
     work = work * scale
@@ -552,7 +557,7 @@
     home_slot = jnp.zeros((), jnp.int32)
     for bit in range(LEVELS - 1):
         home_slot = home_slot + (my_group % (2 << bit) == 0).astype(jnp.int32)
-    home_at = jnp.stack([home_slot * LEAF + my_front * SHARE, my_half]).astype(jnp.int32)
+    home_at = (home_slot * LEAF + my_front * SHARE).astype(jnp.int32).reshape(1)
     half = my_half.astype(jnp.int32).reshape(1)
     V = pltpu.VMEM
     S = pltpu.SemaphoreType.DMA
@@ -590,7 +595,7 @@
     pushed, leaf_solved, tree = call(
         forward_kernel,
         [((HALF * S2, 128), F32), ((64, SPAN), F32), ((64, PAD), F32)],
-        (home_at, arrived, leaf_rows, leaf_inverse, leaf_below, link),
+        (home_at, half, arrived, leaf_rows, leaf_inverse, leaf_below, link),
         [
             V((PAD, PAD), BF16),
             V((128, PAD), BF16),
@@ -600,9 +605,9 @@
             V((NLEAF, LEAF, LEAF), F32),
             V((64, SPAN), F32),
             V((64, PAD), F32),
-            S((4,)),
+            S((20,)),
         ],
-        1,
+        2,
         far=3,
         limit=50,
         far_outs=(1, 2),
@@ -630,6 +635,7 @@
         [S((7,))],
         1,
         far=2,
+        limit=50,
     )
     across = [(i, i ^ 12) for i in range(GROUPS)]
     other_top = lax.ppermute(top, ("half", "group"), across)
@@ -640,12 +646,14 @@
         [V((7, LEAF, LEAF), F32), S((9,))],
         1,
         far=2,
+        limit=50,
         micros=2,
     )
     (paths,) = call(
         down_kernel,
         [((HALF * S3, 128), F32)],
         (top, other_top, line, links, high),
+        limit=50,
     )
     paths = exchange(paths, S3, NEAR)
     (returning,) = call(
@@ -653,6 +661,7 @@
         [((DEV * S4, 128), F32)],
         (
             home_at,
+            half,
             paths,
             leaf_rows,
             idx,
@@ -672,7 +681,7 @@
             V((256, PAD), BF16),
             S((2,)),
         ],
-        1,
+        2,
         far=2,
         limit=46,
     )

time: 132 us -> 128 us (0.970)
  Pallas kernels: 45.3 us -> 41.3 us
    pallas_call x11, Pallas kernels: 45.3 us -> 41.3 us  [call(): pl.pallas_call(kernel, out_shape=[jax.ShapeDtypeStruct(shape, dtype) for...]
  transfers between devices with their start and end apart: 4 -> 4, of which waited for: 4 -> 4; matrix products, arithmetic and copies ran while one was open for 0% -> 0% of each run, Pallas kernels for 12% -> 13%
where the time goes in v7:
time: 128 us; the launch traced here: 127 us
  Pallas kernels  41.3 us (32%)
  blocking collectives  35.1 us (27%)
  waiting for transfers between devices  27.9 us (22%)
  starting transfers between devices  22.1 us (17%)
    pallas_call x11, Pallas kernels, call(): pl.pallas_call(kernel, out_shape=[jax.ShapeDtypeStruct(shape, dtype) for...  41.3 us
    all_to_all x2, blocking collectives, exchange(): lax.all_to_all(x.reshape(peers, 1, lines * 128), axes, split_axis=0, conc...  35.1 us
    all_to_all x3, waiting for transfers between devices, exchange(): lax.all_to_all(x.reshape(peers, 1, lines * 128), axes, split_axis=0, conc...  26.6 us
    all_to_all x3, starting transfers between devices, exchange(): lax.all_to_all(x.reshape(peers, 1, lines * 128), axes, split_axis=0, conc...  21.5 us
  transfers between devices with their start and end apart: 4, of which 4 were waited for; matrix products, arithmetic and copies ran while one was open for 0% of the time, Pallas kernels for 13%

profile of v7, /device:TPU:1, one launch (start us, length us, event | category | flops | bytes accessed | tf_op | source)
XLA Modules:
  0.0 127.2 jit_solution(2548310104813721489)
XLA Ops:
  0.6 6.1 %shard_map.112 = (f32[2304,128]{1,0:T(8,128)}, s32[1,2176]{1,0:T(1,128)}) custom-call(s32[2080]{0:T(1024)} %vt_ref.1, f32[64,2080]{1,0:T(8,128)} %now_ref.1, f32[64,2080]{1,0:T(8,128)} %before_ref.1), custom_call_target="tpu_custom_call" | custom-call | flops 4000000000 | bytes 12000000 | tf_op jit(solution)/shard_map/pallas_call | solution.py:519
  6.7 11.5 %all-to-all-start = ((f32[128,1,2304]{2,1,0:T(1,128)}), f32[128,1,2304]{2,1,0:T(1,128)S(1)}, u32[]{:S(2)}, u32[]{:S(2)}) async-start(f32[128,1,2304]{2,1,0:T(1,128)} %bitcast.21), calls=%async_computation | async-start | bytes 2359296 | tf_op jit(solution)/shard_map/all_to_all | solution.py:537
  18.3 0.0 copy-start.6
  18.3 8.2 %shard_map.113 = (f32[16,256,256]{2,1,0:T(8,128)}, f32[15,256,256]{2,1,0:T(8,128)}) custom-call(f32[16,256,256]{2,1,0:T(8,128)} %inv_hbm.2, f32[15,256,256]{2,1,0:T(8,128)} %parent_hbm.1), custom_call_target="tpu_custom_call" | custom-call | flops 4000000000 | bytes 12000000 | tf_op jit(solution)/shard_map/pallas_call | solution.py:519
  26.5 12.2 %all-to-all-done = f32[128,1,2304]{2,1,0:T(1,128)S(1)} async-done(((f32[128,1,2304]{2,1,0:T(1,128)}), f32[128,1,2304]{2,1,0:T(1,128)S(1)}, u32[]{:S(2)}, u32[]{:S(2)}) %all-to-all-start) | async-done | bytes 1179680 | tf_op jit(solution)/shard_map/all_to_all | solution.py:537
  38.7 0.0 copy-done.6
  38.7 6.5 %shard_map.114 = (f32[640,128]{1,0:T(8,128)}, f32[64,2048]{1,0:T(8,128)S(1)}, f32[64,2176]{1,0:T(8,128)S(1)}) custom-call(s32[1]{0:T(128)} %bitcast.home_ref, s32[1]{0:T(128)} %bitcast.1.half_ref, f32[2304,128]{1,0:T(8,128)S(1)} %bitcast.12, s32[8,256]{1,0:T(8,128)S(1)} %copy-done.6, f32[8,256,256]{2,1,0:T(8,128)} %inv_ref.1, f32[8,256,256]{2,1,0:T(8,128)} %below_ref.1, ...), custom_call_target="tpu_custom_call" | custom-call | flops 4000000000 | bytes 12000000 | tf_op jit(solution)/shard_map/pallas_call | solution.py:519
  45.2 0.0 copy-done
  45.2 5.2 %all-to-all-start.1 = ((f32[64,1,1280]{2,1,0:T(1,128)}), f32[64,1,1280]{2,1,0:T(1,128)S(1)}, u32[]{:S(2)}, u32[]{:S(2)}) async-start(f32[64,1,1280]{2,1,0:T(1,128)} %bitcast.4), calls=%async_computation.1 | async-start | bytes 655360 | tf_op jit(solution)/shard_map/all_to_all | solution.py:537
  50.4 4.3 %shard_map.115 = (bf16[256,2176]{1,0:T(8,128)(2,1)S(1)}, f32[128,128]{1,0:T(8,128)S(1)}, f32[128,128]{1,0:T(8,128)S(1)}) custom-call(f32[2304,128]{1,0:T(8,128)} %bitcast.13, f32[64,2176]{1,0:T(8,128)S(1)} %get-tuple-element.21.tree_hbm), custom_call_target="tpu_custom_call" | custom-call | flops 4000000000 | bytes 12000000 | tf_op jit(solution)/shard_map/pallas_call | solution.py:519
  54.7 6.2 %all-to-all-done.1 = f32[64,1,1280]{2,1,0:T(1,128)S(1)} async-done(((f32[64,1,1280]{2,1,0:T(1,128)}), f32[64,1,1280]{2,1,0:T(1,128)S(1)}, u32[]{:S(2)}, u32[]{:S(2)}) %all-to-all-start.1) | async-done | bytes 327712 | tf_op jit(solution)/shard_map/all_to_all | solution.py:537
  60.9 2.0 %shard_map.116 = (f32[8,256]{1,0:T(8,128)S(1)}, f32[8,256]{1,0:T(8,128)S(1)}, f32[7,256,256]{2,1,0:T(8,128)S(1)}) custom-call(s32[1]{0:T(128)} %bitcast.1.half_ref, f32[640,128]{1,0:T(8,128)S(1)} %bitcast.17, f32[15,256,256]{2,1,0:T(8,128)} %get-tuple-element.19.ready_hbm.link_hbm, bf16[256,2176]{1,0:T(8,128)(2,1)S(1)} %get-tuple-element.22.ready_hbm.other_hbm), custom_call_target="tpu_custom_call" | custom-call | flops 4000000000 | bytes 12000000 | tf_op jit(solution)/shard_map/pallas_call | solution.py:519
  62.9 0.6 collective-permute-start
  63.5 2.1 %shard_map.117 = (f32[8,256]{1,0:T(8,128)S(1)}, f32[3,256,256]{2,1,0:T(8,128)S(1)}) custom-call(s32[1]{0:T(128)} %bitcast.1.half_ref, f32[8,256]{1,0:T(8,128)S(1)} %get-tuple-element.24.source_ref, f32[16,256,256]{2,1,0:T(8,128)} %get-tuple-element.25.square_hbm, f32[15,256,256]{2,1,0:T(8,128)} %get-tuple-element.19.ready_hbm.link_hbm), custom_call_target="tpu_custom_call" | custom-call | flops 2000000000 | bytes 6000000 | tf_op jit(solution)/shard_map/pallas_call | solution.py:519
  65.6 1.3 collective-permute-done.other_ref
  66.9 1.1 shard_map.118
  68.0 15.6 %all_to_all.25 = f32[64,1,1280]{2,1,0:T(1,128)S(1)} all-to-all(f32[64,1,1280]{2,1,0:T(1,128)S(1)} %bitcast.19), channel_id=1, replica_groups=mesh['half'=2,'group'=8,'front'=8] {'group','front'}, dimensions={0} | all-to-all | bytes 655360 | tf_op jit(solution)/shard_map/all_to_all | solution.py:537
  83.6 0.0 copy-done.1
  83.6 0.0 copy-done.2
  83.6 4.5 %shard_map.119 = f32[1280,128]{1,0:T(8,128)S(1)} custom-call(s32[1]{0:T(128)} %bitcast.home_ref, s32[1]{0:T(128)} %bitcast.1.half_ref, f32[640,128]{1,0:T(8,128)S(1)} %bitcast.18, s32[8,256]{1,0:T(8,128)S(1)} %copy-done.6, f32[128,128]{1,0:T(8,128)S(1)} %get-tuple-element.29.idx_ref, f32[128,128]{1,0:T(8,128)S(1)} %get-tuple-element.30.gram_ref, ...), custom_call_target="tpu_custom_call" | custom-call | flops 4000000000 | bytes 12000000 | tf_op jit(solution)/shard_map/pallas_call | solution.py:519
  88.1 19.4 %all_to_all.26 = f32[128,1,1280]{2,1,0:T(1,128)S(1)} all-to-all(f32[128,1,1280]{2,1,0:T(1,128)S(1)} %bitcast.16), channel_id=1, replica_groups=mesh['half'=2,'group'=8,'front'=8] {'half','group','front'}, dimensions={0} | all-to-all | bytes 1310720 | tf_op jit(solution)/shard_map/all_to_all | solution.py:537
  107.6 0.7 shard_map.120
  108.3 4.8 %all-to-all-start.4 = ((f32[128,1,256]{2,1,0:T(1,128)}), f32[128,1,256]{2,1,0:T(1,128)S(1)}, u32[]{:S(2)}, u32[]{:S(2)}) async-start(f32[128,1,256]{2,1,0:T(1,128)} %bitcast.10), calls=%async_computation.4 | async-start | bytes 262144 | tf_op jit(solution)/shard_map/all_to_all | solution.py:537
  113.0 0.0 copy-done.7
  113.0 0.0 copy-start.3
  113.0 0.0 copy-start.4
  113.1 0.0 copy-start.5
  113.1 1.7 %shard_map.121.solved_ref = f32[64,2080]{1,0:T(8,128)S(1)} custom-call(s32[1,2176]{1,0:T(1,128)S(1)} %copy-done.7, f32[1280,128]{1,0:T(8,128)S(1)} %bitcast.15), custom_call_target="tpu_custom_call" | custom-call | flops 4000000000 | bytes 12000000 | tf_op jit(solution)/shard_map/pallas_call | solution.py:519
  114.8 8.2 %all-to-all-done.4 = f32[128,1,256]{2,1,0:T(1,128)S(1)} async-done(((f32[128,1,256]{2,1,0:T(1,128)}), f32[128,1,256]{2,1,0:T(1,128)S(1)}, u32[]{:S(2)}, u32[]{:S(2)}) %all-to-all-start.4) | async-done | bytes 131104 | tf_op jit(solution)/shard_map/all_to_all | solution.py:537
  123.0 0.0 copy-done.3
  123.0 0.0 copy-done.5
  123.0 4.2 %shard_map.122 = (f32[64,64]{1,0:T(8,128)}, f32[64,64]{1,0:T(8,128)}, f32[64,2080]{1,0:T(8,128)}) custom-call(f32[256,128]{1,0:T(8,128)S(1)} %bitcast.20, f32[64,2080]{1,0:T(8,128)S(1)} %shard_map.121.solved_ref, f32[64,2080]{1,0:T(8,128)S(1)} %copy-done.3, f32[64,2080]{1,0:T(8,128)S(1)} %copy-done.4, f32[64,64]{1,0:T(8,128)S(1)} %copy-done.5), custom_call_target="tpu_custom_call" | custom-call | flops 4000000000 | bytes 12000000 | tf_op jit(solution)/shard_map/pallas_call | solution.py:519
  (5 shorter events, 0.0 us)
Async XLA Ops:
  6.7 32.0 %all-to-all-start = ((f32[128,1,2304]{2,1,0:T(1,128)}), f32[128,1,2304]{2,1,0:T(1,128)S(1)}, u32[]{:S(2)}, u32[]{:S(2)}) async-start(f32[128,1,2304]{2,1,0:T(1,128)} %bitcast.21), calls=%async_computation | async-start | bytes 2359296 | tf_op jit(solution)/shard_map/all_to_all | solution.py:537
  18.3 20.4 %copy-start.6 = (s32[8,256]{1,0:T(8,128)S(1)}, s32[8,256]{1,0:T(8,128)}, u32[]{:S(2)}) copy-start(s32[8,256]{1,0:T(8,128)} %rows_ref.3) | copy-start | bytes 24580
  38.7 6.5 %copy-start = (f32[128,1,2304]{2,1,0:T(1,128)}, f32[128,1,2304]{2,1,0:T(1,128)S(1)}, u32[]{:S(2)}) copy-start(f32[128,1,2304]{2,1,0:T(1,128)S(1)} %all-to-all-done) | copy-start | bytes 3538948
  45.2 15.7 %all-to-all-start.1 = ((f32[64,1,1280]{2,1,0:T(1,128)}), f32[64,1,1280]{2,1,0:T(1,128)S(1)}, u32[]{:S(2)}, u32[]{:S(2)}) async-start(f32[64,1,1280]{2,1,0:T(1,128)} %bitcast.4), calls=%async_computation.1 | async-start | bytes 655360 | tf_op jit(solution)/shard_map/all_to_all | solution.py:537
  62.9 4.0 %collective-permute-start = (f32[8,256]{1,0:T(8,128)S(1)}, f32[8,256]{1,0:T(8,128)S(1)}, u32[]{:S(2)}, u32[]{:S(2)}) collective-permute-start(f32[8,256]{1,0:T(8,128)S(1)} %get-tuple-element.23.top_ref), channel_id=1, source_target_pairs={{0,96},{8,104},{16,112},{24,120},{32,64},{40,72},{48,80},{56,88},{... | collective-permute-start | bytes 24584 | tf_op jit(solution)/shard_map/ppermute | solution.py:641
  66.9 16.8 %copy-start.1 = (f32[8,256,256]{2,1,0:T(8,128)S(1)}, f32[8,256,256]{2,1,0:T(8,128)}, u32[]{:S(2)}) copy-start(f32[8,256,256]{2,1,0:T(8,128)} %inv_ref.1) | copy-start | bytes 6291460
  66.9 16.8 %copy-start.2 = (f32[8,256,256]{2,1,0:T(8,128)S(1)}, f32[8,256,256]{2,1,0:T(8,128)}, u32[]{:S(2)}) copy-start(f32[8,256,256]{2,1,0:T(8,128)} %below_ref.1) | copy-start | bytes 6291460
  107.6 5.5 %copy-start.7 = (s32[1,2176]{1,0:T(1,128)S(1)}, s32[1,2176]{1,0:T(1,128)}, u32[]{:S(2)}) copy-start(s32[1,2176]{1,0:T(1,128)} %get-tuple-element.32.key_ref) | copy-start | bytes 26116
  108.3 14.7 %all-to-all-start.4 = ((f32[128,1,256]{2,1,0:T(1,128)}), f32[128,1,256]{2,1,0:T(1,128)S(1)}, u32[]{:S(2)}, u32[]{:S(2)}) async-start(f32[128,1,256]{2,1,0:T(1,128)} %bitcast.10), calls=%async_computation.4 | async-start | bytes 262144 | tf_op jit(solution)/shard_map/all_to_all | solution.py:537
  113.0 9.9 %copy-start.3 = (f32[64,2080]{1,0:T(8,128)S(1)}, f32[64,2080]{1,0:T(8,128)}, u32[]{:S(2)}) copy-start(f32[64,2080]{1,0:T(8,128)} %now_ref.1) | copy-start | bytes 1597444
  113.0 9.9 %copy-start.4 = (f32[64,2080]{1,0:T(8,128)S(1)}, f32[64,2080]{1,0:T(8,128)}, u32[]{:S(2)}) copy-start(f32[64,2080]{1,0:T(8,128)} %before_ref.1) | copy-start | bytes 1597444
  113.1 9.9 %copy-start.5 = (f32[64,64]{1,0:T(8,128)S(1)}, f32[64,64]{1,0:T(8,128)}, u32[]{:S(2)}) copy-start(f32[64,64]{1,0:T(8,128)} %coupling_ref.1) | copy-start | bytes 49156

commit v8 on v7

--- a/solution.py
+++ b/solution.py
@@ -28,7 +28,8 @@
 S1 = 18
 S2 = 10
 S3 = 10
-S4 = 10
+S4 = 12
+S5 = 3
 MIB = 1024 * 1024
 
 
@@ -140,6 +141,21 @@
         carry = carry + counts[:, 128:256]
     rank = jnp.concatenate(ranks, axis=1).astype(jnp.int32)
     key = jnp.where(target < 0, -1, rank * DEV + bucket)
+    ranked = jnp.broadcast_to(rank, (32, PAD)) == iota((32, PAD), 0)
+    high = place // 64
+    marks = jnp.concatenate(
+        [
+            jnp.where(ranked, jnp.broadcast_to(high, (32, PAD)).astype(F32), 0.0),
+            jnp.where(ranked, jnp.broadcast_to(place - high * 64, (32, PAD)).astype(F32), 0.0),
+            jnp.zeros((64, PAD), F32),
+        ],
+        axis=0,
+    ).astype(BF16)
+    found = nt(member[...], marks)
+    where = found * 64.0 + pltpu.roll(found, 96, 1)
+    lane = iota((DEV, 128), 1)
+    filled = (lane.astype(F32) < carry) & (lane < CAP)
+    out_ref[pl.ds(CAP, DEV, stride=S1), :] = jnp.where(filled, where, -1.0)
     for k in range(8):
         mark[k * DEV : (k + 1) * DEV, :] = mark_row(key, DEV, k * DEV)
     for load in loads:
@@ -158,21 +174,6 @@
     block = block[:, 0:128] + block[:, 128:256]
     for k in range(CAP):
         out_ref[pl.ds(k, DEV, stride=S1), :] = block[k * DEV : (k + 1) * DEV]
-    ranked = jnp.broadcast_to(rank, (32, PAD)) == iota((32, PAD), 0)
-    high = place // 64
-    marks = jnp.concatenate(
-        [
-            jnp.where(ranked, jnp.broadcast_to(high, (32, PAD)).astype(F32), 0.0),
-            jnp.where(ranked, jnp.broadcast_to(place - high * 64, (32, PAD)).astype(F32), 0.0),
-            jnp.zeros((64, PAD), F32),
-        ],
-        axis=0,
-    ).astype(BF16)
-    found = nt(member[...], marks)
-    where = found * 64.0 + pltpu.roll(found, 96, 1)
-    lane = iota((DEV, 128), 1)
-    filled = (lane.astype(F32) < carry) & (lane < CAP)
-    out_ref[pl.ds(CAP, DEV, stride=S1), :] = jnp.where(filled, where, -1.0)
 
 
 def forward_kernel(
@@ -437,16 +438,17 @@
         out_ref[pl.ds(j, DEV, stride=S4), :] = jnp.concatenate(pair, axis=0).T
     last = packed[:, 16 * DEV : 17 * DEV]
     last = jnp.concatenate([last, last], axis=0).T
-    late = jnp.concatenate([square, gram_ref[64:128, :]], axis=0)
-    out_ref[pl.ds(8, DEV, stride=S4), :] = jnp.where(iota((DEV, 128), 1) < 64, last, late)
-    out_ref[pl.ds(9, DEV, stride=S4), :] = jnp.concatenate([cross, gram_ref[0:64, :]], axis=0)
+    low = iota((DEV, 128), 1) < 64
+    out_ref[pl.ds(8, DEV, stride=S4), :] = jnp.where(low, last, 0.0)
+    late = jnp.where(low[0:64], square, gram_ref[64:128, :])
+    for i, block in enumerate((cross, gram_ref[0:64, :], late)):
+        out_ref[pl.ds(9 + i, DEV, stride=S4), :] = jnp.concatenate([block, block], axis=0)
 
 
 def total_kernel(recv_ref, out_ref):
-    first = jnp.sum(recv_ref[pl.ds(9, DEV, stride=S4), :], axis=0, keepdims=True)
-    second = jnp.sum(recv_ref[pl.ds(8, DEV, stride=S4), :], axis=0, keepdims=True)
-    out_ref[pl.ds(0, DEV, stride=2), :] = jnp.broadcast_to(first, (DEV, 128))
-    out_ref[pl.ds(1, DEV, stride=2), :] = jnp.broadcast_to(second, (DEV, 128))
+    for i in range(S5):
+        line = jnp.sum(recv_ref[pl.ds(9 + i, DEV, stride=S4), :], axis=0, keepdims=True)
+        out_ref[pl.ds(i, HALF, stride=S5), :] = jnp.broadcast_to(line, (HALF, 128))
 
 
 def unpack_kernel(key_ref, recv_ref, out_ref, mark, value):
@@ -463,15 +465,11 @@
 def finish_kernel(
     recv_ref, solved_ref, now_ref, before_ref, coupling_ref, proj_ref, factor_ref, next_ref, value
 ):
-    first = recv_ref[pl.ds(0, DEV, stride=2), :]
-    second = recv_ref[pl.ds(1, DEV, stride=2), :]
     count = 1.0 / (ROWS * DEV)
-    s_b = first[0:64, 0:64] * count
-    s_a = first[0:64, 64:128] * count
-    b_b = first[64:128, 0:64] * count
-    b_a = first[64:128, 64:128] * count
-    s_s = second[0:64, 64:128] * count
-    a_a = second[64:128, 64:128] * count
+    cross, own, late = [recv_ref[pl.ds(i, HALF, stride=S5), :] * count for i in range(S5)]
+    s_b, s_a = cross[:, 0:64], cross[:, 64:128]
+    b_b, b_a = own[:, 0:64], own[:, 64:128]
+    s_s, a_a = late[:, 0:64], late[:, 64:128]
     coupling = coupling_ref[...]
     proj_ref[...] = s_b.T
     line_s = s_s - nt32(s_b, s_b) - nt32(coupling, s_a)
@@ -686,8 +684,8 @@
         limit=46,
     )
     returned = exchange(returning, S4)
-    (sums,) = call(total_kernel, [((DEV * 2, 128), F32)], (returned,), micros=1)
-    sums = exchange(sums, 2)
+    (sums,) = call(total_kernel, [((HALF * S5, 128), F32)], (returned,), micros=1)
+    sums = exchange(sums, S5, NEAR)
     (solved,) = call(
         unpack_kernel,
         [((64, ROWS), F32)],

time: 128 us -> 128 us (level)
  waiting for transfers between devices: 27.9 us -> 26.3 us
  blocking collectives: 35.1 us -> 36.6 us
    all_to_all x3, waiting for transfers between devices: 26.6 us -> 25 us  [exchange(): lax.all_to_all(x.reshape(peers, 1, lines * 128), axes, split_axis=0, conc...]
    all_to_all x2, blocking collectives: 35.1 us -> 36.6 us  [exchange(): lax.all_to_all(x.reshape(peers, 1, lines * 128), axes, split_axis=0, conc...]
where the time goes in v8:
time: 128 us; the launch traced here: 127 us
  Pallas kernels  40.9 us (32%)
  blocking collectives  36.6 us (29%)
  waiting for transfers between devices  26.3 us (21%)
  starting transfers between devices  22.5 us (18%)
    pallas_call x11, Pallas kernels, call(): pl.pallas_call(kernel, out_shape=[jax.ShapeDtypeStruct(shape, dtype) for...  40.9 us
    all_to_all x2, blocking collectives, exchange(): lax.all_to_all(x.reshape(peers, 1, lines * 128), axes, split_axis=0, conc...  36.6 us
    all_to_all x3, waiting for transfers between devices, exchange(): lax.all_to_all(x.reshape(peers, 1, lines * 128), axes, split_axis=0, conc...  25 us
    all_to_all x3, starting transfers between devices, exchange(): lax.all_to_all(x.reshape(peers, 1, lines * 128), axes, split_axis=0, conc...  21.9 us
  transfers between devices with their start and end apart: 4, of which 4 were waited for; matrix products, arithmetic and copies ran while one was open for 0% of the time, Pallas kernels for 13%

profile of v8, /device:TPU:1, one launch (start us, length us, event | category | flops | bytes accessed | tf_op | source)
XLA Modules:
  0.0 127.1 jit_solution(7567150938727557492)
XLA Ops:
  0.6 6.1 %shard_map.112 = (f32[2304,128]{1,0:T(8,128)}, s32[1,2176]{1,0:T(1,128)}) custom-call(s32[2080]{0:T(1024)} %vt_ref.1, f32[64,2080]{1,0:T(8,128)} %now_ref.1, f32[64,2080]{1,0:T(8,128)} %before_ref.1), custom_call_target="tpu_custom_call" | custom-call | flops 4000000000 | bytes 12000000 | tf_op jit(solution)/shard_map/pallas_call | solution.py:517
  6.7 11.5 %all-to-all-start = ((f32[128,1,2304]{2,1,0:T(1,128)}), f32[128,1,2304]{2,1,0:T(1,128)S(1)}, u32[]{:S(2)}, u32[]{:S(2)}) async-start(f32[128,1,2304]{2,1,0:T(1,128)} %bitcast.21), calls=%async_computation | async-start | bytes 2359296 | tf_op jit(solution)/shard_map/all_to_all | solution.py:535
  18.3 0.0 copy-start.6
  18.3 8.2 %shard_map.113 = (f32[16,256,256]{2,1,0:T(8,128)}, f32[15,256,256]{2,1,0:T(8,128)}) custom-call(f32[16,256,256]{2,1,0:T(8,128)} %inv_hbm.2, f32[15,256,256]{2,1,0:T(8,128)} %parent_hbm.1), custom_call_target="tpu_custom_call" | custom-call | flops 4000000000 | bytes 12000000 | tf_op jit(solution)/shard_map/pallas_call | solution.py:517
  26.5 12.2 %all-to-all-done = f32[128,1,2304]{2,1,0:T(1,128)S(1)} async-done(((f32[128,1,2304]{2,1,0:T(1,128)}), f32[128,1,2304]{2,1,0:T(1,128)S(1)}, u32[]{:S(2)}, u32[]{:S(2)}) %all-to-all-start) | async-done | bytes 1179680 | tf_op jit(solution)/shard_map/all_to_all | solution.py:535
  38.7 0.0 copy-done.6
  38.7 6.5 %shard_map.114 = (f32[640,128]{1,0:T(8,128)}, f32[64,2048]{1,0:T(8,128)S(1)}, f32[64,2176]{1,0:T(8,128)S(1)}) custom-call(s32[1]{0:T(128)} %bitcast.home_ref, s32[1]{0:T(128)} %bitcast.1.half_ref, f32[2304,128]{1,0:T(8,128)S(1)} %bitcast.12, s32[8,256]{1,0:T(8,128)S(1)} %copy-done.6, f32[8,256,256]{2,1,0:T(8,128)} %inv_ref.1, f32[8,256,256]{2,1,0:T(8,128)} %below_ref.1, ...), custom_call_target="tpu_custom_call" | custom-call | flops 4000000000 | bytes 12000000 | tf_op jit(solution)/shard_map/pallas_call | solution.py:517
  45.2 0.0 copy-done
  45.2 5.2 %all-to-all-start.1 = ((f32[64,1,1280]{2,1,0:T(1,128)}), f32[64,1,1280]{2,1,0:T(1,128)S(1)}, u32[]{:S(2)}, u32[]{:S(2)}) async-start(f32[64,1,1280]{2,1,0:T(1,128)} %bitcast.4), calls=%async_computation.1 | async-start | bytes 655360 | tf_op jit(solution)/shard_map/all_to_all | solution.py:535
  50.4 4.3 %shard_map.115 = (bf16[256,2176]{1,0:T(8,128)(2,1)S(1)}, f32[128,128]{1,0:T(8,128)S(1)}, f32[128,128]{1,0:T(8,128)S(1)}) custom-call(f32[2304,128]{1,0:T(8,128)} %bitcast.13, f32[64,2176]{1,0:T(8,128)S(1)} %get-tuple-element.21.tree_hbm), custom_call_target="tpu_custom_call" | custom-call | flops 4000000000 | bytes 12000000 | tf_op jit(solution)/shard_map/pallas_call | solution.py:517
  54.7 6.2 %all-to-all-done.1 = f32[64,1,1280]{2,1,0:T(1,128)S(1)} async-done(((f32[64,1,1280]{2,1,0:T(1,128)}), f32[64,1,1280]{2,1,0:T(1,128)S(1)}, u32[]{:S(2)}, u32[]{:S(2)}) %all-to-all-start.1) | async-done | bytes 327712 | tf_op jit(solution)/shard_map/all_to_all | solution.py:535
  60.9 2.0 %shard_map.116 = (f32[8,256]{1,0:T(8,128)S(1)}, f32[8,256]{1,0:T(8,128)S(1)}, f32[7,256,256]{2,1,0:T(8,128)S(1)}) custom-call(s32[1]{0:T(128)} %bitcast.1.half_ref, f32[640,128]{1,0:T(8,128)S(1)} %bitcast.17, f32[15,256,256]{2,1,0:T(8,128)} %get-tuple-element.19.ready_hbm.link_hbm, bf16[256,2176]{1,0:T(8,128)(2,1)S(1)} %get-tuple-element.22.ready_hbm.other_hbm), custom_call_target="tpu_custom_call" | custom-call | flops 4000000000 | bytes 12000000 | tf_op jit(solution)/shard_map/pallas_call | solution.py:517
  62.9 0.7 collective-permute-start
  63.5 2.1 %shard_map.117 = (f32[8,256]{1,0:T(8,128)S(1)}, f32[3,256,256]{2,1,0:T(8,128)S(1)}) custom-call(s32[1]{0:T(128)} %bitcast.1.half_ref, f32[8,256]{1,0:T(8,128)S(1)} %get-tuple-element.24.source_ref, f32[16,256,256]{2,1,0:T(8,128)} %get-tuple-element.25.square_hbm, f32[15,256,256]{2,1,0:T(8,128)} %get-tuple-element.19.ready_hbm.link_hbm), custom_call_target="tpu_custom_call" | custom-call | flops 2000000000 | bytes 6000000 | tf_op jit(solution)/shard_map/pallas_call | solution.py:517
  65.6 1.3 collective-permute-done.other_ref
  66.9 1.1 shard_map.118
  68.0 15.6 %all_to_all.25 = f32[64,1,1280]{2,1,0:T(1,128)S(1)} all-to-all(f32[64,1,1280]{2,1,0:T(1,128)S(1)} %bitcast.19), channel_id=1, replica_groups=mesh['half'=2,'group'=8,'front'=8] {'group','front'}, dimensions={0} | all-to-all | bytes 655360 | tf_op jit(solution)/shard_map/all_to_all | solution.py:535
  83.6 0.0 copy-done.1
  83.6 0.0 copy-done.2
  83.6 4.5 %shard_map.119 = f32[1536,128]{1,0:T(8,128)S(1)} custom-call(s32[1]{0:T(128)} %bitcast.home_ref, s32[1]{0:T(128)} %bitcast.1.half_ref, f32[640,128]{1,0:T(8,128)S(1)} %bitcast.18, s32[8,256]{1,0:T(8,128)S(1)} %copy-done.6, f32[128,128]{1,0:T(8,128)S(1)} %get-tuple-element.29.idx_ref, f32[128,128]{1,0:T(8,128)S(1)} %get-tuple-element.30.gram_ref, ...), custom_call_target="tpu_custom_call" | custom-call | flops 4000000000 | bytes 12000000 | tf_op jit(solution)/shard_map/pallas_call | solution.py:517
  88.1 20.9 %all_to_all.26 = f32[128,1,1536]{2,1,0:T(1,128)S(1)} all-to-all(f32[128,1,1536]{2,1,0:T(1,128)S(1)} %bitcast.16), channel_id=1, replica_groups=mesh['half'=2,'group'=8,'front'=8] {'half','group','front'}, dimensions={0} | all-to-all | bytes 1572864 | tf_op jit(solution)/shard_map/all_to_all | solution.py:535
  109.1 0.7 shard_map.120
  109.7 5.1 %all-to-all-start.4 = ((f32[64,1,384]{2,1,0:T(1,128)}), f32[64,1,384]{2,1,0:T(1,128)S(1)}, u32[]{:S(2)}, u32[]{:S(2)}) async-start(f32[64,1,384]{2,1,0:T(1,128)} %bitcast.10), calls=%async_computation.4 | async-start | bytes 196608 | tf_op jit(solution)/shard_map/all_to_all | solution.py:535
  114.9 0.0 copy-done.7
  114.9 0.0 copy-start.3
  114.9 0.0 copy-start.4
  114.9 0.0 copy-start.5
  114.9 1.7 %shard_map.121.solved_ref = f32[64,2080]{1,0:T(8,128)S(1)} custom-call(s32[1,2176]{1,0:T(1,128)S(1)} %copy-done.7, f32[1536,128]{1,0:T(8,128)S(1)} %bitcast.15), custom_call_target="tpu_custom_call" | custom-call | flops 4000000000 | bytes 12000000 | tf_op jit(solution)/shard_map/pallas_call | solution.py:517
  116.6 6.6 %all-to-all-done.4 = f32[64,1,384]{2,1,0:T(1,128)S(1)} async-done(((f32[64,1,384]{2,1,0:T(1,128)}), f32[64,1,384]{2,1,0:T(1,128)S(1)}, u32[]{:S(2)}, u32[]{:S(2)}) %all-to-all-start.4) | async-done | bytes 98336 | tf_op jit(solution)/shard_map/all_to_all | solution.py:535
  123.2 0.0 copy-done.3
  123.2 0.0 copy-done.4
  123.2 3.9 %shard_map.122 = (f32[64,64]{1,0:T(8,128)}, f32[64,64]{1,0:T(8,128)}, f32[64,2080]{1,0:T(8,128)}) custom-call(f32[192,128]{1,0:T(8,128)S(1)} %bitcast.20, f32[64,2080]{1,0:T(8,128)S(1)} %shard_map.121.solved_ref, f32[64,2080]{1,0:T(8,128)S(1)} %copy-done.3, f32[64,2080]{1,0:T(8,128)S(1)} %copy-done.4, f32[64,64]{1,0:T(8,128)S(1)} %copy-done.5), custom_call_target="tpu_custom_call" | custom-call | flops 4000000000 | bytes 12000000 | tf_op jit(solution)/shard_map/pallas_call | solution.py:517
  (5 shorter events, 0.0 us)
Async XLA Ops:
  6.7 32.0 %all-to-all-start = ((f32[128,1,2304]{2,1,0:T(1,128)}), f32[128,1,2304]{2,1,0:T(1,128)S(1)}, u32[]{:S(2)}, u32[]{:S(2)}) async-start(f32[128,1,2304]{2,1,0:T(1,128)} %bitcast.21), calls=%async_computation | async-start | bytes 2359296 | tf_op jit(solution)/shard_map/all_to_all | solution.py:535
  18.3 20.4 %copy-start.6 = (s32[8,256]{1,0:T(8,128)S(1)}, s32[8,256]{1,0:T(8,128)}, u32[]{:S(2)}) copy-start(s32[8,256]{1,0:T(8,128)} %rows_ref.3) | copy-start | bytes 24580
  38.7 6.5 %copy-start = (f32[128,1,2304]{2,1,0:T(1,128)}, f32[128,1,2304]{2,1,0:T(1,128)S(1)}, u32[]{:S(2)}) copy-start(f32[128,1,2304]{2,1,0:T(1,128)S(1)} %all-to-all-done) | copy-start | bytes 3538948
  45.2 15.7 %all-to-all-start.1 = ((f32[64,1,1280]{2,1,0:T(1,128)}), f32[64,1,1280]{2,1,0:T(1,128)S(1)}, u32[]{:S(2)}, u32[]{:S(2)}) async-start(f32[64,1,1280]{2,1,0:T(1,128)} %bitcast.4), calls=%async_computation.1 | async-start | bytes 655360 | tf_op jit(solution)/shard_map/all_to_all | solution.py:535
  62.9 4.0 %collective-permute-start = (f32[8,256]{1,0:T(8,128)S(1)}, f32[8,256]{1,0:T(8,128)S(1)}, u32[]{:S(2)}, u32[]{:S(2)}) collective-permute-start(f32[8,256]{1,0:T(8,128)S(1)} %get-tuple-element.23.top_ref), channel_id=1, source_target_pairs={{0,96},{8,104},{16,112},{24,120},{32,64},{40,72},{48,80},{56,88},{... | collective-permute-start | bytes 24584 | tf_op jit(solution)/shard_map/ppermute | solution.py:639
  66.9 16.8 %copy-start.1 = (f32[8,256,256]{2,1,0:T(8,128)S(1)}, f32[8,256,256]{2,1,0:T(8,128)}, u32[]{:S(2)}) copy-start(f32[8,256,256]{2,1,0:T(8,128)} %inv_ref.1) | copy-start | bytes 6291460
  66.9 16.8 %copy-start.2 = (f32[8,256,256]{2,1,0:T(8,128)S(1)}, f32[8,256,256]{2,1,0:T(8,128)}, u32[]{:S(2)}) copy-start(f32[8,256,256]{2,1,0:T(8,128)} %below_ref.1) | copy-start | bytes 6291460
  109.1 5.8 %copy-start.7 = (s32[1,2176]{1,0:T(1,128)S(1)}, s32[1,2176]{1,0:T(1,128)}, u32[]{:S(2)}) copy-start(s32[1,2176]{1,0:T(1,128)} %get-tuple-element.32.key_ref) | copy-start | bytes 26116
  109.7 13.5 %all-to-all-start.4 = ((f32[64,1,384]{2,1,0:T(1,128)}), f32[64,1,384]{2,1,0:T(1,128)S(1)}, u32[]{:S(2)}, u32[]{:S(2)}) async-start(f32[64,1,384]{2,1,0:T(1,128)} %bitcast.10), calls=%async_computation.4 | async-start | bytes 196608 | tf_op jit(solution)/shard_map/all_to_all | solution.py:535
  114.9 8.3 %copy-start.3 = (f32[64,2080]{1,0:T(8,128)S(1)}, f32[64,2080]{1,0:T(8,128)}, u32[]{:S(2)}) copy-start(f32[64,2080]{1,0:T(8,128)} %now_ref.1) | copy-start | bytes 1597444
  114.9 8.3 %copy-start.4 = (f32[64,2080]{1,0:T(8,128)S(1)}, f32[64,2080]{1,0:T(8,128)}, u32[]{:S(2)}) copy-start(f32[64,2080]{1,0:T(8,128)} %before_ref.1) | copy-start | bytes 1597444
  114.9 8.3 %copy-start.5 = (f32[64,64]{1,0:T(8,128)S(1)}, f32[64,64]{1,0:T(8,128)}, u32[]{:S(2)}) copy-start(f32[64,64]{1,0:T(8,128)} %coupling_ref.1) | copy-start | bytes 49156

commit v9 on v7

--- a/solution.py
+++ b/solution.py
@@ -410,9 +410,9 @@
         chunk = crossed(recv_ref[pl.ds(j, HALF, stride=S3), :], half_ref[0])
         known[:, j * 128 : (j + 1) * 128] = chunk
         parts[:, j * 128 : (j + 1) * 128] = stacked(chunk)
-    picked = folded(nn(parts[...], moved[...]))
     for load in loads:
         load.wait()
+    picked = folded(nn(parts[...], moved[...]))
     start = home_ref[0]
     tile = pl.multiple_of((start // 128) * 128, 128)
     home = pltpu.roll(known[:, pl.ds(tile, 128)], (128 - start % 128) % 128, 1)

time: 128 us -> 128 us (level)
  no operation moved by 1% of the time
where the time goes in v9:
time: 128 us; the launch traced here: 127 us
  Pallas kernels  41.4 us (32%)
  blocking collectives  35.1 us (27%)
  waiting for transfers between devices  27.9 us (22%)
  starting transfers between devices  22.1 us (17%)
    pallas_call x11, Pallas kernels, call(): pl.pallas_call(kernel, out_shape=[jax.ShapeDtypeStruct(shape, dtype) for...  41.4 us
    all_to_all x2, blocking collectives, exchange(): lax.all_to_all(x.reshape(peers, 1, lines * 128), axes, split_axis=0, conc...  35.1 us
    all_to_all x3, waiting for transfers between devices, exchange(): lax.all_to_all(x.reshape(peers, 1, lines * 128), axes, split_axis=0, conc...  26.6 us
    all_to_all x3, starting transfers between devices, exchange(): lax.all_to_all(x.reshape(peers, 1, lines * 128), axes, split_axis=0, conc...  21.5 us
  transfers between devices with their start and end apart: 4, of which 4 were waited for; matrix products, arithmetic and copies ran while one was open for 0% of the time, Pallas kernels for 13%

profile of v9, /device:TPU:1, one launch (start us, length us, event | category | flops | bytes accessed | tf_op | source)
XLA Modules:
  0.0 127.4 jit_solution(18359816485944158860)
XLA Ops:
  0.6 6.1 %shard_map.112 = (f32[2304,128]{1,0:T(8,128)}, s32[1,2176]{1,0:T(1,128)}) custom-call(s32[2080]{0:T(1024)} %vt_ref.1, f32[64,2080]{1,0:T(8,128)} %now_ref.1, f32[64,2080]{1,0:T(8,128)} %before_ref.1), custom_call_target="tpu_custom_call" | custom-call | flops 4000000000 | bytes 12000000 | tf_op jit(solution)/shard_map/pallas_call | solution.py:519
  6.7 11.5 %all-to-all-start = ((f32[128,1,2304]{2,1,0:T(1,128)}), f32[128,1,2304]{2,1,0:T(1,128)S(1)}, u32[]{:S(2)}, u32[]{:S(2)}) async-start(f32[128,1,2304]{2,1,0:T(1,128)} %bitcast.21), calls=%async_computation | async-start | bytes 2359296 | tf_op jit(solution)/shard_map/all_to_all | solution.py:537
  18.3 0.0 copy-start.6
  18.3 8.2 %shard_map.113 = (f32[16,256,256]{2,1,0:T(8,128)}, f32[15,256,256]{2,1,0:T(8,128)}) custom-call(f32[16,256,256]{2,1,0:T(8,128)} %inv_hbm.2, f32[15,256,256]{2,1,0:T(8,128)} %parent_hbm.1), custom_call_target="tpu_custom_call" | custom-call | flops 4000000000 | bytes 12000000 | tf_op jit(solution)/shard_map/pallas_call | solution.py:519
  26.5 12.2 %all-to-all-done = f32[128,1,2304]{2,1,0:T(1,128)S(1)} async-done(((f32[128,1,2304]{2,1,0:T(1,128)}), f32[128,1,2304]{2,1,0:T(1,128)S(1)}, u32[]{:S(2)}, u32[]{:S(2)}) %all-to-all-start) | async-done | bytes 1179680 | tf_op jit(solution)/shard_map/all_to_all | solution.py:537
  38.7 0.0 copy-done.6
  38.7 6.5 %shard_map.114 = (f32[640,128]{1,0:T(8,128)}, f32[64,2048]{1,0:T(8,128)S(1)}, f32[64,2176]{1,0:T(8,128)S(1)}) custom-call(s32[1]{0:T(128)} %bitcast.home_ref, s32[1]{0:T(128)} %bitcast.1.half_ref, f32[2304,128]{1,0:T(8,128)S(1)} %bitcast.12, s32[8,256]{1,0:T(8,128)S(1)} %copy-done.6, f32[8,256,256]{2,1,0:T(8,128)} %inv_ref.1, f32[8,256,256]{2,1,0:T(8,128)} %below_ref.1, ...), custom_call_target="tpu_custom_call" | custom-call | flops 4000000000 | bytes 12000000 | tf_op jit(solution)/shard_map/pallas_call | solution.py:519
  45.2 0.0 copy-done
  45.2 5.2 %all-to-all-start.1 = ((f32[64,1,1280]{2,1,0:T(1,128)}), f32[64,1,1280]{2,1,0:T(1,128)S(1)}, u32[]{:S(2)}, u32[]{:S(2)}) async-start(f32[64,1,1280]{2,1,0:T(1,128)} %bitcast.4), calls=%async_computation.1 | async-start | bytes 655360 | tf_op jit(solution)/shard_map/all_to_all | solution.py:537
  50.4 4.3 %shard_map.115 = (bf16[256,2176]{1,0:T(8,128)(2,1)S(1)}, f32[128,128]{1,0:T(8,128)S(1)}, f32[128,128]{1,0:T(8,128)S(1)}) custom-call(f32[2304,128]{1,0:T(8,128)} %bitcast.13, f32[64,2176]{1,0:T(8,128)S(1)} %get-tuple-element.21.tree_hbm), custom_call_target="tpu_custom_call" | custom-call | flops 4000000000 | bytes 12000000 | tf_op jit(solution)/shard_map/pallas_call | solution.py:519
  54.7 6.2 %all-to-all-done.1 = f32[64,1,1280]{2,1,0:T(1,128)S(1)} async-done(((f32[64,1,1280]{2,1,0:T(1,128)}), f32[64,1,1280]{2,1,0:T(1,128)S(1)}, u32[]{:S(2)}, u32[]{:S(2)}) %all-to-all-start.1) | async-done | bytes 327712 | tf_op jit(solution)/shard_map/all_to_all | solution.py:537
  60.9 2.0 %shard_map.116 = (f32[8,256]{1,0:T(8,128)S(1)}, f32[8,256]{1,0:T(8,128)S(1)}, f32[7,256,256]{2,1,0:T(8,128)S(1)}) custom-call(s32[1]{0:T(128)} %bitcast.1.half_ref, f32[640,128]{1,0:T(8,128)S(1)} %bitcast.17, f32[15,256,256]{2,1,0:T(8,128)} %get-tuple-element.19.ready_hbm.link_hbm, bf16[256,2176]{1,0:T(8,128)(2,1)S(1)} %get-tuple-element.22.ready_hbm.other_hbm), custom_call_target="tpu_custom_call" | custom-call | flops 4000000000 | bytes 12000000 | tf_op jit(solution)/shard_map/pallas_call | solution.py:519
  62.9 0.6 collective-permute-start
  63.5 2.1 %shard_map.117 = (f32[8,256]{1,0:T(8,128)S(1)}, f32[3,256,256]{2,1,0:T(8,128)S(1)}) custom-call(s32[1]{0:T(128)} %bitcast.1.half_ref, f32[8,256]{1,0:T(8,128)S(1)} %get-tuple-element.24.source_ref, f32[16,256,256]{2,1,0:T(8,128)} %get-tuple-element.25.square_hbm, f32[15,256,256]{2,1,0:T(8,128)} %get-tuple-element.19.ready_hbm.link_hbm), custom_call_target="tpu_custom_call" | custom-call | flops 2000000000 | bytes 6000000 | tf_op jit(solution)/shard_map/pallas_call | solution.py:519
  65.6 1.3 collective-permute-done.other_ref
  66.9 1.1 shard_map.118
  68.0 15.6 %all_to_all.25 = f32[64,1,1280]{2,1,0:T(1,128)S(1)} all-to-all(f32[64,1,1280]{2,1,0:T(1,128)S(1)} %bitcast.19), channel_id=1, replica_groups=mesh['half'=2,'group'=8,'front'=8] {'group','front'}, dimensions={0} | all-to-all | bytes 655360 | tf_op jit(solution)/shard_map/all_to_all | solution.py:537
  83.6 0.0 copy-done.1
  83.6 0.0 copy-done.2
  83.6 4.6 %shard_map.119 = f32[1280,128]{1,0:T(8,128)S(1)} custom-call(s32[1]{0:T(128)} %bitcast.home_ref, s32[1]{0:T(128)} %bitcast.1.half_ref, f32[640,128]{1,0:T(8,128)S(1)} %bitcast.18, s32[8,256]{1,0:T(8,128)S(1)} %copy-done.6, f32[128,128]{1,0:T(8,128)S(1)} %get-tuple-element.29.idx_ref, f32[128,128]{1,0:T(8,128)S(1)} %get-tuple-element.30.gram_ref, ...), custom_call_target="tpu_custom_call" | custom-call | flops 4000000000 | bytes 12000000 | tf_op jit(solution)/shard_map/pallas_call | solution.py:519
  88.3 19.4 %all_to_all.26 = f32[128,1,1280]{2,1,0:T(1,128)S(1)} all-to-all(f32[128,1,1280]{2,1,0:T(1,128)S(1)} %bitcast.16), channel_id=1, replica_groups=mesh['half'=2,'group'=8,'front'=8] {'half','group','front'}, dimensions={0} | all-to-all | bytes 1310720 | tf_op jit(solution)/shard_map/all_to_all | solution.py:537
  107.7 0.7 shard_map.120
  108.4 4.8 %all-to-all-start.4 = ((f32[128,1,256]{2,1,0:T(1,128)}), f32[128,1,256]{2,1,0:T(1,128)S(1)}, u32[]{:S(2)}, u32[]{:S(2)}) async-start(f32[128,1,256]{2,1,0:T(1,128)} %bitcast.10), calls=%async_computation.4 | async-start | bytes 262144 | tf_op jit(solution)/shard_map/all_to_all | solution.py:537
  113.2 0.0 copy-done.7
  113.2 0.0 copy-start.3
  113.2 0.0 copy-start.4
  113.2 0.0 copy-start.5
  113.2 1.7 %shard_map.121.solved_ref = f32[64,2080]{1,0:T(8,128)S(1)} custom-call(s32[1,2176]{1,0:T(1,128)S(1)} %copy-done.7, f32[1280,128]{1,0:T(8,128)S(1)} %bitcast.15), custom_call_target="tpu_custom_call" | custom-call | flops 4000000000 | bytes 12000000 | tf_op jit(solution)/shard_map/pallas_call | solution.py:519
  114.9 8.2 %all-to-all-done.4 = f32[128,1,256]{2,1,0:T(1,128)S(1)} async-done(((f32[128,1,256]{2,1,0:T(1,128)}), f32[128,1,256]{2,1,0:T(1,128)S(1)}, u32[]{:S(2)}, u32[]{:S(2)}) %all-to-all-start.4) | async-done | bytes 131104 | tf_op jit(solution)/shard_map/all_to_all | solution.py:537
  123.1 0.0 copy-done.3
  123.1 0.0 copy-done.5
  123.1 4.2 %shard_map.122 = (f32[64,64]{1,0:T(8,128)}, f32[64,64]{1,0:T(8,128)}, f32[64,2080]{1,0:T(8,128)}) custom-call(f32[256,128]{1,0:T(8,128)S(1)} %bitcast.20, f32[64,2080]{1,0:T(8,128)S(1)} %shard_map.121.solved_ref, f32[64,2080]{1,0:T(8,128)S(1)} %copy-done.3, f32[64,2080]{1,0:T(8,128)S(1)} %copy-done.4, f32[64,64]{1,0:T(8,128)S(1)} %copy-done.5), custom_call_target="tpu_custom_call" | custom-call | flops 4000000000 | bytes 12000000 | tf_op jit(solution)/shard_map/pallas_call | solution.py:519
  (5 shorter events, 0.0 us)
Async XLA Ops:
  6.7 32.0 %all-to-all-start = ((f32[128,1,2304]{2,1,0:T(1,128)}), f32[128,1,2304]{2,1,0:T(1,128)S(1)}, u32[]{:S(2)}, u32[]{:S(2)}) async-start(f32[128,1,2304]{2,1,0:T(1,128)} %bitcast.21), calls=%async_computation | async-start | bytes 2359296 | tf_op jit(solution)/shard_map/all_to_all | solution.py:537
  18.3 20.4 %copy-start.6 = (s32[8,256]{1,0:T(8,128)S(1)}, s32[8,256]{1,0:T(8,128)}, u32[]{:S(2)}) copy-start(s32[8,256]{1,0:T(8,128)} %rows_ref.3) | copy-start | bytes 24580
  38.7 6.5 %copy-start = (f32[128,1,2304]{2,1,0:T(1,128)}, f32[128,1,2304]{2,1,0:T(1,128)S(1)}, u32[]{:S(2)}) copy-start(f32[128,1,2304]{2,1,0:T(1,128)S(1)} %all-to-all-done) | copy-start | bytes 3538948
  45.2 15.7 %all-to-all-start.1 = ((f32[64,1,1280]{2,1,0:T(1,128)}), f32[64,1,1280]{2,1,0:T(1,128)S(1)}, u32[]{:S(2)}, u32[]{:S(2)}) async-start(f32[64,1,1280]{2,1,0:T(1,128)} %bitcast.4), calls=%async_computation.1 | async-start | bytes 655360 | tf_op jit(solution)/shard_map/all_to_all | solution.py:537
  62.9 4.0 %collective-permute-start = (f32[8,256]{1,0:T(8,128)S(1)}, f32[8,256]{1,0:T(8,128)S(1)}, u32[]{:S(2)}, u32[]{:S(2)}) collective-permute-start(f32[8,256]{1,0:T(8,128)S(1)} %get-tuple-element.23.top_ref), channel_id=1, source_target_pairs={{0,96},{8,104},{16,112},{24,120},{32,64},{40,72},{48,80},{56,88},{... | collective-permute-start | bytes 24584 | tf_op jit(solution)/shard_map/ppermute | solution.py:641
  66.9 16.8 %copy-start.1 = (f32[8,256,256]{2,1,0:T(8,128)S(1)}, f32[8,256,256]{2,1,0:T(8,128)}, u32[]{:S(2)}) copy-start(f32[8,256,256]{2,1,0:T(8,128)} %inv_ref.1) | copy-start | bytes 6291460
  66.9 16.8 %copy-start.2 = (f32[8,256,256]{2,1,0:T(8,128)S(1)}, f32[8,256,256]{2,1,0:T(8,128)}, u32[]{:S(2)}) copy-start(f32[8,256,256]{2,1,0:T(8,128)} %below_ref.1) | copy-start | bytes 6291460
  107.7 5.5 %copy-start.7 = (s32[1,2176]{1,0:T(1,128)S(1)}, s32[1,2176]{1,0:T(1,128)}, u32[]{:S(2)}) copy-start(s32[1,2176]{1,0:T(1,128)} %get-tuple-element.32.key_ref) | copy-start | bytes 26116
  108.4 14.7 %all-to-all-start.4 = ((f32[128,1,256]{2,1,0:T(1,128)}), f32[128,1,256]{2,1,0:T(1,128)S(1)}, u32[]{:S(2)}, u32[]{:S(2)}) async-start(f32[128,1,256]{2,1,0:T(1,128)} %bitcast.10), calls=%async_computation.4 | async-start | bytes 262144 | tf_op jit(solution)/shard_map/all_to_all | solution.py:537
  113.2 9.9 %copy-start.3 = (f32[64,2080]{1,0:T(8,128)S(1)}, f32[64,2080]{1,0:T(8,128)}, u32[]{:S(2)}) copy-start(f32[64,2080]{1,0:T(8,128)} %now_ref.1) | copy-start | bytes 1597444
  113.2 9.9 %copy-start.4 = (f32[64,2080]{1,0:T(8,128)S(1)}, f32[64,2080]{1,0:T(8,128)}, u32[]{:S(2)}) copy-start(f32[64,2080]{1,0:T(8,128)} %before_ref.1) | copy-start | bytes 1597444
  113.2 9.9 %copy-start.5 = (f32[64,64]{1,0:T(8,128)S(1)}, f32[64,64]{1,0:T(8,128)}, u32[]{:S(2)}) copy-start(f32[64,64]{1,0:T(8,128)} %coupling_ref.1) | copy-start | bytes 49156
